TPU v7x, 32 devices: a whole 2x2x4 slice. The times are simulated.
32 devices in a mesh: groups: 2 (over y), dom: 4 (over z), head: 2 (over x), aux: 2 (over core).
Axes of the slice: x: 2, y: 2, z: 4, core: 2. Of those that a mesh axis runs over, the one named last changes fastest.
Arguments:
- features: float32 [4096, 192], P(('groups', 'dom', 'aux')), parts along dimension 0, may hold values from -6 to 6
- face_weight: float32 [24576], P(('groups', 'dom', 'aux')), parts along dimension 0, may hold values from 0.5 to 2
- faces: int32 [3, 24576], P(None, ('groups', 'dom', 'aux')), parts along dimension 1, may hold values from 0 to 255, as said below
- face_live: int32 [16], P(('groups', 'dom', 'aux')), parts along dimension 0, may hold values from 24 to 1536, as said below
- send_index: int32 [2, 512], P(None, ('groups', 'dom', 'aux')), parts along dimension 1, may hold values from 0 to 255
- anchor_index: int32 [1024], P(('groups', 'dom', 'head', 'aux')), parts along dimension 0, may hold values from 0 to 255
- w_in: float32 [384, 768], P(None, 'head'), may hold values from -0.3125 to 0.3125
- w_out: float32 [768, 192], P('head'), may hold values from -0.21875 to 0.21875
- w_query: float32 [192, 192], replicated, may hold values from -8 to 8
- w_key: float32 [192, 192], replicated, may hold values from -8 to 8
- w_value: float32 [192, 192], replicated, may hold values from -0.4375 to 0.4375
- w_attn_out: float32 [192, 192], replicated, may hold values from -0.4375 to 0.4375
- out_grad: float32 [4096, 192], P(('groups', 'dom', 'aux')), parts along dimension 0, may hold values from -6 to 6
Outputs:
- output: float32 [4096, 192], P(('groups', 'dom', 'aux')), parts along dimension 0
- anchor_grad: float32 [1024, 192], P(('groups', 'dom', 'head', 'aux')), parts along dimension 0
There are 2 independent parts, one for each index of `groups`. A program takes and returns all parts, laid end to end along the dimension named above; an argument that names none is the same for every part. Nothing has to cross between parts.
Inputs may be any that keep to these rules, and one draw needn't show every extreme that they name: `faces`: row 0 is a row of the receiving block; row 1 is 0 (own block), 1 (lower neighbour along dom) or 2 (upper); row 2 is a row of the own block when row 1 is 0, else a slot below 32 of that neighbour's halo rows. `face_live`: live face slots of a block come first; some block has all 1536 live.
All inputs are finite; a program needn't handle non-finite values.
Results may differ from a plain program's by a relative error of at most 0.0003.
Values sent between devices are 32-bit elements; how exact they have to be, the bound alone decides.
No kernel may reach another device: no remote copies, remote signals or barrier semaphores. Data moves between devices by JAX's collectives and lax.ppermute only.
A program may use at most 64 MiB of HBM per device.

v0:
```python
import math

import jax
import jax.numpy as jnp
from jax import lax
from jax.sharding import PartitionSpec as P

HEADS = 3
DH = 64


HIGH = lax.Precision.HIGHEST


def padded_2(value, sides, width):
    for axis, dim in sides:
        size, length = (lax.axis_size(axis), value.shape[dim])
        up = [(i, (i + 1) % size) for i in range(size)]
        down = [(j, i) for i, j in up]
        last = lax.slice_in_dim(value, length - width, length, axis=dim)
        first = lax.slice_in_dim(value, 0, width, axis=dim)
        before = lax.ppermute(last, axis, up)
        after = lax.ppermute(first, axis, down)
        value = jnp.concatenate([before, value, after], axis=dim)
    return value


def joined(part, axis, combine):
    gathered = jax.tree.map(lambda a: lax.all_gather(a, axis), part)

    def take(source):
        return jax.tree.map(lambda a: lax.dynamic_index_in_dim(a, source, 0, False), gathered)

    return lax.fori_loop(
        1, lax.axis_size(axis), lambda source, state: combine(state, take(source)), take(0)
    )


def matmul(left, right):
    return jnp.dot(left, right, precision=HIGH, preferred_element_type=jnp.float32)


def layer_norm(value):
    mean = jnp.mean(value, axis=-1, keepdims=True)
    centred = value - mean
    spread = jnp.mean(centred * centred, axis=-1, keepdims=True)
    return centred * lax.rsqrt(spread + 1e-05)


def combine_parts(first, second):
    top_a, total_a, acc_a = first
    top_b, total_b, acc_b = second
    top = jnp.maximum(top_a, top_b)
    factor_a = jnp.exp(top_a - top)
    factor_b = jnp.exp(top_b - top)
    total = total_a * factor_a + total_b * factor_b
    acc = acc_a * jnp.repeat(factor_a.T, DH, axis=1) + acc_b * jnp.repeat(factor_b.T, DH, axis=1)
    return (top, total, acc)


def shards(
    features,
    face_weight,
    faces,
    face_live,
    send_index,
    anchor_index,
    w_in,
    w_out,
    w_query,
    w_key,
    w_value,
    w_attn_out,
    out_grad,
):
    cell_rows, width = features.shape
    halo_count = send_index.shape[1]
    normed = layer_norm(features)
    outgoing = jnp.stack([normed[send_index[0]], normed[send_index[1]]])
    padded = padded_2(outgoing, (("dom", 0),), 1)
    extended = jnp.concatenate([normed, padded[0], padded[3]], axis=0)
    offset = jnp.where(
        faces[1] == 0, 0, jnp.where(faces[1] == 1, cell_rows, cell_rows + halo_count)
    )
    source = faces[2] + offset
    live = jnp.arange(faces.shape[1]) < face_live[0]
    weights = jnp.where(live, face_weight, 0.0)
    messages = extended[source] * weights[:, None]
    gathered = jax.ops.segment_sum(messages, faces[0], num_segments=cell_rows)
    hidden = jax.nn.gelu(
        matmul(jnp.concatenate([normed, gathered], axis=1), w_in), approximate=False
    )
    mixed = features + lax.psum(matmul(hidden, w_out), "head")
    query_normed = layer_norm(mixed)
    query = matmul(query_normed, w_query)
    anchor_feats = query_normed[anchor_index]
    paired = jnp.concatenate([matmul(anchor_feats, w_key), matmul(anchor_feats, w_value)], axis=1)
    paired_all = lax.all_gather(paired, ("dom", "aux"), axis=0, tiled=True)
    keys = paired_all[:, :width]
    values = paired_all[:, width:]
    scale = 1.0 / math.sqrt(DH)
    block_rows = min(512, cell_rows)
    block_count = cell_rows // block_rows

    def partial_block(q_block):
        tops, totals, sums = ([], [], [])
        for head in range(HEADS):
            cols = slice(head * DH, (head + 1) * DH)
            scores = matmul(q_block[:, cols], keys[:, cols].T) * scale
            top = jnp.max(scores, axis=1)
            expo = jnp.exp(scores - top[:, None])
            tops.append(top)
            totals.append(jnp.sum(expo, axis=1))
            sums.append(matmul(expo, values[:, cols]))
        return (jnp.stack(tops), jnp.stack(totals), jnp.concatenate(sums, axis=1))

    tops, totals, sums = lax.map(partial_block, query.reshape(block_count, block_rows, width))
    tops = tops.transpose(1, 0, 2).reshape(HEADS, cell_rows)
    totals = totals.transpose(1, 0, 2).reshape(HEADS, cell_rows)
    sums = sums.reshape(cell_rows, width)
    tops, totals, sums = joined((tops, totals, sums), "head", combine_parts)
    attended = sums / jnp.repeat(totals.T, DH, axis=1)
    output = mixed + matmul(attended, w_attn_out)
    d_att = matmul(out_grad, w_attn_out.T)
    delta = jnp.stack(
        [
            jnp.sum(
                d_att[:, head * DH : (head + 1) * DH] * attended[:, head * DH : (head + 1) * DH],
                axis=1,
            )
            for head in range(HEADS)
        ]
    )
    keys_parts = []
    value_parts = []
    for head in range(HEADS):
        cols = slice(head * DH, (head + 1) * DH)
        q_head = query[:, cols]
        g_head = d_att[:, cols]
        scores = matmul(q_head, keys[:, cols].T) * scale
        probs = jnp.exp(scores - tops[head][:, None]) / totals[head][:, None]
        dprob = matmul(g_head, values[:, cols].T)
        dscore = probs * (dprob - delta[head][:, None])
        keys_parts.append(matmul(dscore.T, q_head) * scale)
        value_parts.append(matmul(probs.T, g_head))
    grad_k = jnp.concatenate(keys_parts, axis=1)
    grad_v = jnp.concatenate(value_parts, axis=1)
    summed = lax.psum_scatter(
        jnp.concatenate([grad_k, grad_v], axis=1), ("dom", "aux"), scatter_dimension=0, tiled=True
    )
    anchor_grad = matmul(summed[:, :width], w_key.T) + matmul(summed[:, width:], w_value.T)
    return (output, anchor_grad)


def solution(mesh):
    placed = (
        P(("groups", "dom", "aux"), None),
        P(("groups", "dom", "aux")),
        P(None, ("groups", "dom", "aux")),
        P(("groups", "dom", "aux")),
        P(None, ("groups", "dom", "aux")),
        P(("groups", "dom", "head", "aux")),
        P(None, "head"),
        P("head", None),
        P(),
        P(),
        P(),
        P(),
        P(("groups", "dom", "aux"), None),
    )
    return jax.shard_map(
        shards,
        mesh=mesh,
        in_specs=placed,
        out_specs=(P(("groups", "dom", "aux"), None), P(("groups", "dom", "head", "aux"), None)),
        check_vma=False,
    )
```

profile of v0, /device:TPU:0, one launch (start us, length us, event | category | flops | bytes accessed | tf_op | source)
XLA Modules:
  0.0 140.5 jit_solution(1424147450441912269)
XLA Ops:
  7.2 1.1 copy.19
  8.8 0.6 gather_fusion
  9.5 3.1 %collective-permute-start = (f32[1,32,192]{2,1,0:T(8,128)S(1)}, f32[1,32,192]{2,1,0:T(8,128)S(1)}, u32[]{:S(2)}, u32[]{:S(2)}) collective-permute-start(f32[1,32,192]{2,1,0:T(8,128)S(1)} %bitcast.96), channel_id=1, source_target_pairs={{0,4},{4,8},{8,12},{12,0},{1,5},{5,9},{9,13},{13,1},{2,6},{6,10},{... | collective-permute-start | bytes 73736 | tf_op jit(solution)/shard_map/ppermute | solution.py:22
  12.5 0.6 gather_fusion.1
  13.1 2.1 %collective-permute-start.1 = (f32[1,32,192]{2,1,0:T(8,128)S(1)}, f32[1,32,192]{2,1,0:T(8,128)S(1)}, u32[]{:S(2)}, u32[]{:S(2)}) collective-permute-start(f32[1,32,192]{2,1,0:T(8,128)S(1)} %bitcast.98), channel_id=1, source_target_pairs={{4,0},{8,4},{12,8},{0,12},{5,1},{9,5},{13,9},{1,13},{6,2},{10,6},{... | collective-permute-start | bytes 73736 | tf_op jit(solution)/shard_map/ppermute | solution.py:23
  16.5 0.6 collective-permute-done.1
  17.1 15.0 %scatter_custom_fusion = f32[256,192]{1,0:T(8,128)S(1)} fusion(s32[1536]{0:T(1024)S(1)} %slice_reduce_fusion, f32[1536]{0:T(1024)S(1)} %fusion.141, f32[]{:T(128)} %constant.39.clone.1, f32[320,192]{1,0:T(8,128)S(1)} %pad_maximum_fusion, s32[2048]{0:T(1024)S(1)} %pad_clamp_fusion), kind=kCustom, calls=%fused_computation.5 | custom fusion | flops 589824 | bytes 540676 | tf_op jit(solution)/shard_map/scatter-add | solution.py:89
  32.1 0.9 fusion.13
  33.1 2.1 %fusion.11 = f32[256,192]{0,1:T(8,128)} fusion(f32[384,192]{0,1:T(8,128)S(1)} %copy-done.10, f32[256,384]{1,0:T(8,128)S(1)} %fusion.13), kind=kOutput, calls=%fused_computation.31 | convolution fusion | flops 232783872 | bytes 884736 | tf_op jit(solution)/shard_map/dot_general | solution.py:40
  35.6 23.7 %all-reduce.2.cloned.1.call-done = f32[256,192]{0,1:T(8,128)} async-done(((f32[256,192]{0,1:T(8,128)}), f32[256,192]{0,1:T(8,128)}) %all-reduce.2.cloned.1.call-update) | async-done | bytes 196624 | tf_op jit(solution)/shard_map/psum | solution.py:93
  59.4 1.0 fusion.185
  60.6 0.7 copy-done.6
  61.3 0.6 fusion.191
  61.9 0.6 gather_fusion.2
  63.0 14.7 %all_gather.12 = f32[256,384]{1,0:T(8,128)S(1)} all-gather(f32[32,384]{1,0:T(8,128)S(1)} %pad_maximum_fusion.2), channel_id=1, replica_groups=mesh['groups'=2,'dom'=4,'head'=2,'aux'=2] {'dom','aux'}, dimensions={0}, use_global_device_ids=true | all-gather | bytes 442368 | tf_op jit(solution)/shard_map/all_gather | solution.py:98
  79.9 0.4 fusion.73
  80.3 4.3 %all-gather.3 = f32[2,3,256]{2,1,0:T(4,128)S(1)} all-gather(f32[1,3,256]{2,1,0:T(4,128)S(1)} %maximum_bitcast_fusion), channel_id=3, replica_groups=mesh['groups'=2,'dom'=4,'head'=2,'aux'=2] {'head'}, dimensions={0}, use_global_device_ids=true | all-gather | bytes 9216 | tf_op jit(solution)/shard_map/all_gather | solution.py:29
  84.7 4.3 %all-gather.4 = f32[2,3,256]{2,1,0:T(4,128)S(1)} all-gather(f32[1,3,256]{2,1,0:T(4,128)S(1)} %maximum_bitcast_fusion.1), channel_id=4, replica_groups=mesh['groups'=2,'dom'=4,'head'=2,'aux'=2] {'head'}, dimensions={0}, use_global_device_ids=true | all-gather | bytes 9216 | tf_op jit(solution)/shard_map/all_gather | solution.py:29
  89.1 6.3 %all-gather = f32[512,192]{0,1:T(8,128)S(1)} all-gather(f32[256,192]{0,1:T(8,128)S(1)} %pad_maximum_fusion.1), channel_id=2, replica_groups=mesh['groups'=2,'dom'=4,'head'=2,'aux'=2] {'head'}, dimensions={0}, use_global_device_ids=true | all-gather | bytes 589824 | tf_op jit(solution)/shard_map/all_gather | solution.py:29
  99.1 0.9 copy.27
  100.0 1.3 convolution_add_fusion
  101.3 29.6 %reduce-scatter.4.cloned.1.call-done = f32[32,384]{1,0:T(8,128)} async-done(((f32[256,384]{1,0:T(8,128)}), f32[32,384]{1,0:T(8,128)}) %reduce-scatter.4.cloned.1.call-update) | async-done | bytes 49168
  130.9 1.0 fusion.139
  131.9 1.7 %convolution_add_fusion.1 = f32[32,192]{1,0:T(8,128)} fusion(f32[32,192]{1,0:T(8,128)S(1)} %fusion.139, f32[192,192]{1,0:T(8,128)S(1)} %copy-done.2, f32[32,384]{1,0:T(8,128)} %reduce-scatter.4.cloned.1.call-done), kind=kOutput, calls=%fused_computation.26 | convolution fusion | flops 14161920 | bytes 229376 | tf_op jit(solution)/shard_map/dot_general | solution.py:40
  (77 shorter events, 8.0 us)
Async XLA Ops:
  7.2 25.0 %copy-start = (f32[384,384]{1,0:T(8,128)S(1)}, f32[384,384]{1,0:T(8,128)}, u32[]{:S(2)}) copy-start(f32[384,384]{1,0:T(8,128)} %param.19) | copy-start | bytes 1769476
  7.2 1.2 copy-start.1
  7.2 1.2 copy-start.9
  7.2 52.2 %all-reduce.2.cloned.1.call-start = ((), (), s32[]{:S(2)}) async-start(), calls=%async_computation.1 | async-start | bytes 393216 | tf_op jit(solution)/shard_map/psum | solution.py:93
  8.6 6.6 %copy-start.7 = (s32[3,1536]{1,0:T(4,128)S(1)}, s32[3,1536]{1,0:T(4,128)}, u32[]{:S(2)}) copy-start(s32[3,1536]{1,0:T(4,128)} %param.15) | copy-start | bytes 55300
  8.7 7.3 %copy-start.11 = (s32[32]{0:T(128)S(1)}, s32[32]{0:T(128)}, u32[]{:S(2)}) copy-start(s32[32]{0:T(128)} %param.18) | copy-start | bytes 388
  8.7 7.3 %copy-start.8 = (f32[1536]{0:T(1024)S(1)}, f32[1536]{0:T(1024)}, u32[]{:S(2)}) copy-start(f32[1536]{0:T(1024)} %param.14) | copy-start | bytes 18436
  9.5 7.0 %collective-permute-start = (f32[1,32,192]{2,1,0:T(8,128)S(1)}, f32[1,32,192]{2,1,0:T(8,128)S(1)}, u32[]{:S(2)}, u32[]{:S(2)}) collective-permute-start(f32[1,32,192]{2,1,0:T(8,128)S(1)} %bitcast.96), channel_id=1, source_target_pairs={{0,4},{4,8},{8,12},{12,0},{1,5},{5,9},{9,13},{13,1},{2,6},{6,10},{... | collective-permute-start | bytes 73736 | tf_op jit(solution)/shard_map/ppermute | solution.py:22
  13.1 4.0 %collective-permute-start.1 = (f32[1,32,192]{2,1,0:T(8,128)S(1)}, f32[1,32,192]{2,1,0:T(8,128)S(1)}, u32[]{:S(2)}, u32[]{:S(2)}) collective-permute-start(f32[1,32,192]{2,1,0:T(8,128)S(1)} %bitcast.98), channel_id=1, source_target_pairs={{4,0},{8,4},{12,8},{0,12},{5,1},{9,5},{13,9},{1,13},{6,2},{10,6},{... | collective-permute-start | bytes 73736 | tf_op jit(solution)/shard_map/ppermute | solution.py:23
  32.1 1.0 copy-start.10
  33.1 2.2 %copy-start.4 = (f32[192,192]{1,0:T(8,128)S(1)}, f32[192,192]{1,0:T(8,128)}, u32[]{:S(2)}) copy-start(f32[192,192]{1,0:T(8,128)} %param.24) | copy-start | bytes 442372
  33.1 2.2 %copy-start.5 = (f32[256,192]{0,1:T(8,128)S(1)}, f32[256,192]{0,1:T(8,128)}, u32[]{:S(2)}) copy-start(f32[256,192]{0,1:T(8,128)} %param.25) | copy-start | bytes 589828
  35.2 95.6 %reduce-scatter.4.cloned.1.call-start = ((), (), s32[]{:S(2)}) async-start(), calls=%async_computation.2 | async-start | bytes 442368
  60.4 0.9 copy-start.6
  60.5 2.0 %copy-start.3 = (f32[192,192]{1,0:T(8,128)S(1)}, f32[192,192]{1,0:T(8,128)}, u32[]{:S(2)}) copy-start(f32[192,192]{1,0:T(8,128)} %param.22) | copy-start | bytes 442372
  61.3 1.4 %copy-start.2 = (f32[192,192]{1,0:T(8,128)S(1)}, f32[192,192]{1,0:T(8,128)}, u32[]{:S(2)}) copy-start(f32[192,192]{1,0:T(8,128)} %param.23) | copy-start | bytes 442372
Sparse Core Ops, SparseCore 0:
  35.4 23.9 all-reduce.1
  100.1 30.7 reduce-scatter.3
where the time goes:
time: 141 us; the launch traced here: 140 us
  waiting for transfers between devices  54.5 us (39%)
  blocking collectives  29.7 us (21%)
  other arithmetic  16.9 us (12%)
  between operations  15.1 us (11%)
  matrix products  14.3 us (10%)
  starting transfers between devices  5.25 us (4%)
  local copies, waits for them, and re-layouts  4.74 us (3%)
    unnamed x3, waiting for transfers between devices  29.6 us
    psum x1, waiting for transfers between devices, shards(): mixed = features + lax.psum(matmul(hidden, w_out), 'head')  23.7 us
    all_gather x3, blocking collectives, joined(): gathered = jax.tree.map(lambda a: lax.all_gather(a, axis), part)  15 us
    scatter-add x1, other arithmetic, shards(): gathered = jax.ops.segment_sum(messages, faces[0], num_segments=cell_rows)  15 us
    all_gather x1, blocking collectives, shards(): paired_all = lax.all_gather(paired, ('dom', 'aux'), axis=0, tiled=True)  14.7 us
    dot_general x24, matrix products, matmul(): jnp.dot(left, right, precision=HIGH, preferred_element_type=jnp.float32)  14.3 us
    ppermute x1, starting transfers between devices, padded_2(): before = lax.ppermute(last, axis, up)  3.08 us
  transfers between devices with their start and end apart: 4, of which 4 were waited for; matrix products, arithmetic and copies ran while one was open for 2% of the time, Pallas kernels for 0%

commit v1 on v0

v1 whole, which is shorter than its diff:
```python
import functools
import math

import jax
import jax.numpy as jnp
from jax import lax
from jax.experimental import pallas as pl
from jax.experimental.pallas import tpu as pltpu
from jax.sharding import PartitionSpec as P

HEADS = 3
DH = 64
HIGH = lax.Precision.HIGH
NN = (((1,), (0,)), ((), ()))
NT = (((1,), (1,)), ((), ()))
BF = jnp.bfloat16
F32 = jnp.float32


def dot(left, right, dims=NN, precision=HIGH):
    return lax.dot_general(left, right, dims, precision=precision, preferred_element_type=F32)


def dot_bf(left, right, dims=NN):
    return lax.dot_general(left, right, dims, preferred_element_type=F32)


def split(value):
    top = value.astype(BF)
    return top, (value - top.astype(F32)).astype(BF)


def layer_norm(value):
    mean = jnp.mean(value, axis=-1, keepdims=True)
    centred = value - mean
    spread = jnp.mean(centred * centred, axis=-1, keepdims=True)
    return centred * lax.rsqrt(spread + 1e-05)


def call(body, outs, ins, smem=(), scratch=(), flops=10**8):
    specs = [
        pl.BlockSpec(memory_space=pltpu.SMEM if i in smem else pltpu.VMEM)
        for i in range(len(ins))
    ]
    return pl.pallas_call(
        body,
        out_shape=[jax.ShapeDtypeStruct(s, F32) for s in outs],
        in_specs=specs,
        out_specs=[pl.BlockSpec(memory_space=pltpu.VMEM)] * len(outs),
        scratch_shapes=list(scratch),
        compiler_params=pltpu.CompilerParams(vmem_limit_bytes=48 * 2**20),
        cost_estimate=pl.CostEstimate(flops=flops, bytes_accessed=10**6, transcendentals=0),
    )(*ins)


def take_rows(source, index, count, target):
    if count <= 64:
        for i in range(count):
            target[pl.ds(i, 1), :] = source[pl.ds(index(i), 1), :]
    else:

        def step(i, carry):
            target[pl.ds(i, 1), :] = source[pl.ds(index(i), 1), :]
            return carry

        lax.fori_loop(0, count, step, 0)


def take_anchors(head_ref, own_ref, other_ref, source, target):
    own = own_ref.shape[1]
    n_head = other_ref.shape[1] // own + 1
    for place in range(n_head):
        step = lax.rem(head_ref[0] - place + n_head, n_head)
        base = jnp.maximum(step - 1, 0) * own

        def index(i, step=step, base=base):
            return jnp.where(step == 0, own_ref[0, i], other_ref[0, base + i])

        take_rows(source, index, own, target.at[pl.ds(place * own, own)])


def outgoing_kernel(parity_ref, send_ref, x_ref, first_ref, second_ref):
    parity = parity_ref[0]
    count = first_ref.shape[0]
    take_rows(x_ref, lambda i: send_ref[1 - parity, i], count, first_ref)
    take_rows(x_ref, lambda i: send_ref[parity, i], count, second_ref)
    first_ref[...] = layer_norm(first_ref[...])
    second_ref[...] = layer_norm(second_ref[...])


def own_faces_kernel(
    parity_ref, live_ref, head_ref, own_ref, other_ref, x_ref, faces_ref, weight_ref, w_in_ref,
    pre_ref, halo_mat_ref, anchor_ref,
):
    rows, width = x_ref.shape
    halos = halo_mat_ref.shape[1] // 2
    slots = faces_ref.shape[1]
    x = x_ref[...]
    normed = layer_norm(x)
    take_anchors(head_ref, own_ref, other_ref, x_ref, anchor_ref)
    receiver = faces_ref[0:1, :]
    kind = faces_ref[1:2, :]
    first_kind = 2 - parity_ref[0]
    offset = jnp.where(kind == 0, 0, jnp.where(kind == first_kind, rows, rows + halos))
    source = faces_ref[2:3, :] + offset
    live = lax.broadcasted_iota(jnp.int32, (1, slots), 1) < live_ref[0]
    weight = jnp.where(live, weight_ref[...], 0.0)
    top = weight.astype(BF).astype(F32)
    low = (weight - top).astype(BF).astype(F32)
    into = jnp.where(
        lax.broadcasted_iota(jnp.int32, (rows, slots), 0) == receiver, 1.0, 0.0
    ).astype(BF)
    match = lax.broadcasted_iota(jnp.int32, (rows + 2 * halos, slots), 0) == source
    matrix = dot_bf(into, jnp.where(match, top, 0.0).astype(BF), NT)
    matrix = matrix + dot_bf(into, jnp.where(match, low, 0.0).astype(BF), NT)
    halo_mat_ref[...] = matrix[:, rows:]
    agg = dot(matrix[:, :rows], normed)
    pre_ref[...] = dot(normed, w_in_ref[:width]) + dot(agg, w_in_ref[width:])


def mlp_kernel(
    head_ref, own_ref, other_ref, first_ref, second_ref, pre_ref, halo_mat_ref, w_in_ref, w_out_ref,
    part_ref, anchor_ref,
):
    width = first_ref.shape[1]
    halo = jnp.concatenate([first_ref[...], second_ref[...]], axis=0)
    halo = dot(halo, w_in_ref[width:])
    pre = pre_ref[...] + dot(halo_mat_ref[...], halo)
    hidden = 0.5 * pre * (1.0 + lax.erf(pre * math.sqrt(0.5)))
    part_ref[...] = dot(hidden, w_out_ref[...])
    take_anchors(head_ref, own_ref, other_ref, part_ref, anchor_ref)


def grad_in_kernel(g_ref, w_ref, d_ref, d_t_ref):
    d = dot(g_ref[...], w_ref[...], NT)
    d_ref[...] = d
    d_t_ref[...] = d.T


def anchor_kernel(x_ref, part_ref, recv_ref, out_ref):
    out_ref[...] = layer_norm(x_ref[...] + (part_ref[...] + recv_ref[...]))


def query_kernel(x_ref, part_ref, recv_ref, w_ref, mixed_ref, q_ref, q_t_ref):
    mixed = x_ref[...] + (part_ref[...] + recv_ref[...])
    mixed_ref[...] = mixed
    q = dot(layer_norm(mixed), w_ref[...]) * (1.0 / math.sqrt(DH))
    q_ref[...] = q
    q_t_ref[...] = q.T


def pairs(value):
    top, low = split(value)
    return jnp.concatenate([top, low, top, low], axis=1)


def pairs_right(value):
    top, low = split(value)
    return jnp.concatenate([top, top, low, low], axis=1)


def wide(value):
    top, low = split(value)
    return jnp.concatenate([top, low], axis=1)


def attention_kernel(blocks, own, head_ref, *refs):
    feats = refs[:blocks]
    q_ref, q_t_ref, d_ref, d_t_ref, wk_ref, wv_ref, att_ref, keep_ref, give_ref = refs[
        blocks : blocks + 9
    ]
    n_head = feats[0].shape[0] // own
    head = head_ref[0]

    def of_head(step):
        start = pl.multiple_of(lax.rem(head + step, n_head) * own, own)
        return jnp.concatenate([f[pl.ds(start, own), :] for f in feats], axis=0)

    mine = of_head(0)
    rest = jnp.concatenate([of_head(step) for step in range(1, n_head)], axis=0)
    count = mine.shape[0]
    rest_count = rest.shape[0]
    chunk = min(rest_count, 512)
    wk, wv = wk_ref[...], wv_ref[...]
    k_mine, v_mine = dot(mine, wk), dot(mine, wv)
    if rest_count == chunk:
        k_rest, v_rest = dot(rest, wk), dot(rest, wv)
    else:
        rest_ref = refs[-1]
        rest_ref[...] = rest
    grads_k, grads_v = [], []
    for at in range(HEADS):
        cols = slice(at * DH, (at + 1) * DH)
        q_pairs = pairs(q_ref[:, cols])
        d = d_ref[:, cols]
        score = dot_bf(q_pairs, pairs_right(k_mine[:, cols]), NT)
        v_wide = wide(v_mine[:, cols])
        if rest_count == chunk:
            score_rest = dot_bf(q_pairs, pairs_right(k_rest[:, cols]), NT)
            top = jnp.maximum(
                jnp.max(score, axis=1, keepdims=True), jnp.max(score_rest, axis=1, keepdims=True)
            )
            expo = jnp.exp(score - top)
            expo_rest = jnp.exp(score_rest - top)
            total = jnp.sum(expo, axis=1, keepdims=True) + jnp.sum(
                expo_rest, axis=1, keepdims=True
            )
            e_top, e_low = split(expo_rest)
            rest_wide = wide(v_rest[:, cols])
            acc = dot_bf(e_top, rest_wide) + dot_bf(e_low, rest_wide)
        else:
            top = jnp.max(score, axis=1, keepdims=True)

            def step(i, state):
                top, total, acc = state
                feat = rest_ref[pl.ds(pl.multiple_of(i * chunk, chunk), chunk), :]
                score_rest = dot_bf(q_pairs, pairs_right(dot(feat, wk_ref[:, cols])), NT)
                new = jnp.maximum(top, jnp.max(score_rest, axis=1, keepdims=True))
                expo_rest = jnp.exp(score_rest - new)
                factor = jnp.exp(top - new)
                total = total * factor + jnp.sum(expo_rest, axis=1, keepdims=True)
                e_top, e_low = split(expo_rest)
                rest_wide = wide(dot(feat, wv_ref[:, cols]))
                acc = acc * factor + dot_bf(e_top, rest_wide) + dot_bf(e_low, rest_wide)
                return new, total, acc

            start = (top, jnp.zeros_like(top), jnp.zeros((q_ref.shape[0], 2 * DH), F32))
            top, total, acc = lax.fori_loop(0, rest_count // chunk, step, start)
            expo = jnp.exp(score - top)
            total = total + jnp.sum(expo, axis=1, keepdims=True)
        e_top, e_low = split(expo)
        acc = acc + (dot_bf(e_top, v_wide) + dot_bf(e_low, v_wide))
        inverse = 1.0 / total
        att = (acc[:, :DH] + acc[:, DH:]) * inverse
        att_ref[:, cols] = att
        probs = expo * inverse
        d_prob = dot_bf(pairs(d), pairs_right(v_mine[:, cols]), NT)
        delta = jnp.sum(d * att, axis=1, keepdims=True)
        s_top, s_low = split(probs * (d_prob - delta))
        p_top, p_low = split(probs)
        q_t = jnp.concatenate(split(q_t_ref[cols, :]), axis=0)
        d_t = jnp.concatenate(split(d_t_ref[cols, :]), axis=0)
        grad_k = dot_bf(q_t, s_top) + dot_bf(q_t, s_low)
        grad_v = dot_bf(d_t, p_top) + dot_bf(d_t, p_low)
        grads_k.append(grad_k[:DH] + grad_k[DH:])
        grads_v.append(grad_v[:DH] + grad_v[DH:])
    grad_k = jnp.concatenate(grads_k, axis=0)
    grad_v = jnp.concatenate(grads_v, axis=0)
    grad = (dot(wk, grad_k) + dot(wv, grad_v)).T
    keep_ref[...] = grad[: count // 2]
    give_ref[...] = grad[count // 2 :]


def add_kernel(own, keep_ref, recv_ref, *outs):
    for i, out in enumerate(outs):
        rows = pl.ds(i * own, own)
        out[...] = keep_ref[rows, :] + recv_ref[rows, :]


def output_kernel(mixed_ref, att_ref, w_ref, out_ref):
    out_ref[...] = mixed_ref[...] + dot(att_ref[...], w_ref[...])


def sum_kernel(*refs):
    total = refs[0][...]
    for ref in refs[1:-1]:
        total = total + ref[...]
    refs[-1][...] = total


def shards(
    features,
    face_weight,
    faces,
    face_live,
    send_index,
    anchor_index,
    w_in,
    w_out,
    w_query,
    w_key,
    w_value,
    w_attn_out,
    out_grad,
):
    rows, width = features.shape
    halos = send_index.shape[1]
    units = w_in.shape[1]
    own = anchor_index.shape[0]
    n_dom, n_head, n_aux = (lax.axis_size(a) for a in ("dom", "head", "aux"))
    assert n_dom % 2 == 0 and n_aux == 2
    anchors = own * n_head
    head = lax.axis_index("head").astype(jnp.int32).reshape(1)
    parity = (lax.axis_index("dom") % 2).astype(jnp.int32).reshape(1)
    swap = [(0, 1), (1, 0)]
    inner = [(i, i ^ 1) for i in range(n_dom)]
    outer = [(i, (i - 1 if i % 2 == 0 else i + 1) % n_dom) for i in range(n_dom)]

    def across(value, step):
        if n_dom & (n_dom - 1) == 0:
            perm = [(i, i ^ step) for i in range(n_dom)]
        else:
            perm = [(i, (i + step) % n_dom) for i in range(n_dom)]
        return lax.ppermute(value, "dom", perm)

    def back(step):
        return step if n_dom & (n_dom - 1) == 0 else n_dom - step

    index = anchor_index.reshape(1, own)
    other_index = [
        lax.ppermute(index, "head", [(i, (i + s) % n_head) for i in range(n_head)])
        for s in range(1, n_head)
    ]
    other_index = other_index[0] if n_head == 2 else jnp.concatenate(other_index, axis=1)

    def head_sum(part):
        if n_head == 2:
            return part, lax.ppermute(part, "head", swap)
        return lax.psum(part, "head"), jnp.zeros_like(part)

    first, second = call(
        outgoing_kernel, [(halos, width)] * 2, [parity, send_index, features], smem=(0, 1)
    )
    first = lax.ppermute(first, "dom", inner)
    second = lax.ppermute(second, "dom", outer)
    pre, halo_mat, anchor_x = call(
        own_faces_kernel,
        [(rows, units), (rows, 2 * halos), (anchors, width)],
        [
            parity, face_live, head, index, other_index,
            features, faces, face_weight.reshape(1, -1), w_in,
        ],
        smem=(0, 1, 2, 3, 4),
        flops=2 * 10**9,
    )
    part, anchor_part = call(
        mlp_kernel,
        [(rows, width), (anchors, width)],
        [head, index, other_index, first, second, pre, halo_mat, w_in, w_out],
        smem=(0, 1, 2),
        flops=10**9,
    )
    anchor_part, anchor_recv = head_sum(anchor_part)
    part, recv = head_sum(part)
    d, d_t = call(grad_in_kernel, [(rows, width), (width, rows)], [out_grad, w_attn_out])
    (feat,) = call(anchor_kernel, [(anchors, width)], [anchor_x, anchor_part, anchor_recv])
    feats = [feat] + [across(feat, s) for s in range(1, n_dom)]
    mixed, q, q_t = call(
        query_kernel,
        [(rows, width), (rows, width), (width, rows)],
        [features, part, recv, w_query],
        flops=10**9,
    )
    feats = feats + [lax.ppermute(f, "aux", swap) for f in feats]
    half = n_dom * own
    att, keep, give = call(
        functools.partial(attention_kernel, len(feats), own),
        [(rows, width), (half, width), (half, width)],
        [head, *feats, q, q_t, d, d_t, w_key, w_value],
        smem=(0,),
        scratch=[pltpu.VMEM((half * 2 * (n_head - 1), width), F32)] if n_head > 2 else [],
        flops=2 * 10**9,
    )
    recv = lax.ppermute(give, "aux", swap)
    sums = call(functools.partial(add_kernel, own), [(own, width)] * n_dom, [keep, recv])
    sums = [sums[0]] + [across(sums[s], back(s)) for s in range(1, n_dom)]
    (output,) = call(output_kernel, [(rows, width)], [mixed, att, w_attn_out])
    (anchor_grad,) = call(sum_kernel, [(own, width)], sums)
    return output, anchor_grad


def solution(mesh):
    placed = (
        P(("groups", "dom", "aux"), None),
        P(("groups", "dom", "aux")),
        P(None, ("groups", "dom", "aux")),
        P(("groups", "dom", "aux")),
        P(None, ("groups", "dom", "aux")),
        P(("groups", "dom", "head", "aux")),
        P(None, "head"),
        P("head", None),
        P(),
        P(),
        P(),
        P(),
        P(("groups", "dom", "aux"), None),
    )
    return jax.shard_map(
        shards,
        mesh=mesh,
        in_specs=placed,
        out_specs=(P(("groups", "dom", "aux"), None), P(("groups", "dom", "head", "aux"), None)),
        check_vma=False,
    )
```

time: 141 us -> 48.8 us (0.35)
  waiting for transfers between devices: 54.5 us -> 14.3 us
  blocking collectives: 29.7 us -> 0 us
  other arithmetic: 16.9 us -> 0 us
  matrix products: 14.3 us -> 0 us
  starting transfers between devices: 5.25 us -> 18.8 us
  between operations: 15.1 us -> 1.56 us
  Pallas kernels: 0 us -> 10.5 us
    all_gather x4 -> x0, blocking collectives: 29.7 us -> none  [the longest x3 15 us: joined(): gathered = jax.tree.map(lambda a: lax.all_gather(a, axis), part)]
    unnamed x3 -> x0, waiting for transfers between devices: 29.6 us -> none
    psum x1 -> x0, waiting for transfers between devices: 23.7 us -> none  [shards(): mixed = features + lax.psum(matmul(hidden, w_out), 'head')]
    scatter-add x1 -> x0, other arithmetic: 15 us -> none  [shards(): gathered = jax.ops.segment_sum(messages, faces[0], num_segments=cell_rows)]
    dot_general x24 -> x0, matrix products: 14.3 us -> none  [matmul(): jnp.dot(left, right, precision=HIGH, preferred_element_type=jnp.float32)]
    ppermute x2 -> x16, starting transfers between devices: 5.17 us -> 18.8 us  [the longest x6 8.9 us: across(): return lax.ppermute(value, 'dom', perm)]
    ppermute x2 -> x16, waiting for transfers between devices: 1.08 us -> 14.3 us  [the longest x2 6.6 us: head_sum(): return (part, lax.ppermute(part, 'head', swap))]
    pallas_call x0 -> x10, Pallas kernels: none -> 10.5 us  [call(): pl.pallas_call(body, out_shape=[jax.ShapeDtypeStruct(s, F32) for s in out...]
  transfers between devices with their start and end apart: 4 -> 16, of which waited for: 4 -> 6; matrix products, arithmetic and copies ran while one was open for 2% -> 5% of each run, Pallas kernels for 0% -> 10%
where the time goes in v1:
time: 48.8 us; the launch traced here: 48.6 us
  starting transfers between devices  18.8 us (39%)
  waiting for transfers between devices  14.3 us (29%)
  Pallas kernels  10.5 us (22%)
  local copies, waits for them, and re-layouts  3.43 us (7%)
  between operations  1.56 us (3%)
    pallas_call x10, Pallas kernels, call(): pl.pallas_call(body, out_shape=[jax.ShapeDtypeStruct(s, F32) for s in out...  10.5 us
    ppermute x6, starting transfers between devices, across(): return lax.ppermute(value, 'dom', perm)  8.9 us
    ppermute x2, waiting for transfers between devices, head_sum(): return (part, lax.ppermute(part, 'head', swap))  6.6 us
    ppermute x6, waiting for transfers between devices, across(): return lax.ppermute(value, 'dom', perm)  5.74 us
    unnamed x26, local copies, waits for them, and re-layouts  3.42 us
    ppermute x1, starting transfers between devices, shards(): lax.ppermute(index, 'head', [(i, (i + s) % n_head) for i in range(n_head)])  2.94 us
    ppermute x1, starting transfers between devices, shards(): second = lax.ppermute(second, 'dom', outer)  2.47 us
    ppermute x2, starting transfers between devices, head_sum(): return (part, lax.ppermute(part, 'head', swap))  2.09 us
  transfers between devices with their start and end apart: 16, of which 6 were waited for; matrix products, arithmetic and copies ran while one was open for 5% of the time, Pallas kernels for 10%

profile of v1, /device:TPU:0, one launch (start us, length us, event | category | flops | bytes accessed | tf_op | source)
XLA Modules:
  0.0 48.6 jit_solution(13757052656342858446)
XLA Ops:
  0.6 0.6 %copy-done.7 = s32[32]{0:T(128)S(1)} copy-done((s32[32]{0:T(128)S(1)}, s32[32]{0:T(128)}, u32[]{:S(2)}) %copy-start.7) | copy-done | bytes 152
  1.3 2.9 %collective-permute-start = (s32[1,32]{1,0:T(1,128)S(1)}, s32[1,32]{1,0:T(1,128)S(1)}, u32[]{:S(2)}, u32[]{:S(2)}) collective-permute-start(s32[1,32]{1,0:T(1,128)S(1)} %bitcast.3), channel_id=1, source_target_pairs={{0,2},{2,0},{1,3},{3,1},{4,6},{6,4},{5,7},{7,5},{8,10},{10,8},{9,1... | collective-permute-start | bytes 392 | tf_op jit(solution)/shard_map/ppermute | solution.py:311
  4.2 1.1 %copy.18.x_ref = f32[256,192]{1,0:T(8,128)S(1)} copy(f32[256,192]{0,1:T(8,128)} %param.13) | data formatting | bytes 393216 | tf_op args[0]
  5.4 0.8 %shard_map.140 = (f32[32,192]{1,0:T(8,128)S(1)}, f32[32,192]{1,0:T(8,128)S(1)}) custom-call(s32[1]{0:T(128)} %bitcast.2.parity_ref, s32[2,32]{1,0:T(2,128)S(1)} %copy-done.6, f32[256,192]{1,0:T(8,128)S(1)} %copy.18.x_ref), custom_call_target="tpu_custom_call" | custom-call | flops 100000000 | bytes 1000000 | tf_op jit(solution)/shard_map/pallas_call | solution.py:45
  6.2 1.6 %collective-permute-start.1 = (f32[32,192]{1,0:T(8,128)S(1)}, f32[32,192]{1,0:T(8,128)S(1)}, u32[]{:S(2)}, u32[]{:S(2)}) collective-permute-start(f32[32,192]{1,0:T(8,128)S(1)} %get-tuple-element.21), channel_id=1, source_target_pairs={{0,4},{4,0},{8,12},{12,8},{1,5},{5,1},{9,13},{13,9},{2,6},{6,2},{1... | collective-permute-start | bytes 73736 | tf_op jit(solution)/shard_map/ppermute | solution.py:324
  7.8 2.5 %collective-permute-start.2 = (f32[32,192]{1,0:T(8,128)S(1)}, f32[32,192]{1,0:T(8,128)S(1)}, u32[]{:S(2)}, u32[]{:S(2)}) collective-permute-start(f32[32,192]{1,0:T(8,128)S(1)} %get-tuple-element.22), channel_id=1, source_target_pairs={{0,12},{4,8},{8,4},{12,0},{1,13},{5,9},{9,5},{13,1},{2,14},{6,10},... | collective-permute-start | bytes 73736 | tf_op jit(solution)/shard_map/ppermute | solution.py:325
  11.2 0.5 %copy-done.5 = s32[3,1536]{1,0:T(4,128)S(1)} copy-done((s32[3,1536]{1,0:T(4,128)S(1)}, s32[3,1536]{1,0:T(4,128)}, u32[]{:S(2)}) %copy-start.5) | copy-done | bytes 18456
  11.7 2.5 %shard_map.141 = (f32[256,384]{1,0:T(8,128)S(1)}, f32[256,64]{1,0:T(8,128)S(1)}, f32[64,192]{1,0:T(8,128)S(1)}) custom-call(s32[1]{0:T(128)} %bitcast.2.parity_ref, s32[1]{0:T(128)S(6)} %copy.21.live_ref, s32[1]{0:T(128)} %bitcast.head_ref, s32[1,32]{1,0:T(1,128)S(1)} %bitcast.4, s32[1,32]{1,0:T(1,128)S(1)} %collective-permute-done.other_ref, ...), custom_call_target="tpu_custom_call" | custom-call | flops 2000000000 | bytes 1000000 | tf_op jit(solution)/shard_map/pallas_call | solution.py:45
  14.3 1.5 %shard_map.142 = (f32[256,192]{1,0:T(8,128)S(1)}, f32[64,192]{1,0:T(8,128)S(1)}) custom-call(s32[1]{0:T(128)} %bitcast.head_ref, s32[1,32]{1,0:T(1,128)S(1)} %bitcast.5, s32[1,32]{1,0:T(1,128)S(1)} %collective-permute-done.other_ref, f32[32,192]{1,0:T(8,128)S(1)} %collective-permute-done.1.first_ref, f32[32,192]{1,0:T(8,128)S(1)} %collective-permute-done.2.second_ref, ...), custom_call_target="tpu_custom_call" | custom-call | flops 1000000000 | bytes 1000000 | tf_op jit(solution)/shard_map/pallas_call | solution.py:45
  15.8 0.6 %collective-permute-start.3 = (f32[256,192]{1,0:T(8,128)S(1)}, f32[256,192]{1,0:T(8,128)S(1)}, u32[]{:S(2)}, u32[]{:S(2)}) collective-permute-start(f32[256,192]{1,0:T(8,128)S(1)} %get-tuple-element.25.part_ref), channel_id=1, source_target_pairs={{0,2},{2,0},{1,3},{3,1},{4,6},{6,4},{5,7},{7,5},{8,10},{10,8},{9,1... | collective-permute-start | bytes 589832 | tf_op jit(solution)/shard_map/ppermute | solution.py:318
  16.4 1.5 %collective-permute-start.4 = (f32[64,192]{1,0:T(8,128)S(1)}, f32[64,192]{1,0:T(8,128)S(1)}, u32[]{:S(2)}, u32[]{:S(2)}) collective-permute-start(f32[64,192]{1,0:T(8,128)S(1)} %get-tuple-element.28.part_ref), channel_id=1, source_target_pairs={{0,2},{2,0},{1,3},{3,1},{4,6},{6,4},{5,7},{7,5},{8,10},{10,8},{9,1... | collective-permute-start | bytes 147464 | tf_op jit(solution)/shard_map/ppermute | solution.py:318
  17.9 6.6 %collective-permute-done.4.recv_ref = f32[64,192]{1,0:T(8,128)S(1)} collective-permute-done((f32[64,192]{1,0:T(8,128)S(1)}, f32[64,192]{1,0:T(8,128)S(1)}, u32[]{:S(2)}, u32[]{:S(2)}) %collective-permute-start.4) | collective-permute-done | bytes 49184 | tf_op jit(solution)/shard_map/ppermute | solution.py:318
  24.7 0.7 %collective-permute-start.5 = (f32[64,192]{1,0:T(8,128)S(1)}, f32[64,192]{1,0:T(8,128)S(1)}, u32[]{:S(2)}, u32[]{:S(2)}) collective-permute-start(f32[64,192]{1,0:T(8,128)S(1)} %shard_map.144.refs_0_), channel_id=1, source_target_pairs={{0,4},{4,0},{8,12},{12,8},{1,5},{5,1},{9,13},{13,9},{2,6},{6,2},{1... | collective-permute-start | bytes 147464 | tf_op jit(solution)/shard_map/ppermute | solution.py:304
  25.4 1.2 %collective-permute-start.6 = (f32[64,192]{1,0:T(8,128)S(1)}, f32[64,192]{1,0:T(8,128)S(1)}, u32[]{:S(2)}, u32[]{:S(2)}) collective-permute-start(f32[64,192]{1,0:T(8,128)S(1)} %shard_map.144.refs_0_), channel_id=1, source_target_pairs={{0,8},{4,12},{8,0},{12,4},{1,9},{5,13},{9,1},{13,5},{2,10},{6,14},... | collective-permute-start | bytes 147464 | tf_op jit(solution)/shard_map/ppermute | solution.py:304
  26.7 2.5 %collective-permute-start.7 = (f32[64,192]{1,0:T(8,128)S(1)}, f32[64,192]{1,0:T(8,128)S(1)}, u32[]{:S(2)}, u32[]{:S(2)}) collective-permute-start(f32[64,192]{1,0:T(8,128)S(1)} %shard_map.144.refs_0_), channel_id=1, source_target_pairs={{0,12},{4,8},{8,4},{12,0},{1,13},{5,9},{9,5},{13,1},{2,14},{6,10},... | collective-permute-start | bytes 147464 | tf_op jit(solution)/shard_map/ppermute | solution.py:304
  30.6 2.1 %collective-permute-done.7.refs_3_ = f32[64,192]{1,0:T(8,128)S(1)} collective-permute-done((f32[64,192]{1,0:T(8,128)S(1)}, f32[64,192]{1,0:T(8,128)S(1)}, u32[]{:S(2)}, u32[]{:S(2)}) %collective-permute-start.7) | collective-permute-done | bytes 49184 | tf_op jit(solution)/shard_map/ppermute | solution.py:304
  33.3 0.7 %collective-permute-done.11.refs_7_ = f32[64,192]{1,0:T(8,128)S(1)} collective-permute-done((f32[64,192]{1,0:T(8,128)S(1)}, f32[64,192]{1,0:T(8,128)S(1)}, u32[]{:S(2)}, u32[]{:S(2)}) %collective-permute-start.11) | collective-permute-done | bytes 49184 | tf_op jit(solution)/shard_map/ppermute | solution.py:354
  34.0 3.7 %shard_map.146 = (f32[256,192]{1,0:T(8,128)S(1)}, f32[128,192]{1,0:T(8,128)S(1)}, f32[128,192]{1,0:T(8,128)S(1)}) custom-call(s32[1]{0:T(128)} %bitcast.head_ref, f32[64,192]{1,0:T(8,128)S(1)} %shard_map.144.refs_0_, f32[64,192]{1,0:T(8,128)S(1)} %collective-permute-done.5.refs_1_, f32[64,192]{1,0:T(8,128)S(1)} %collective-permute-done.6.refs_2_, ...), custom_call_target="tpu_custom_call" | custom-call | flops 2000000000 | bytes 1000000 | tf_op jit(solution)/shard_map/pallas_call | solution.py:45
  37.9 1.2 %collective-permute-done.12.recv_ref = f32[128,192]{1,0:T(8,128)S(1)} collective-permute-done((f32[128,192]{1,0:T(8,128)S(1)}, f32[128,192]{1,0:T(8,128)S(1)}, u32[]{:S(2)}, u32[]{:S(2)}) %collective-permute-start.12) | collective-permute-done | bytes 98336 | tf_op jit(solution)/shard_map/ppermute | solution.py:364
  39.2 3.0 %collective-permute-start.14 = (f32[32,192]{1,0:T(8,128)S(1)}, f32[32,192]{1,0:T(8,128)S(1)}, u32[]{:S(2)}, u32[]{:S(2)}) collective-permute-start(f32[32,192]{1,0:T(8,128)S(1)} %get-tuple-element.38), channel_id=1, source_target_pairs={{0,8},{4,12},{8,0},{12,4},{1,9},{5,13},{9,1},{13,5},{2,10},{6,14},... | collective-permute-start | bytes 73736 | tf_op jit(solution)/shard_map/ppermute | solution.py:304
  42.3 1.3 %collective-permute-start.15 = (f32[32,192]{1,0:T(8,128)S(1)}, f32[32,192]{1,0:T(8,128)S(1)}, u32[]{:S(2)}, u32[]{:S(2)}) collective-permute-start(f32[32,192]{1,0:T(8,128)S(1)} %get-tuple-element.39), channel_id=1, source_target_pairs={{0,12},{4,8},{8,4},{12,0},{1,13},{5,9},{9,5},{13,1},{2,14},{6,10},... | collective-permute-start | bytes 73736 | tf_op jit(solution)/shard_map/ppermute | solution.py:304
  43.9 0.8 %copy.20 = f32[256,192]{0,1:T(8,128)} copy(f32[256,192]{1,0:T(8,128)S(1)} %shard_map.147) | data formatting | bytes 393216
  44.7 3.3 %collective-permute-done.15.refs_3_ = f32[32,192]{1,0:T(8,128)S(1)} collective-permute-done((f32[32,192]{1,0:T(8,128)S(1)}, f32[32,192]{1,0:T(8,128)S(1)}, u32[]{:S(2)}, u32[]{:S(2)}) %collective-permute-start.15) | collective-permute-done | bytes 24608 | tf_op jit(solution)/shard_map/ppermute | solution.py:304
  48.0 0.6 %shard_map.149 = f32[32,192]{1,0:T(8,128)} custom-call(f32[32,192]{1,0:T(8,128)S(1)} %get-tuple-element.36.refs_0_, f32[32,192]{1,0:T(8,128)S(1)} %collective-permute-done.13.refs_1_, f32[32,192]{1,0:T(8,128)S(1)} %collective-permute-done.14.refs_2_, f32[32,192]{1,0:T(8,128)S(1)} %collective-permute-done.15.refs_3_), custom_call_target="tpu_custom_call" | custom-call | flops 100000000 | bytes 1000000 | tf_op jit(solution)/shard_map/pallas_call | solution.py:45
  (45 shorter events, 2.9 us)
Async XLA Ops:
  1.3 9.9 %collective-permute-start = (s32[1,32]{1,0:T(1,128)S(1)}, s32[1,32]{1,0:T(1,128)S(1)}, u32[]{:S(2)}, u32[]{:S(2)}) collective-permute-start(s32[1,32]{1,0:T(1,128)S(1)} %bitcast.3), channel_id=1, source_target_pairs={{0,2},{2,0},{1,3},{3,1},{4,6},{6,4},{5,7},{7,5},{8,10},{10,8},{9,1... | collective-permute-start | bytes 392 | tf_op jit(solution)/shard_map/ppermute | solution.py:311
  4.2 6.7 %copy-start.10 = (f32[1536]{0:T(1024)S(1)}, f32[1536]{0:T(1024)}, u32[]{:S(2)}) copy-start(f32[1536]{0:T(1024)} %param.14) | copy-start | bytes 18436
  4.2 6.8 %copy-start.8 = (f32[384,192]{0,1:T(8,128)S(1)}, f32[384,192]{0,1:T(8,128)}, u32[]{:S(2)}) copy-start(f32[384,192]{0,1:T(8,128)} %param.20) | copy-start | bytes 884740
  5.3 5.9 %copy-start.1 = (f32[384,384]{1,0:T(8,128)S(1)}, f32[384,384]{1,0:T(8,128)}, u32[]{:S(2)}) copy-start(f32[384,384]{1,0:T(8,128)} %w_in_ref.3) | copy-start | bytes 1769476
  6.2 8.1 %collective-permute-start.1 = (f32[32,192]{1,0:T(8,128)S(1)}, f32[32,192]{1,0:T(8,128)S(1)}, u32[]{:S(2)}, u32[]{:S(2)}) collective-permute-start(f32[32,192]{1,0:T(8,128)S(1)} %get-tuple-element.21), channel_id=1, source_target_pairs={{0,4},{4,0},{8,12},{12,8},{1,5},{5,1},{9,13},{13,9},{2,6},{6,2},{1... | collective-permute-start | bytes 73736 | tf_op jit(solution)/shard_map/ppermute | solution.py:324
  7.8 6.4 %collective-permute-start.2 = (f32[32,192]{1,0:T(8,128)S(1)}, f32[32,192]{1,0:T(8,128)S(1)}, u32[]{:S(2)}, u32[]{:S(2)}) collective-permute-start(f32[32,192]{1,0:T(8,128)S(1)} %get-tuple-element.22), channel_id=1, source_target_pairs={{0,12},{4,8},{8,4},{12,0},{1,13},{5,9},{9,5},{13,1},{2,14},{6,10},... | collective-permute-start | bytes 73736 | tf_op jit(solution)/shard_map/ppermute | solution.py:325
  15.8 13.3 %copy-start.9 = (f32[256,192]{0,1:T(8,128)S(1)}, f32[256,192]{0,1:T(8,128)}, u32[]{:S(2)}) copy-start(f32[256,192]{0,1:T(8,128)} %param.25) | copy-start | bytes 589828
  15.8 16.9 %collective-permute-start.3 = (f32[256,192]{1,0:T(8,128)S(1)}, f32[256,192]{1,0:T(8,128)S(1)}, u32[]{:S(2)}, u32[]{:S(2)}) collective-permute-start(f32[256,192]{1,0:T(8,128)S(1)} %get-tuple-element.25.part_ref), channel_id=1, source_target_pairs={{0,2},{2,0},{1,3},{3,1},{4,6},{6,4},{5,7},{7,5},{8,10},{10,8},{9,1... | collective-permute-start | bytes 589832 | tf_op jit(solution)/shard_map/ppermute | solution.py:318
  16.4 8.1 %collective-permute-start.4 = (f32[64,192]{1,0:T(8,128)S(1)}, f32[64,192]{1,0:T(8,128)S(1)}, u32[]{:S(2)}, u32[]{:S(2)}) collective-permute-start(f32[64,192]{1,0:T(8,128)S(1)} %get-tuple-element.28.part_ref), channel_id=1, source_target_pairs={{0,2},{2,0},{1,3},{3,1},{4,6},{6,4},{5,7},{7,5},{8,10},{10,8},{9,1... | collective-permute-start | bytes 147464 | tf_op jit(solution)/shard_map/ppermute | solution.py:318
  24.7 4.6 %copy-start = (f32[192,192]{1,0:T(8,128)S(1)}, f32[192,192]{1,0:T(8,128)}, u32[]{:S(2)}) copy-start(f32[192,192]{1,0:T(8,128)} %w_ref.5) | copy-start | bytes 442372
  24.7 5.1 %collective-permute-start.5 = (f32[64,192]{1,0:T(8,128)S(1)}, f32[64,192]{1,0:T(8,128)S(1)}, u32[]{:S(2)}, u32[]{:S(2)}) collective-permute-start(f32[64,192]{1,0:T(8,128)S(1)} %shard_map.144.refs_0_), channel_id=1, source_target_pairs={{0,4},{4,0},{8,12},{12,8},{1,5},{5,1},{9,13},{13,9},{2,6},{6,2},{1... | collective-permute-start | bytes 147464 | tf_op jit(solution)/shard_map/ppermute | solution.py:304
  25.4 5.2 %collective-permute-start.6 = (f32[64,192]{1,0:T(8,128)S(1)}, f32[64,192]{1,0:T(8,128)S(1)}, u32[]{:S(2)}, u32[]{:S(2)}) collective-permute-start(f32[64,192]{1,0:T(8,128)S(1)} %shard_map.144.refs_0_), channel_id=1, source_target_pairs={{0,8},{4,12},{8,0},{12,4},{1,9},{5,13},{9,1},{13,5},{2,10},{6,14},... | collective-permute-start | bytes 147464 | tf_op jit(solution)/shard_map/ppermute | solution.py:304
  26.7 6.1 %collective-permute-start.7 = (f32[64,192]{1,0:T(8,128)S(1)}, f32[64,192]{1,0:T(8,128)S(1)}, u32[]{:S(2)}, u32[]{:S(2)}) collective-permute-start(f32[64,192]{1,0:T(8,128)S(1)} %shard_map.144.refs_0_), channel_id=1, source_target_pairs={{0,12},{4,8},{8,4},{12,0},{1,13},{5,9},{9,5},{13,1},{2,14},{6,10},... | collective-permute-start | bytes 147464 | tf_op jit(solution)/shard_map/ppermute | solution.py:304
  29.3 3.5 %copy-start.2 = (f32[192,192]{1,0:T(8,128)S(1)}, f32[192,192]{1,0:T(8,128)}, u32[]{:S(2)}) copy-start(f32[192,192]{1,0:T(8,128)} %w_ref.3) | copy-start | bytes 442372
  29.7 4.3 %copy-start.3 = (f32[192,192]{1,0:T(8,128)S(1)}, f32[192,192]{1,0:T(8,128)}, u32[]{:S(2)}) copy-start(f32[192,192]{1,0:T(8,128)} %refs_12_.1) | copy-start | bytes 442372
  29.7 4.3 %copy-start.4 = (f32[192,192]{1,0:T(8,128)S(1)}, f32[192,192]{1,0:T(8,128)}, u32[]{:S(2)}) copy-start(f32[192,192]{1,0:T(8,128)} %refs_13_.1) | copy-start | bytes 442372
  29.7 3.5 %collective-permute-start.8 = (f32[64,192]{1,0:T(8,128)S(1)}, f32[64,192]{1,0:T(8,128)S(1)}, u32[]{:S(2)}, u32[]{:S(2)}) collective-permute-start(f32[64,192]{1,0:T(8,128)S(1)} %shard_map.144.refs_0_), channel_id=1, source_target_pairs={{0,1},{1,0},{2,3},{3,2},{4,5},{5,4},{6,7},{7,6},{8,9},{9,8},{10,11... | collective-permute-start | bytes 147464 | tf_op jit(solution)/shard_map/ppermute | solution.py:354
  29.8 3.4 %collective-permute-start.9 = (f32[64,192]{1,0:T(8,128)S(1)}, f32[64,192]{1,0:T(8,128)S(1)}, u32[]{:S(2)}, u32[]{:S(2)}) collective-permute-start(f32[64,192]{1,0:T(8,128)S(1)} %collective-permute-done.5.refs_1_), channel_id=1, source_target_pairs={{0,1},{1,0},{2,3},{3,2},{4,5},{5,4},{6,7},{7,6},{8,9},{9,8},{10,11... | collective-permute-start | bytes 147464 | tf_op jit(solution)/shard_map/ppermute | solution.py:354
  30.6 2.6 %collective-permute-start.10 = (f32[64,192]{1,0:T(8,128)S(1)}, f32[64,192]{1,0:T(8,128)S(1)}, u32[]{:S(2)}, u32[]{:S(2)}) collective-permute-start(f32[64,192]{1,0:T(8,128)S(1)} %collective-permute-done.6.refs_2_), channel_id=1, source_target_pairs={{0,1},{1,0},{2,3},{3,2},{4,5},{5,4},{6,7},{7,6},{8,9},{9,8},{10,11... | collective-permute-start | bytes 147464 | tf_op jit(solution)/shard_map/ppermute | solution.py:354
  32.7 1.3 %collective-permute-start.11 = (f32[64,192]{1,0:T(8,128)S(1)}, f32[64,192]{1,0:T(8,128)S(1)}, u32[]{:S(2)}, u32[]{:S(2)}) collective-permute-start(f32[64,192]{1,0:T(8,128)S(1)} %collective-permute-done.7.refs_3_), channel_id=1, source_target_pairs={{0,1},{1,0},{2,3},{3,2},{4,5},{5,4},{6,7},{7,6},{8,9},{9,8},{10,11... | collective-permute-start | bytes 147464 | tf_op jit(solution)/shard_map/ppermute | solution.py:354
  37.7 1.4 %collective-permute-start.12 = (f32[128,192]{1,0:T(8,128)S(1)}, f32[128,192]{1,0:T(8,128)S(1)}, u32[]{:S(2)}, u32[]{:S(2)}) collective-permute-start(f32[128,192]{1,0:T(8,128)S(1)} %get-tuple-element.35), channel_id=1, source_target_pairs={{0,1},{1,0},{2,3},{3,2},{4,5},{5,4},{6,7},{7,6},{8,9},{9,8},{10,11... | collective-permute-start | bytes 294920 | tf_op jit(solution)/shard_map/ppermute | solution.py:364
  39.1 5.5 %collective-permute-start.13 = (f32[32,192]{1,0:T(8,128)S(1)}, f32[32,192]{1,0:T(8,128)S(1)}, u32[]{:S(2)}, u32[]{:S(2)}) collective-permute-start(f32[32,192]{1,0:T(8,128)S(1)} %get-tuple-element.37), channel_id=1, source_target_pairs={{0,4},{4,0},{8,12},{12,8},{1,5},{5,1},{9,13},{13,9},{2,6},{6,2},{1... | collective-permute-start | bytes 73736 | tf_op jit(solution)/shard_map/ppermute | solution.py:304
  39.2 5.4 %collective-permute-start.14 = (f32[32,192]{1,0:T(8,128)S(1)}, f32[32,192]{1,0:T(8,128)S(1)}, u32[]{:S(2)}, u32[]{:S(2)}) collective-permute-start(f32[32,192]{1,0:T(8,128)S(1)} %get-tuple-element.38), channel_id=1, source_target_pairs={{0,8},{4,12},{8,0},{12,4},{1,9},{5,13},{9,1},{13,5},{2,10},{6,14},... | collective-permute-start | bytes 73736 | tf_op jit(solution)/shard_map/ppermute | solution.py:304
  42.3 5.7 %collective-permute-start.15 = (f32[32,192]{1,0:T(8,128)S(1)}, f32[32,192]{1,0:T(8,128)S(1)}, u32[]{:S(2)}, u32[]{:S(2)}) collective-permute-start(f32[32,192]{1,0:T(8,128)S(1)} %get-tuple-element.39), channel_id=1, source_target_pairs={{0,12},{4,8},{8,4},{12,0},{1,13},{5,9},{9,5},{13,1},{2,14},{6,10},... | collective-permute-start | bytes 73736 | tf_op jit(solution)/shard_map/ppermute | solution.py:304
  (3 other events, 2.5 us)

commit v2 on v0

v2 whole, which is shorter than its diff:
```python
import functools
import math

import jax
import jax.numpy as jnp
from jax import lax
from jax.experimental import pallas as pl
from jax.experimental.pallas import tpu as pltpu
from jax.sharding import PartitionSpec as P

HEADS = 3
DH = 64
NN = (((1,), (0,)), ((), ()))
NT = (((1,), (1,)), ((), ()))
TN = (((0,), (0,)), ((), ()))
BF = jnp.bfloat16
F32 = jnp.float32
I32 = jnp.int32
LOG2E = math.log2(math.e)


def dot_bf(left, right, dims=NN):
    return lax.dot_general(left, right, dims, preferred_element_type=F32)


def split(value):
    top = value.astype(BF)
    return top, (value - top.astype(F32)).astype(BF)


def dot_halves(left, right, dims=NN):
    rows = left[0].shape[0]
    both = dot_bf(jnp.concatenate(left, axis=0), right[0], dims)
    return both[:rows] + (both[rows:] + dot_bf(left[0], right[1], dims))


def dot(left, right, dims=NN):
    return dot_halves(split(left), split(right), dims)


def layer_norm(value, axis=-1):
    mean = jnp.mean(value, axis=axis, keepdims=True)
    centred = value - mean
    spread = jnp.mean(centred * centred, axis=axis, keepdims=True)
    return centred * lax.rsqrt(spread + 1e-05)


def call(body, outs, ins, smem=(), hbm=(), scratch=(), flops=10**8):
    def space(i):
        return pltpu.SMEM if i in smem else pltpu.HBM if i in hbm else pltpu.VMEM

    return pl.pallas_call(
        body,
        out_shape=[jax.ShapeDtypeStruct(o[:2], o[2] if len(o) > 2 else F32) for o in outs],
        in_specs=[pl.BlockSpec(memory_space=space(i)) for i in range(len(ins))],
        out_specs=[pl.BlockSpec(memory_space=pltpu.VMEM)] * len(outs),
        scratch_shapes=list(scratch),
        compiler_params=pltpu.CompilerParams(vmem_limit_bytes=48 * 2**20),
        cost_estimate=pl.CostEstimate(flops=flops, bytes_accessed=10**6, transcendentals=0),
    )(*[
        pltpu.with_memory_space_constraint(x, pltpu.HBM) if i in hbm else x
        for i, x in enumerate(ins)
    ])


def chosen(index, rows):
    places = lax.broadcasted_iota(I32, (rows, index.shape[1]), 0)
    return jnp.where(places == index, 1.0, 0.0).astype(BF)


def exact_parts(value):
    top, mid = split(value)
    return top, mid, (value - top.astype(F32) - mid.astype(F32)).astype(BF)


def outgoing_kernel(
    send_hbm, index_hbm, faces_hbm, x_t_hbm, w_in_hbm,
    lower_ref, upper_ref, index_ref, faces_ref, x_t_ref, w_in_ref, send_ref, sems,
):
    copies = [
        pltpu.make_async_copy(source, target, sems.at[i])
        for i, (source, target) in enumerate(
            [
                (send_hbm, send_ref), (x_t_hbm, x_t_ref), (index_hbm, index_ref),
                (faces_hbm, faces_ref), (w_in_hbm, w_in_ref),
            ]
        )
    ]
    for copy in copies:
        copy.start()
    copies[0].wait()
    halos = lower_ref.shape[0]
    index = jnp.concatenate([send_ref[0:1, :], send_ref[1:2, :]], axis=1)
    pick = chosen(index, x_t_ref.shape[1])
    copies[1].wait()
    top, mid, low = exact_parts(x_t_ref[...])
    sent = layer_norm((dot_bf(top, pick) + dot_bf(mid, pick) + dot_bf(low, pick)).T)
    lower_ref[...] = sent[:halos]
    upper_ref[...] = sent[halos:]
    for copy in copies[2:]:
        copy.wait()


def small_chosen(index, rows, value):
    places = lax.broadcasted_iota(I32, (rows, index.shape[1]), 0).astype(F32).astype(BF)
    return jnp.where(places == index, value, jnp.zeros_like(value))


def own_faces_kernel(
    live_ref, x_t_ref, faces_ref, weight_ref, w_in_ref,
    pre_t_ref, halo_mat_ref, w_top_ref, w_low_ref,
):
    width, rows = x_t_ref.shape
    units = pre_t_ref.shape[0]
    halos = halo_mat_ref.shape[0] // 2
    slots = faces_ref.shape[1]
    w_top, w_low = split(
        jnp.concatenate([w_in_ref[:width].T, w_in_ref[width:].T], axis=0)
    )
    w_top_ref[...] = w_top[units:]
    w_low_ref[...] = w_low[units:]
    normed_t = split(layer_norm(x_t_ref[...], axis=0))
    straight = dot_halves((w_top, w_low), normed_t)
    kind = faces_ref[1:2, :]
    receiver = faces_ref[0:1, :].astype(F32).astype(BF)
    source = faces_ref[2:3, :].astype(F32)
    cells = jnp.where(kind == 0, source, -1.0).astype(BF)
    halo_rows = jnp.where(kind == 0, -1.0, jnp.where(kind == 1, source, source + halos))
    halo_rows = halo_rows.astype(BF)
    live = lax.broadcasted_iota(I32, (1, slots), 1) < live_ref[...]
    top, low = split(jnp.where(live, weight_ref[...], 0.0))
    out_of = jnp.concatenate(
        [
            small_chosen(cells, rows, top), small_chosen(halo_rows, 2 * halos, top),
            small_chosen(cells, rows, low), small_chosen(halo_rows, 2 * halos, low),
        ],
        axis=0,
    )
    both = dot_bf(out_of, small_chosen(receiver, rows, jnp.ones_like(receiver)), NT)
    sources = rows + 2 * halos
    matrix_t = both[:sources] + both[sources:]
    halo_mat_ref[...] = matrix_t[rows:]
    pre_t_ref[...] = straight[:units] + dot(straight[units:], matrix_t[:rows])


def every_index(head_ref, own_ref, other_ref):
    own = own_ref.shape[1]
    if other_ref.shape[1] > own:
        return other_ref[...]
    first = head_ref[0] == 0
    return jnp.concatenate(
        [
            jnp.where(first, own_ref[...], other_ref[...]),
            jnp.where(first, other_ref[...], own_ref[...]),
        ],
        axis=1,
    )


def hidden_kernel(
    head_ref, own_ref, other_ref, lower_ref, upper_ref, pre_t_ref, halo_mat_ref, w_top_ref,
    w_low_ref, w_out_t_ref, top_ref, low_ref, anchor_ref,
):
    halo_t = jnp.concatenate([lower_ref[...], upper_ref[...]], axis=0).T
    halo_agg = dot(halo_t, halo_mat_ref[...])
    pre = pre_t_ref[...] + dot_halves((w_top_ref[...], w_low_ref[...]), split(halo_agg))
    units, rows = pre.shape
    halves = split(0.5 * pre * (1.0 + lax.erf(pre * math.sqrt(0.5))))
    pick = chosen(every_index(head_ref, own_ref, other_ref), rows)
    anchors = dot_bf(jnp.concatenate(halves, axis=0), pick).astype(BF)
    part = dot_halves(split(w_out_t_ref[...]), (anchors[:units], anchors[units:]))
    anchor_ref[...] = part.T
    top_ref[...], low_ref[...] = halves


def pairs_right(value):
    top, low = split(value)
    return jnp.concatenate([top, top, low, low], axis=1)


def wide(value):
    return jnp.concatenate(split(value), axis=1)


def by_head(value, build):
    return jnp.concatenate(
        [build(value[:, h * DH : (h + 1) * DH]) for h in range(HEADS)], axis=1
    )


def pairs(value_t):
    out = []
    for h in range(HEADS):
        out += split(value_t[h * DH : (h + 1) * DH]) * 2
    return jnp.concatenate(out, axis=0)


def twice(value_t):
    out = []
    for h in range(HEADS):
        out += [value_t[h * DH : (h + 1) * DH]] * 2
    return out


def rest_kernel(
    head_ref, own_ref, other_ref, top_ref, low_ref, w_out_t_ref, x_t_ref, g_t_ref, w_ref,
    wk_ref, wv_ref,
    part_t_ref, anchor_x_ref, d_t_ref, d_pairs_ref, d_wide_ref, k_top_ref, k_low_ref, v_top_ref,
    v_low_ref, back_top_ref, back_low_ref,
):
    part_t_ref[...] = dot_halves(split(w_out_t_ref[...]), (top_ref[...], low_ref[...]))
    pick = chosen(every_index(head_ref, own_ref, other_ref), x_t_ref.shape[1])
    anchor_x_ref[...] = sum(dot_bf(piece, pick) for piece in exact_parts(x_t_ref[...])).T
    d_t = dot(w_ref[...], g_t_ref[...])
    d_t_ref[...] = d_t
    d_pairs_ref[...] = pairs(d_t)
    d_wide_ref[...] = by_head(d_t.T, wide)
    k_top_ref[...], k_low_ref[...] = split(wk_ref[...])
    v_top_ref[...], v_low_ref[...] = split(wv_ref[...])
    back = jnp.concatenate(twice(wk_ref[...].T) + twice(wv_ref[...].T), axis=0)
    back_top_ref[...], back_low_ref[...] = split(back)


def anchor_kernel(x_ref, part_ref, recv_ref, out_ref):
    out_ref[...] = layer_norm(x_ref[...] + (part_ref[...] + recv_ref[...]))


def query_kernel(x_t_ref, part_ref, recv_ref, w_ref, mixed_t_ref, q_pairs_ref, q_wide_ref):
    mixed_t = x_t_ref[...] + (part_ref[...] + recv_ref[...])
    mixed_t_ref[...] = mixed_t
    q_t = dot(w_ref[...].T, layer_norm(mixed_t, axis=0)) * (1.0 / math.sqrt(DH))
    q_pairs_ref[...] = pairs(q_t * LOG2E)
    q_wide_ref[...] = by_head(q_t.T, wide)


def join_kernel(own, _, *refs):
    out = refs[-1]
    blocks = len(refs) - 1
    for place in range(refs[0].shape[0] // own):
        for i, ref in enumerate(refs[:-1]):
            out[pl.ds((place * blocks + i) * own, own), :] = ref[pl.ds(place * own, own), :]


CHUNK = 512


def over_chunks(count, step, carry):
    size = min(count, CHUNK)
    if count == size:
        return step(0, size, carry)
    return lax.fori_loop(
        0, count // size, lambda i, c: step(pl.multiple_of(i * size, size), size, c), carry
    )


def of_head(h, wide_by):
    return slice(wide_by * h * DH, wide_by * (h + 1) * DH)


def score(head_ref, feat_ref, q_pairs_ref, d_pairs_ref, wk, wv, s_ref, dp_ref, v_ref):
    rows = q_pairs_ref.shape[1]
    mine = dp_ref.shape[0]

    def step(start, size, carry):
        at = pl.ds(start, size)
        feat = split(feat_ref[at, :])
        k = dot_halves(feat, wk)
        v = dot_halves(feat, wv)
        v_ref[at, :] = by_head(v, wide)
        for h in range(HEADS):
            s_ref[at, h * rows : (h + 1) * rows] = dot_bf(
                pairs_right(k[:, of_head(h, 1)]), q_pairs_ref[of_head(h, 4), :]
            )
        return carry

    over_chunks(feat_ref.shape[0], step, 0)
    place = pl.ds(pl.multiple_of(head_ref[0] * mine, mine), mine)
    for h in range(HEADS):
        v = v_ref[place, of_head(h, 2)]
        top, low = v[:, :DH], v[:, DH:]
        v_pairs = jnp.concatenate([top, top, low, low], axis=1)
        dp_ref[:, h * rows : (h + 1) * rows] = dot_bf(v_pairs, d_pairs_ref[of_head(h, 4), :])


def score_kernel(
    head_ref, feat_ref, q_pairs_ref, d_pairs_ref, k_top_ref, k_low_ref, v_top_ref, v_low_ref,
    s_ref, dp_ref, v_ref,
):
    wk, wv = (k_top_ref[...], k_low_ref[...]), (v_top_ref[...], v_low_ref[...])
    score(head_ref, feat_ref, q_pairs_ref, d_pairs_ref, wk, wv, s_ref, dp_ref, v_ref)


def attention_kernel(
    head_ref, s_a_ref, dp_a_ref, v_a_ref, feat_ref, q_pairs_ref, q_wide_ref, d_t_ref,
    d_pairs_ref, d_wide_ref, k_top_ref, k_low_ref, v_top_ref, v_low_ref, back_top_ref,
    back_low_ref, att_t_ref, keep_ref, give_ref, s_b_ref, dp_b_ref, v_b_ref,
):
    wk, wv = (k_top_ref[...], k_low_ref[...]), (v_top_ref[...], v_low_ref[...])
    score(head_ref, feat_ref, q_pairs_ref, d_pairs_ref, wk, wv, s_b_ref, dp_b_ref, v_b_ref)
    rows = d_t_ref.shape[1]
    count = feat_ref.shape[0]
    mine = dp_a_ref.shape[0]
    halves = ((s_a_ref, v_a_ref), (s_b_ref, v_b_ref))
    place = pl.ds(pl.multiple_of(head_ref[0] * mine, mine), mine)
    heads = range(HEADS)
    cells = [slice(h * rows, (h + 1) * rows) for h in heads]
    tops, totals, accs = [], [], []
    for h in heads:

        def highest(start, size, top, h=h):
            for s, _ in halves:
                part = jnp.max(s[pl.ds(start, size), cells[h]], axis=0, keepdims=True)
                top = part if top is None else jnp.maximum(top, part)
            return top

        low = None if count <= CHUNK else jnp.full((1, rows), -jnp.inf, F32)
        tops.append(over_chunks(count, highest, low))
    for h in heads:

        def weigh(start, size, state, h=h):
            total, acc = state
            at = pl.ds(start, size)
            for s, v in halves:
                expo = jnp.exp2(s[at, cells[h]] - tops[h])
                top, low = split(expo)
                value = v[at, of_head(h, 2)]
                total = total + jnp.sum(expo, axis=0, keepdims=True)
                acc = acc + (dot_bf(value, top, TN) + dot_bf(value, low, TN))
            return total, acc

        start = (jnp.zeros((1, rows), F32), jnp.zeros((2 * DH, rows), F32))
        total, acc = over_chunks(count, weigh, start)
        totals.append(total)
        accs.append(acc)
    grads_k, grads_v = [], []
    for h in heads:
        inverse = 1.0 / totals[h]
        att = (accs[h][:DH] + accs[h][DH:]) * inverse
        att_t_ref[of_head(h, 1), :] = att
        delta = jnp.sum(d_t_ref[of_head(h, 1), :] * att, axis=0, keepdims=True)
        own = jnp.concatenate([s[place, cells[h]] for s, _ in halves], axis=0)
        d_prob = jnp.concatenate([dp_a_ref[:, cells[h]], dp_b_ref[:, cells[h]]], axis=0)
        probs = jnp.exp2(own - tops[h]) * inverse
        s_top, s_low = split(probs * (d_prob - delta))
        p_top, p_low = split(probs)
        q_wide, d_wide = q_wide_ref[:, of_head(h, 2)], d_wide_ref[:, of_head(h, 2)]
        grads_k.append(dot_bf(s_top, q_wide) + dot_bf(s_low, q_wide))
        grads_v.append(dot_bf(p_top, d_wide) + dot_bf(p_low, d_wide))
    grad = dot_halves(
        split(jnp.concatenate(grads_k + grads_v, axis=1)), (back_top_ref[...], back_low_ref[...])
    )
    keep_ref[...] = grad[:mine]
    give_ref[...] = grad[mine:]


def add_kernel(own, keep_ref, recv_ref, *outs):
    for i, out in enumerate(outs):
        rows = pl.ds(i * own, own)
        out[...] = keep_ref[rows, :] + recv_ref[rows, :]


def output_kernel(mixed_t_ref, att_t_ref, w_ref, out_t_ref):
    out_t_ref[...] = mixed_t_ref[...] + dot(w_ref[...].T, att_t_ref[...])


def sum_kernel(*refs):
    total = refs[0][...]
    for ref in refs[1:-1]:
        total = total + ref[...]
    refs[-1][...] = total


def shards(
    features,
    face_weight,
    faces,
    face_live,
    send_index,
    anchor_index,
    w_in,
    w_out,
    w_query,
    w_key,
    w_value,
    w_attn_out,
    out_grad,
):
    rows, width = features.shape
    halos = send_index.shape[1]
    units = w_in.shape[1]
    own = anchor_index.shape[0]
    n_dom, n_head, n_aux = (lax.axis_size(a) for a in ("dom", "head", "aux"))
    assert n_aux == 2
    anchors = own * n_head
    mine = own * n_dom
    count = anchors * n_dom
    head = lax.axis_index("head").astype(I32).reshape(1)
    swap = [(0, 1), (1, 0)]
    doubling = n_dom & (n_dom - 1) == 0

    def along(value, step):
        return lax.ppermute(value, "dom", [(i, (i + step) % n_dom) for i in range(n_dom)])

    def across(value, step):
        if doubling:
            return lax.ppermute(value, "dom", [(i, i ^ step) for i in range(n_dom)])
        return along(value, step)

    def head_sum(part):
        if n_head == 2:
            return part, lax.ppermute(part, "head", swap)
        return lax.psum(part, "head"), jnp.zeros_like(part)

    x_t, g_t, w_out_t = features.T, out_grad.T, w_out.T
    to_lower, to_upper, index, faces, x_t, w_in = call(
        outgoing_kernel,
        [
            (halos, width), (halos, width), (1, own, I32), (*faces.shape, I32), (width, rows),
            w_in.shape,
        ],
        [send_index, anchor_index.reshape(1, own), faces, x_t, w_in],
        hbm=range(5),
        scratch=[pltpu.VMEM((2, halos), I32), pltpu.SemaphoreType.DMA((5,))],
    )
    from_upper = along(to_lower, n_dom - 1)
    from_lower = along(to_upper, 1)
    if n_head == 2:
        other_index = lax.ppermute(index, "head", swap)
    else:
        other_index = lax.all_gather(index, "head").reshape(1, anchors)
    pre_t, halo_mat, w_top, w_low = call(
        own_faces_kernel,
        [(units, rows), (2 * halos, rows)] + [(units, width, BF)] * 2,
        [face_live.reshape(1, 1), x_t, faces, face_weight.reshape(1, -1), w_in],
        flops=2 * 10**9,
    )
    top, low, anchor_part = call(
        hidden_kernel,
        [(units, rows, BF), (units, rows, BF), (anchors, width)],
        [
            head, index, other_index, from_lower, from_upper, pre_t, halo_mat, w_top, w_low,
            w_out_t,
        ],
        smem=(0,),
        flops=10**9,
    )
    anchor_part, anchor_recv = head_sum(anchor_part)
    part, anchor_x, d_t, d_pairs, d_wide, *weights = call(
        rest_kernel,
        [
            (width, rows), (anchors, width), (width, rows), (4 * width, rows, BF),
            (rows, 2 * width, BF),
        ]
        + [(width, width, BF)] * 4
        + [(4 * width, width, BF)] * 2,
        [
            head, index, other_index, top, low, w_out_t, x_t, g_t, w_attn_out, w_key, w_value,
        ],
        smem=(0,),
        flops=10**9,
    )
    part, recv = head_sum(part)
    (feat,) = call(
        anchor_kernel,
        [(anchors, width)],
        [anchor_x, anchor_part, anchor_recv],
        flops=5 * 10**9,
    )
    feats = [feat] + [across(feat, s) for s in range(1, n_dom)]
    mixed, q_pairs, q_wide = call(
        query_kernel,
        [(width, rows), (4 * width, rows, BF), (rows, 2 * width, BF)],
        [x_t, part, recv, w_query],
        flops=10**9,
    )
    (feat_a,) = call(functools.partial(join_kernel, own), [(count, width)], [mixed] + feats)
    feat_b = lax.ppermute(feat_a, "aux", swap)
    sizes = [(count, HEADS * rows), (mine, HEADS * rows), (count, 2 * width, BF)]
    s_a, dp_a, v_a = call(
        score_kernel,
        sizes,
        [head, feat_a, q_pairs, d_pairs, *weights[:4]],
        smem=(0,),
        flops=10**9,
    )
    att, keep, give = call(
        attention_kernel,
        [(width, rows), (mine, width), (mine, width)],
        [
            head, s_a, dp_a, v_a, feat_b, q_pairs, q_wide, d_t, d_pairs, d_wide, *weights,
        ],
        smem=(0,),
        scratch=[
            pltpu.VMEM(sizes[0], F32), pltpu.VMEM(sizes[1], F32), pltpu.VMEM(sizes[2][:2], BF),
        ],
        flops=2 * 10**9,
    )
    recv = lax.ppermute(give, "aux", swap)
    sums = call(functools.partial(add_kernel, own), [(own, width)] * n_dom, [keep, recv])
    sums = [sums[0]] + [
        across(sums[s], s if doubling else n_dom - s) for s in range(1, n_dom)
    ]
    (output_t,) = call(output_kernel, [(width, rows)], [mixed, att, w_attn_out])
    (anchor_grad,) = call(sum_kernel, [(own, width)], sums)
    return output_t.T, anchor_grad


def solution(mesh):
    placed = (
        P(("groups", "dom", "aux"), None),
        P(("groups", "dom", "aux")),
        P(None, ("groups", "dom", "aux")),
        P(("groups", "dom", "aux")),
        P(None, ("groups", "dom", "aux")),
        P(("groups", "dom", "head", "aux")),
        P(None, "head"),
        P("head", None),
        P(),
        P(),
        P(),
        P(),
        P(("groups", "dom", "aux"), None),
    )
    return jax.shard_map(
        shards,
        mesh=mesh,
        in_specs=placed,
        out_specs=(P(("groups", "dom", "aux"), None), P(("groups", "dom", "head", "aux"), None)),
        check_vma=False,
    )
```

time: 141 us -> 40.7 us (0.29)
  waiting for transfers between devices: 54.5 us -> 10.3 us
  blocking collectives: 29.7 us -> 0 us
  other arithmetic: 16.9 us -> 0 us
  matrix products: 14.3 us -> 0 us
  between operations: 15.1 us -> 1.47 us
  starting transfers between devices: 5.25 us -> 18.2 us
  Pallas kernels: 0 us -> 10.6 us
  local copies, waits for them, and re-layouts: 4.74 us -> 0.05 us
    all_gather x4 -> x0, blocking collectives: 29.7 us -> none  [the longest x3 15 us: joined(): gathered = jax.tree.map(lambda a: lax.all_gather(a, axis), part)]
    unnamed x3 -> x0, waiting for transfers between devices: 29.6 us -> none
    psum x1 -> x0, waiting for transfers between devices: 23.7 us -> none  [shards(): mixed = features + lax.psum(matmul(hidden, w_out), 'head')]
    scatter-add x1 -> x0, other arithmetic: 15 us -> none  [shards(): gathered = jax.ops.segment_sum(messages, faces[0], num_segments=cell_rows)]
    dot_general x24 -> x0, matrix products: 14.3 us -> none  [matmul(): jnp.dot(left, right, precision=HIGH, preferred_element_type=jnp.float32)]
    ppermute x2 -> x13, starting transfers between devices: 5.17 us -> 18.2 us  [the longest x6 8.9 us: across(): return lax.ppermute(value, 'dom', [(i, i ^ step) for i in range(n_dom)])]
    pallas_call x0 -> x12, Pallas kernels: none -> 10.6 us  [call(): pl.pallas_call(body, out_shape=[jax.ShapeDtypeStruct(o[:2], o[2] if len(o...]
    ppermute x2 -> x13, waiting for transfers between devices: 1.08 us -> 10.3 us  [the longest x6 6.34 us: across(): return lax.ppermute(value, 'dom', [(i, i ^ step) for i in range(n_dom)])]
  transfers between devices with their start and end apart: 4 -> 13, of which waited for: 4 -> 7; matrix products, arithmetic and copies ran while one was open for 2% -> 0% of each run, Pallas kernels for 0% -> 12%
where the time goes in v2:
time: 40.7 us; the launch traced here: 40.5 us
  starting transfers between devices  18.2 us (45%)
  Pallas kernels  10.6 us (26%)
  waiting for transfers between devices  10.3 us (25%)
  between operations  1.47 us (4%)
    pallas_call x12, Pallas kernels, call(): pl.pallas_call(body, out_shape=[jax.ShapeDtypeStruct(o[:2], o[2] if len(o...  10.6 us
    ppermute x6, starting transfers between devices, across(): return lax.ppermute(value, 'dom', [(i, i ^ step) for i in range(n_dom)])  8.9 us
    ppermute x6, waiting for transfers between devices, across(): return lax.ppermute(value, 'dom', [(i, i ^ step) for i in range(n_dom)])  6.34 us
    ppermute x2, starting transfers between devices, along(): lax.ppermute(value, 'dom', [(i, (i + step) % n_dom) for i in range(n_dom)])  3.82 us
    ppermute x1, starting transfers between devices, shards(): other_index = lax.ppermute(index, 'head', swap)  3 us
    ppermute x2, starting transfers between devices, head_sum(): return (part, lax.ppermute(part, 'head', swap))  2.16 us
    ppermute x2, waiting for transfers between devices, head_sum(): return (part, lax.ppermute(part, 'head', swap))  1.98 us
    ppermute x1, waiting for transfers between devices, shards(): recv = lax.ppermute(give, 'aux', swap)  1.21 us
  transfers between devices with their start and end apart: 13, of which 7 were waited for; matrix products, arithmetic and copies ran while one was open for 0% of the time, Pallas kernels for 12%

profile of v2, /device:TPU:0, one launch (start us, length us, event | category | flops | bytes accessed | tf_op | source)
XLA Modules:
  0.0 40.5 jit_solution(15983855688509255457)
XLA Ops:
  0.6 1.4 %shard_map.140 = (f32[32,192]{1,0:T(8,128)S(1)}, f32[32,192]{1,0:T(8,128)S(1)}, s32[1,32]{1,0:T(1,128)S(1)}, s32[3,1536]{1,0:T(4,128)S(1)}, f32[192,256]{1,0:T(8,128)S(1)}, /*index=5*/f32[384,384]{1,0:T(8,128)S(1)}) custom-call(s32[2,32]{1,0:T(2,128)} %send_hbm.1, s32[1,32]{1,0:T(1,128)} %bitcast.13, s32[3,1536]{1,0:T(4,128)} %faces_hbm.1, ...), custom_call_target="tpu_custom_call" | custom-call | flops 100000000 | bytes 1000000 | tf_op jit(solution)/shard_map/pallas_call | solution.py:52
  2.1 3.0 %collective-permute-start = (s32[1,32]{1,0:T(1,128)S(1)}, s32[1,32]{1,0:T(1,128)S(1)}, u32[]{:S(2)}, u32[]{:S(2)}) collective-permute-start(s32[1,32]{1,0:T(1,128)S(1)} %get-tuple-element.40.own_ref), channel_id=1, source_target_pairs={{0,2},{2,0},{1,3},{3,1},{4,6},{6,4},{5,7},{7,5},{8,10},{10,8},{9,1... | collective-permute-start | bytes 392 | tf_op jit(solution)/shard_map/ppermute | solution.py:428
  5.1 1.6 %collective-permute-start.1 = (f32[32,192]{1,0:T(8,128)S(1)}, f32[32,192]{1,0:T(8,128)S(1)}, u32[]{:S(2)}, u32[]{:S(2)}) collective-permute-start(f32[32,192]{1,0:T(8,128)S(1)} %get-tuple-element.41), channel_id=1, source_target_pairs={{0,4},{4,8},{8,12},{12,0},{1,5},{5,9},{9,13},{13,1},{2,6},{6,10},{... | collective-permute-start | bytes 73736 | tf_op jit(solution)/shard_map/ppermute | solution.py:402
  6.7 2.2 %collective-permute-start.2 = (f32[32,192]{1,0:T(8,128)S(1)}, f32[32,192]{1,0:T(8,128)S(1)}, u32[]{:S(2)}, u32[]{:S(2)}) collective-permute-start(f32[32,192]{1,0:T(8,128)S(1)} %get-tuple-element.42), channel_id=1, source_target_pairs={{0,12},{4,0},{8,4},{12,8},{1,13},{5,1},{9,5},{13,9},{2,14},{6,2},{... | collective-permute-start | bytes 73736 | tf_op jit(solution)/shard_map/ppermute | solution.py:402
  9.6 1.6 %shard_map.141 = (f32[384,256]{1,0:T(8,128)S(1)}, f32[64,256]{1,0:T(8,128)S(1)}, bf16[384,192]{1,0:T(8,128)(2,1)S(1)}, bf16[384,192]{1,0:T(8,128)(2,1)S(1)}) custom-call(s32[1,1]{1,0:T(1,128)} %bitcast.7.live_ref, f32[192,256]{1,0:T(8,128)S(1)} %get-tuple-element.39.x_t_ref, s32[3,1536]{1,0:T(4,128)S(1)} %get-tuple-element.43.faces_ref, ...), custom_call_target="tpu_custom_call" | custom-call | flops 2000000000 | bytes 1000000 | tf_op jit(solution)/shard_map/pallas_call | solution.py:52
  11.3 1.2 %shard_map.142 = (bf16[384,256]{1,0:T(8,128)(2,1)S(1)}, bf16[384,256]{1,0:T(8,128)(2,1)S(1)}, f32[64,192]{1,0:T(8,128)S(1)}) custom-call(s32[1]{0:T(128)} %bitcast.2.head_ref, s32[1,32]{1,0:T(1,128)S(1)} %get-tuple-element.40.own_ref, s32[1,32]{1,0:T(1,128)S(1)} %collective-permute-done.other_ref, f32[32,192]{1,0:T(8,128)S(1)} %collective-permute-done.1.lower_ref, ...), custom_call_target="tpu_custom_call" | custom-call | flops 1000000000 | bytes 1000000 | tf_op jit(solution)/shard_map/pallas_call | solution.py:52
  12.9 0.8 %shard_map.143 = (f32[192,256]{1,0:T(8,128)S(1)}, f32[64,192]{1,0:T(8,128)S(1)}, f32[192,256]{1,0:T(8,128)S(1)}, bf16[768,256]{1,0:T(8,128)(2,1)S(1)}, bf16[256,...) custom-call(s32[1]{0:T(128)} %bitcast.2.head_ref, ...), custom_call_target="tpu_custom_call" | custom-call | flops 1000000000 | bytes 1000000 | tf_op jit(solution)/shard_map/pallas_call | solution.py:52
  13.8 1.8 %collective-permute-start.3 = (f32[192,256]{1,0:T(8,128)S(1)}, f32[192,256]{1,0:T(8,128)S(1)}, u32[]{:S(2)}, u32[]{:S(2)}) collective-permute-start(f32[192,256]{1,0:T(8,128)S(1)} %get-tuple-element.51.part_ref), channel_id=1, source_target_pairs={{0,2},{2,0},{1,3},{3,1},{4,6},{6,4},{5,7},{7,5},{8,10},{10,8},{9,1... | collective-permute-start | bytes 589832 | tf_op jit(solution)/shard_map/ppermute | solution.py:411
  15.6 2.0 %collective-permute-done.4.recv_ref = f32[64,192]{1,0:T(8,128)S(1)} collective-permute-done((f32[64,192]{1,0:T(8,128)S(1)}, f32[64,192]{1,0:T(8,128)S(1)}, u32[]{:S(2)}, u32[]{:S(2)}) %collective-permute-start.4) | collective-permute-done | bytes 49184 | tf_op jit(solution)/shard_map/ppermute | solution.py:411
  17.7 3.3 %collective-permute-start.7 = (f32[64,192]{1,0:T(8,128)S(1)}, f32[64,192]{1,0:T(8,128)S(1)}, u32[]{:S(2)}, u32[]{:S(2)}) collective-permute-start(f32[64,192]{1,0:T(8,128)S(1)} %shard_map.145.refs_0_), channel_id=1, source_target_pairs={{0,12},{4,8},{8,4},{12,0},{1,13},{5,9},{9,5},{13,1},{2,14},{6,10},... | collective-permute-start | bytes 147464 | tf_op jit(solution)/shard_map/ppermute | solution.py:406
  21.0 1.2 %collective-permute-start.5 = (f32[64,192]{1,0:T(8,128)S(1)}, f32[64,192]{1,0:T(8,128)S(1)}, u32[]{:S(2)}, u32[]{:S(2)}) collective-permute-start(f32[64,192]{1,0:T(8,128)S(1)} %shard_map.145.refs_0_), channel_id=1, source_target_pairs={{0,4},{4,0},{8,12},{12,8},{1,5},{5,1},{9,13},{13,9},{2,6},{6,2},{1... | collective-permute-start | bytes 147464 | tf_op jit(solution)/shard_map/ppermute | solution.py:406
  22.2 0.6 %shard_map.144 = (f32[192,256]{1,0:T(8,128)S(1)}, bf16[768,256]{1,0:T(8,128)(2,1)S(1)}, bf16[256,384]{1,0:T(8,128)(2,1)S(1)}) custom-call(f32[192,256]{1,0:T(8,128)S(1)} %get-tuple-element.39.x_t_ref, f32[192,256]{1,0:T(8,128)S(1)} %get-tuple-element.51.part_ref, f32[192,256]{1,0:T(8,128)S(1)} %collective-permute-done.3.recv_ref, f32[192,192]{1,0:T(8,128)S(1)} %copy-done.5), custom_call_target="tpu_custom_call" | custom-call | flops 1000000000 | bytes 1000000 | tf_op jit(solution)/shard_map/pallas_call | solution.py:52
  22.8 1.1 %collective-permute-done.7.refs_3_ = f32[64,192]{1,0:T(8,128)S(1)} collective-permute-done((f32[64,192]{1,0:T(8,128)S(1)}, f32[64,192]{1,0:T(8,128)S(1)}, u32[]{:S(2)}, u32[]{:S(2)}) %collective-permute-start.7) | collective-permute-done | bytes 49184 | tf_op jit(solution)/shard_map/ppermute | solution.py:406
  23.9 2.3 %collective-permute-done.6.refs_2_ = f32[64,192]{1,0:T(8,128)S(1)} collective-permute-done((f32[64,192]{1,0:T(8,128)S(1)}, f32[64,192]{1,0:T(8,128)S(1)}, u32[]{:S(2)}, u32[]{:S(2)}) %collective-permute-start.6) | collective-permute-done | bytes 49184 | tf_op jit(solution)/shard_map/ppermute | solution.py:406
  26.3 0.8 %shard_map.147 = (f32[256,768]{1,0:T(8,128)S(1)}, f32[128,768]{1,0:T(8,128)S(1)}, bf16[256,384]{1,0:T(8,128)(2,1)S(1)}) custom-call(s32[1]{0:T(128)} %bitcast.2.head_ref, f32[256,192]{1,0:T(8,128)S(1)} %shard_map.146.feat_ref, bf16[768,256]{1,0:T(8,128)(2,1)S(1)} %get-tuple-element.55.q_pairs_ref, bf16[768,256]{1,0:T(8,128)(2,1)S(1)} %get-tuple-element.56.d_pairs_ref, ...), custom_call_target="tpu_custom_call" | custom-call | flops 1000000000 | bytes 1000000 | tf_op jit(solution)/shard_map/pallas_call | solution.py:52
  27.0 0.7 %collective-permute-done.8.feat_ref = f32[256,192]{1,0:T(8,128)S(1)} collective-permute-done((f32[256,192]{1,0:T(8,128)S(1)}, f32[256,192]{1,0:T(8,128)S(1)}, u32[]{:S(2)}, u32[]{:S(2)}) %collective-permute-start.8) | collective-permute-done | bytes 196640 | tf_op jit(solution)/shard_map/ppermute | solution.py:477
  27.8 2.3 %shard_map.148 = (f32[192,256]{1,0:T(8,128)S(1)}, f32[128,192]{1,0:T(8,128)S(1)}, f32[128,192]{1,0:T(8,128)S(1)}) custom-call(s32[1]{0:T(128)} %bitcast.2.head_ref, f32[256,768]{1,0:T(8,128)S(1)} %get-tuple-element.61.s_a_ref, f32[128,768]{1,0:T(8,128)S(1)} %get-tuple-element.62.dp_a_ref, bf16[256,384]{1,0:T(8,128)(2,1)S(1)} %get-tuple-element.63.v_a_ref, ...), custom_call_target="tpu_custom_call" | custom-call | flops 2000000000 | bytes 1000000 | tf_op jit(solution)/shard_map/pallas_call | solution.py:52
  30.3 1.2 %collective-permute-done.9.recv_ref = f32[128,192]{1,0:T(8,128)S(1)} collective-permute-done((f32[128,192]{1,0:T(8,128)S(1)}, f32[128,192]{1,0:T(8,128)S(1)}, u32[]{:S(2)}, u32[]{:S(2)}) %collective-permute-start.9) | collective-permute-done | bytes 98336 | tf_op jit(solution)/shard_map/ppermute | solution.py:498
  31.5 0.6 %collective-permute-start.10 = (f32[32,192]{1,0:T(8,128)S(1)}, f32[32,192]{1,0:T(8,128)S(1)}, u32[]{:S(2)}, u32[]{:S(2)}) collective-permute-start(f32[32,192]{1,0:T(8,128)S(1)} %get-tuple-element.73), channel_id=1, source_target_pairs={{0,4},{4,0},{8,12},{12,8},{1,5},{5,1},{9,13},{13,9},{2,6},{6,2},{1... | collective-permute-start | bytes 73736 | tf_op jit(solution)/shard_map/ppermute | solution.py:406
  32.1 2.0 %collective-permute-start.11 = (f32[32,192]{1,0:T(8,128)S(1)}, f32[32,192]{1,0:T(8,128)S(1)}, u32[]{:S(2)}, u32[]{:S(2)}) collective-permute-start(f32[32,192]{1,0:T(8,128)S(1)} %get-tuple-element.74), channel_id=1, source_target_pairs={{0,8},{4,12},{8,0},{12,4},{1,9},{5,13},{9,1},{13,5},{2,10},{6,14},... | collective-permute-start | bytes 73736 | tf_op jit(solution)/shard_map/ppermute | solution.py:406
  34.2 1.8 %collective-permute-start.12 = (f32[32,192]{1,0:T(8,128)S(1)}, f32[32,192]{1,0:T(8,128)S(1)}, u32[]{:S(2)}, u32[]{:S(2)}) collective-permute-start(f32[32,192]{1,0:T(8,128)S(1)} %get-tuple-element.75), channel_id=1, source_target_pairs={{0,12},{4,8},{8,4},{12,0},{1,13},{5,9},{9,5},{13,1},{2,14},{6,10},... | collective-permute-start | bytes 73736 | tf_op jit(solution)/shard_map/ppermute | solution.py:406
  36.0 1.0 %shard_map.149 = f32[192,256]{1,0:T(8,128)} custom-call(f32[192,256]{1,0:T(8,128)S(1)} %get-tuple-element.52._.mixed_t_ref, f32[192,256]{1,0:T(8,128)S(1)} %get-tuple-element.69.att_t_ref, f32[192,192]{1,0:T(8,128)S(1)} %copy-done), custom_call_target="tpu_custom_call" | custom-call | flops 100000000 | bytes 1000000 | tf_op jit(solution)/shard_map/pallas_call | solution.py:52
  37.1 2.8 %collective-permute-done.12.refs_3_ = f32[32,192]{1,0:T(8,128)S(1)} collective-permute-done((f32[32,192]{1,0:T(8,128)S(1)}, f32[32,192]{1,0:T(8,128)S(1)}, u32[]{:S(2)}, u32[]{:S(2)}) %collective-permute-start.12) | collective-permute-done | bytes 24608 | tf_op jit(solution)/shard_map/ppermute | solution.py:406
  39.9 0.6 %shard_map.151 = f32[32,192]{1,0:T(8,128)} custom-call(f32[32,192]{1,0:T(8,128)S(1)} %get-tuple-element.72.refs_0_, f32[32,192]{1,0:T(8,128)S(1)} %collective-permute-done.10.refs_1_, f32[32,192]{1,0:T(8,128)S(1)} %collective-permute-done.11.refs_2_, f32[32,192]{1,0:T(8,128)S(1)} %collective-permute-done.12.refs_3_), custom_call_target="tpu_custom_call" | custom-call | flops 100000000 | bytes 1000000 | tf_op jit(solution)/shard_map/pallas_call | solution.py:52
  (29 shorter events, 1.1 us)
Async XLA Ops:
  0.6 9.0 %copy-start.6 = (f32[1536]{0:T(1024)S(1)}, f32[1536]{0:T(1024)}, u32[]{:S(2)}) copy-start(f32[1536]{0:T(1024)} %param.14) | copy-start | bytes 18436
  2.1 9.1 %collective-permute-start = (s32[1,32]{1,0:T(1,128)S(1)}, s32[1,32]{1,0:T(1,128)S(1)}, u32[]{:S(2)}, u32[]{:S(2)}) collective-permute-start(s32[1,32]{1,0:T(1,128)S(1)} %get-tuple-element.40.own_ref), channel_id=1, source_target_pairs={{0,2},{2,0},{1,3},{3,1},{4,6},{6,4},{5,7},{7,5},{8,10},{10,8},{9,1... | collective-permute-start | bytes 392 | tf_op jit(solution)/shard_map/ppermute | solution.py:428
  5.1 6.1 %collective-permute-start.1 = (f32[32,192]{1,0:T(8,128)S(1)}, f32[32,192]{1,0:T(8,128)S(1)}, u32[]{:S(2)}, u32[]{:S(2)}) collective-permute-start(f32[32,192]{1,0:T(8,128)S(1)} %get-tuple-element.41), channel_id=1, source_target_pairs={{0,4},{4,8},{8,12},{12,0},{1,5},{5,9},{9,13},{13,1},{2,6},{6,10},{... | collective-permute-start | bytes 73736 | tf_op jit(solution)/shard_map/ppermute | solution.py:402
  6.7 4.6 %collective-permute-start.2 = (f32[32,192]{1,0:T(8,128)S(1)}, f32[32,192]{1,0:T(8,128)S(1)}, u32[]{:S(2)}, u32[]{:S(2)}) collective-permute-start(f32[32,192]{1,0:T(8,128)S(1)} %get-tuple-element.42), channel_id=1, source_target_pairs={{0,12},{4,0},{8,4},{12,8},{1,13},{5,1},{9,5},{13,9},{2,14},{6,2},{... | collective-permute-start | bytes 73736 | tf_op jit(solution)/shard_map/ppermute | solution.py:402
  9.6 1.6 %copy-start.1 = (f32[384,192]{0,1:T(8,128)S(1)}, f32[384,192]{0,1:T(8,128)}, u32[]{:S(2)}) copy-start(f32[384,192]{0,1:T(8,128)} %param.20) | copy-start | bytes 884740
  11.3 1.7 %copy-start = (f32[192,192]{1,0:T(8,128)S(1)}, f32[192,192]{1,0:T(8,128)}, u32[]{:S(2)}) copy-start(f32[192,192]{1,0:T(8,128)} %w_ref.5) | copy-start | bytes 442372
  11.3 1.7 %copy-start.2 = (f32[256,192]{0,1:T(8,128)S(1)}, f32[256,192]{0,1:T(8,128)}, u32[]{:S(2)}) copy-start(f32[256,192]{0,1:T(8,128)} %param.25) | copy-start | bytes 589828
  11.3 1.6 %copy-start.3 = (f32[192,192]{1,0:T(8,128)S(1)}, f32[192,192]{1,0:T(8,128)}, u32[]{:S(2)}) copy-start(f32[192,192]{1,0:T(8,128)} %wk_ref.1) | copy-start | bytes 442372
  11.3 1.6 %copy-start.4 = (f32[192,192]{1,0:T(8,128)S(1)}, f32[192,192]{1,0:T(8,128)}, u32[]{:S(2)}) copy-start(f32[192,192]{1,0:T(8,128)} %wv_ref.1) | copy-start | bytes 442372
  12.5 5.0 %collective-permute-start.4 = (f32[64,192]{1,0:T(8,128)S(1)}, f32[64,192]{1,0:T(8,128)S(1)}, u32[]{:S(2)}, u32[]{:S(2)}) collective-permute-start(f32[64,192]{1,0:T(8,128)S(1)} %get-tuple-element.54.part_ref), channel_id=1, source_target_pairs={{0,2},{2,0},{1,3},{3,1},{4,6},{6,4},{5,7},{7,5},{8,10},{10,8},{9,1... | collective-permute-start | bytes 147464 | tf_op jit(solution)/shard_map/ppermute | solution.py:411
  13.8 8.4 %collective-permute-start.3 = (f32[192,256]{1,0:T(8,128)S(1)}, f32[192,256]{1,0:T(8,128)S(1)}, u32[]{:S(2)}, u32[]{:S(2)}) collective-permute-start(f32[192,256]{1,0:T(8,128)S(1)} %get-tuple-element.51.part_ref), channel_id=1, source_target_pairs={{0,2},{2,0},{1,3},{3,1},{4,6},{6,4},{5,7},{7,5},{8,10},{10,8},{9,1... | collective-permute-start | bytes 589832 | tf_op jit(solution)/shard_map/ppermute | solution.py:411
  17.5 4.6 %copy-start.5 = (f32[192,192]{1,0:T(8,128)S(1)}, f32[192,192]{1,0:T(8,128)}, u32[]{:S(2)}) copy-start(f32[192,192]{1,0:T(8,128)} %w_ref.4) | copy-start | bytes 442372
  17.7 6.1 %collective-permute-start.7 = (f32[64,192]{1,0:T(8,128)S(1)}, f32[64,192]{1,0:T(8,128)S(1)}, u32[]{:S(2)}, u32[]{:S(2)}) collective-permute-start(f32[64,192]{1,0:T(8,128)S(1)} %shard_map.145.refs_0_), channel_id=1, source_target_pairs={{0,12},{4,8},{8,4},{12,0},{1,13},{5,9},{9,5},{13,1},{2,14},{6,10},... | collective-permute-start | bytes 147464 | tf_op jit(solution)/shard_map/ppermute | solution.py:406
  21.0 5.2 %collective-permute-start.6 = (f32[64,192]{1,0:T(8,128)S(1)}, f32[64,192]{1,0:T(8,128)S(1)}, u32[]{:S(2)}, u32[]{:S(2)}) collective-permute-start(f32[64,192]{1,0:T(8,128)S(1)} %shard_map.145.refs_0_), channel_id=1, source_target_pairs={{0,8},{4,12},{8,0},{12,4},{1,9},{5,13},{9,1},{13,5},{2,10},{6,14},... | collective-permute-start | bytes 147464 | tf_op jit(solution)/shard_map/ppermute | solution.py:406
  21.0 5.2 %collective-permute-start.5 = (f32[64,192]{1,0:T(8,128)S(1)}, f32[64,192]{1,0:T(8,128)S(1)}, u32[]{:S(2)}, u32[]{:S(2)}) collective-permute-start(f32[64,192]{1,0:T(8,128)S(1)} %shard_map.145.refs_0_), channel_id=1, source_target_pairs={{0,4},{4,0},{8,12},{12,8},{1,5},{5,1},{9,13},{13,9},{2,6},{6,2},{1... | collective-permute-start | bytes 147464 | tf_op jit(solution)/shard_map/ppermute | solution.py:406
  26.2 1.6 %collective-permute-start.8 = (f32[256,192]{1,0:T(8,128)S(1)}, f32[256,192]{1,0:T(8,128)S(1)}, u32[]{:S(2)}, u32[]{:S(2)}) collective-permute-start(f32[256,192]{1,0:T(8,128)S(1)} %shard_map.146.feat_ref), channel_id=1, source_target_pairs={{0,1},{1,0},{2,3},{3,2},{4,5},{5,4},{6,7},{7,6},{8,9},{9,8},{10,11... | collective-permute-start | bytes 589832 | tf_op jit(solution)/shard_map/ppermute | solution.py:477
  30.1 1.4 %collective-permute-start.9 = (f32[128,192]{1,0:T(8,128)S(1)}, f32[128,192]{1,0:T(8,128)S(1)}, u32[]{:S(2)}, u32[]{:S(2)}) collective-permute-start(f32[128,192]{1,0:T(8,128)S(1)} %get-tuple-element.71), channel_id=1, source_target_pairs={{0,1},{1,0},{2,3},{3,2},{4,5},{5,4},{6,7},{7,6},{8,9},{9,8},{10,11... | collective-permute-start | bytes 294920 | tf_op jit(solution)/shard_map/ppermute | solution.py:498
  31.5 5.4 %collective-permute-start.10 = (f32[32,192]{1,0:T(8,128)S(1)}, f32[32,192]{1,0:T(8,128)S(1)}, u32[]{:S(2)}, u32[]{:S(2)}) collective-permute-start(f32[32,192]{1,0:T(8,128)S(1)} %get-tuple-element.73), channel_id=1, source_target_pairs={{0,4},{4,0},{8,12},{12,8},{1,5},{5,1},{9,13},{13,9},{2,6},{6,2},{1... | collective-permute-start | bytes 73736 | tf_op jit(solution)/shard_map/ppermute | solution.py:406
  32.1 5.0 %collective-permute-start.11 = (f32[32,192]{1,0:T(8,128)S(1)}, f32[32,192]{1,0:T(8,128)S(1)}, u32[]{:S(2)}, u32[]{:S(2)}) collective-permute-start(f32[32,192]{1,0:T(8,128)S(1)} %get-tuple-element.74), channel_id=1, source_target_pairs={{0,8},{4,12},{8,0},{12,4},{1,9},{5,13},{9,1},{13,5},{2,10},{6,14},... | collective-permute-start | bytes 73736 | tf_op jit(solution)/shard_map/ppermute | solution.py:406
  34.2 5.7 %collective-permute-start.12 = (f32[32,192]{1,0:T(8,128)S(1)}, f32[32,192]{1,0:T(8,128)S(1)}, u32[]{:S(2)}, u32[]{:S(2)}) collective-permute-start(f32[32,192]{1,0:T(8,128)S(1)} %get-tuple-element.75), channel_id=1, source_target_pairs={{0,12},{4,8},{8,4},{12,0},{1,13},{5,9},{9,5},{13,1},{2,14},{6,10},... | collective-permute-start | bytes 73736 | tf_op jit(solution)/shard_map/ppermute | solution.py:406

commit v3 on v2

v3 whole, which is shorter than its diff:
```python
import functools
import math

import jax
import jax.numpy as jnp
from jax import lax
from jax.experimental import pallas as pl
from jax.experimental.pallas import tpu as pltpu
from jax.sharding import PartitionSpec as P

HEADS = 3
DH = 64
NN = (((1,), (0,)), ((), ()))
NT = (((1,), (1,)), ((), ()))
TN = (((0,), (0,)), ((), ()))
BF = jnp.bfloat16
F32 = jnp.float32
I32 = jnp.int32
LOG2E = math.log2(math.e)


def dot_bf(left, right, dims=NN):
    return lax.dot_general(left, right, dims, preferred_element_type=F32)


def split(value):
    top = value.astype(BF)
    return top, (value - top.astype(F32)).astype(BF)


def dot_halves(left, right, dims=NN):
    rows = left[0].shape[0]
    both = dot_bf(jnp.concatenate(left, axis=0), right[0], dims)
    return both[:rows] + (both[rows:] + dot_bf(left[0], right[1], dims))


def dot(left, right, dims=NN):
    return dot_halves(split(left), split(right), dims)


def dense(value):
    rows, width = value.shape
    tail = width % 128
    if tail != 64:
        return value
    tails = jnp.concatenate([value[: rows // 2, -64:], value[rows // 2 :, -64:]], axis=1)
    return jnp.concatenate([value[:, :-64], tails], axis=0)


def undense(value, width):
    if value.shape[1] == width:
        return value
    rows = value.shape[0] * 2 // 3
    tails = jnp.concatenate([value[rows:, :64], value[rows:, 64:]], axis=0)
    return jnp.concatenate([value[:rows], tails], axis=1)


def dense_shape(rows, width):
    return (rows * 3 // 2, 128) if width == 192 else (rows, width)


def layer_norm(value, axis=-1):
    mean = jnp.mean(value, axis=axis, keepdims=True)
    centred = value - mean
    spread = jnp.mean(centred * centred, axis=axis, keepdims=True)
    return centred * lax.rsqrt(spread + 1e-05)


def call(body, outs, ins, smem=(), hbm=(), scratch=(), flops=10**8):
    def space(i):
        return pltpu.SMEM if i in smem else pltpu.HBM if i in hbm else pltpu.VMEM

    return pl.pallas_call(
        body,
        out_shape=[jax.ShapeDtypeStruct(o[:2], o[2] if len(o) > 2 else F32) for o in outs],
        in_specs=[pl.BlockSpec(memory_space=space(i)) for i in range(len(ins))],
        out_specs=[pl.BlockSpec(memory_space=pltpu.VMEM)] * len(outs),
        scratch_shapes=list(scratch),
        compiler_params=pltpu.CompilerParams(vmem_limit_bytes=48 * 2**20),
        cost_estimate=pl.CostEstimate(flops=flops, bytes_accessed=10**6, transcendentals=0),
    )(*[
        pltpu.with_memory_space_constraint(x, pltpu.HBM) if i in hbm else x
        for i, x in enumerate(ins)
    ])


def chosen(index, rows):
    places = lax.broadcasted_iota(I32, (rows, index.shape[1]), 0)
    return jnp.where(places == index, 1.0, 0.0).astype(BF)


def exact_parts(value):
    top, mid = split(value)
    return top, mid, (value - top.astype(F32) - mid.astype(F32)).astype(BF)


def outgoing_kernel(
    send_hbm, index_hbm, faces_hbm, x_t_hbm, w_in_hbm,
    lower_ref, upper_ref, index_ref, faces_ref, x_t_ref, w_in_ref, send_ref, sems,
):
    copies = [
        pltpu.make_async_copy(source, target, sems.at[i])
        for i, (source, target) in enumerate(
            [
                (send_hbm, send_ref), (x_t_hbm, x_t_ref), (index_hbm, index_ref),
                (faces_hbm, faces_ref), (w_in_hbm, w_in_ref),
            ]
        )
    ]
    for copy in copies:
        copy.start()
    copies[0].wait()
    halos = send_ref.shape[1]
    index = jnp.concatenate([send_ref[0:1, :], send_ref[1:2, :]], axis=1)
    pick = chosen(index, x_t_ref.shape[1])
    copies[1].wait()
    top, mid, low = exact_parts(x_t_ref[...])
    sent = layer_norm((dot_bf(top, pick) + dot_bf(mid, pick) + dot_bf(low, pick)).T)
    lower_ref[...] = dense(sent[:halos])
    upper_ref[...] = dense(sent[halos:])
    for copy in copies[2:]:
        copy.wait()


def small_chosen(index, rows, value):
    places = lax.broadcasted_iota(I32, (rows, index.shape[1]), 0).astype(F32).astype(BF)
    return jnp.where(places == index, value, jnp.zeros_like(value))


def own_faces_kernel(
    live_ref, x_t_ref, faces_ref, weight_ref, w_in_ref,
    pre_t_ref, halo_mat_ref, w_top_ref, w_low_ref,
):
    width, rows = x_t_ref.shape
    units = pre_t_ref.shape[0]
    halos = halo_mat_ref.shape[0] // 2
    slots = faces_ref.shape[1]
    w_top, w_low = split(
        jnp.concatenate([w_in_ref[:width].T, w_in_ref[width:].T], axis=0)
    )
    w_top_ref[...] = w_top[units:]
    w_low_ref[...] = w_low[units:]
    normed_t = split(layer_norm(x_t_ref[...], axis=0))
    straight = dot_halves((w_top, w_low), normed_t)
    kind = faces_ref[1:2, :]
    receiver = faces_ref[0:1, :].astype(F32).astype(BF)
    source = faces_ref[2:3, :].astype(F32)
    cells = jnp.where(kind == 0, source, -1.0).astype(BF)
    halo_rows = jnp.where(kind == 0, -1.0, jnp.where(kind == 1, source, source + halos))
    halo_rows = halo_rows.astype(BF)
    live = lax.broadcasted_iota(I32, (1, slots), 1) < live_ref[...]
    top, low = split(jnp.where(live, weight_ref[...], 0.0))
    out_of = jnp.concatenate(
        [
            small_chosen(cells, rows, top), small_chosen(halo_rows, 2 * halos, top),
            small_chosen(cells, rows, low), small_chosen(halo_rows, 2 * halos, low),
        ],
        axis=0,
    )
    both = dot_bf(out_of, small_chosen(receiver, rows, jnp.ones_like(receiver)), NT)
    sources = rows + 2 * halos
    matrix_t = both[:sources] + both[sources:]
    halo_mat_ref[...] = matrix_t[rows:]
    pre_t_ref[...] = straight[:units] + dot(straight[units:], matrix_t[:rows])


def every_index(head_ref, own_ref, other_ref):
    own = own_ref.shape[1]
    if other_ref.shape[1] > own:
        return other_ref[...]
    first = head_ref[0] == 0
    return jnp.concatenate(
        [
            jnp.where(first, own_ref[...], other_ref[...]),
            jnp.where(first, other_ref[...], own_ref[...]),
        ],
        axis=1,
    )


def take(value, pick):
    rows = value.shape[0]
    taken = dot_bf(jnp.concatenate(exact_parts(value), axis=0), pick)
    return taken[:rows] + (taken[rows : 2 * rows] + taken[2 * rows :])


def pick_kernel(
    head_ref, own_ref, other_ref, pre_t_ref, halo_mat_ref, x_t_ref,
    pre_pick_ref, halo_pick_ref, anchor_x_ref,
):
    pick = chosen(every_index(head_ref, own_ref, other_ref), pre_t_ref.shape[1])
    pre_pick_ref[...] = take(pre_t_ref[...], pick)
    halo_pick_ref[...] = take(halo_mat_ref[...], pick)
    anchor_x_ref[...] = take(x_t_ref[...], pick).T


def hidden_part(halo_t, halo_mat, pre_t, w_in_halves, w_out_t):
    halo_agg = dot_halves(halo_t, split(halo_mat))
    pre = pre_t + dot_halves(w_in_halves, split(halo_agg))
    hidden = 0.5 * pre * (1.0 + lax.erf(pre * math.sqrt(0.5)))
    return dot(w_out_t, hidden)


def anchor_part_kernel(
    lower_ref, upper_ref, pre_pick_ref, halo_pick_ref, w_top_ref, w_low_ref, w_out_t_ref,
    part_ref, top_ref, low_ref,
):
    width = w_top_ref.shape[1]
    halo = jnp.concatenate(
        [undense(lower_ref[...], width), undense(upper_ref[...], width)], axis=0
    )
    halo_t = split(halo.T)
    part = hidden_part(
        halo_t, halo_pick_ref[...], pre_pick_ref[...], (w_top_ref[...], w_low_ref[...]),
        w_out_t_ref[...],
    )
    part_ref[...] = dense(part.T)
    top_ref[...], low_ref[...] = halo_t


def rest_kernel(
    top_ref, low_ref, halo_mat_ref, pre_t_ref, w_top_ref, w_low_ref, w_out_t_ref, part_t_ref
):
    part_t_ref[...] = hidden_part(
        (top_ref[...], low_ref[...]), halo_mat_ref[...], pre_t_ref[...],
        (w_top_ref[...], w_low_ref[...]), w_out_t_ref[...],
    )


def split_heads(value_t):
    out = []
    for h in range(HEADS):
        out += split(value_t[h * DH : (h + 1) * DH])
    return jnp.concatenate(out, axis=0)


def through(w, value_t, front_refs, back_refs, back_scale):
    width = w.shape[0]
    w, value_t = split(w), split(value_t)
    for h in range(HEADS):
        at = of_head(h, 1)
        front = dot_halves([half[:, at] for half in w], [half[at] for half in value_t])
        rows = front.shape[1]
        halves = split(front)
        backs = split(front.T * back_scale)
        for i in range(2):
            front_refs[i][h * width : (h + 1) * width, :] = halves[i]
            back_refs[i][h * rows : (h + 1) * rows, :] = backs[i]


def cotangent_kernel(
    g_t_ref, w_ref, wv_ref, _,
    d_t_ref, v_top_ref, v_low_ref, t_top_ref, t_low_ref, t_back_top_ref, t_back_low_ref,
):
    d_t = dot(w_ref[...], g_t_ref[...])
    d_t_ref[...] = d_t
    v_top_ref[...], v_low_ref[...] = split(wv_ref[...].T)
    through(
        wv_ref[...], d_t, (t_top_ref, t_low_ref), (t_back_top_ref, t_back_low_ref), 1.0
    )


def anchor_kernel(x_ref, part_ref, recv_ref, _, *outs):
    part = undense(part_ref[...] + recv_ref[...], x_ref.shape[1])
    feat = dense(layer_norm(x_ref[...] + part))
    for out in outs:
        out[...] = feat


def query_kernel(
    x_t_ref, part_ref, recv_ref, w_ref, wk_ref,
    mixed_t_ref, u_top_ref, u_low_ref, u_back_top_ref, u_back_low_ref,
):
    mixed_t = x_t_ref[...] + (part_ref[...] + recv_ref[...])
    mixed_t_ref[...] = mixed_t
    q_t = dot(w_ref[...].T, layer_norm(mixed_t, axis=0)) * (LOG2E / math.sqrt(DH))
    through(
        wk_ref[...], q_t, (u_top_ref, u_low_ref), (u_back_top_ref, u_back_low_ref), 1.0 / LOG2E
    )


def join_kernel(own, _, *refs):
    out = refs[-1]
    blocks = len(refs) - 1
    for i, ref in enumerate(refs[:-1]):
        value = undense(ref[...], out.shape[1])
        for place in range(value.shape[0] // own):
            out[pl.ds((place * blocks + i) * own, own), :] = value[place * own : (place + 1) * own]


CHUNK = 512


def over_chunks(count, step, carry):
    size = min(count, CHUNK)
    if count == size:
        return step(0, size, carry)
    return lax.fori_loop(
        0, count // size, lambda i, c: step(pl.multiple_of(i * size, size), size, c), carry
    )


def of_head(h, wide_by):
    return slice(wide_by * h * DH, wide_by * (h + 1) * DH)


def forward(head_ref, feat_ref, u, t, wv, s_ref, v_ref, s_mine_ref, dp_ref):
    width = feat_ref.shape[1]
    count = feat_ref.shape[0]
    rows = u[0].shape[1]
    mine = dp_ref.shape[0]
    cells = [slice(h * rows, (h + 1) * rows) for h in range(HEADS)]
    feats = [slice(h * width, (h + 1) * width) for h in range(HEADS)]

    def step(start, size, carry):
        at = pl.ds(start, size)
        feat = split(feat_ref[at, :])
        for h in range(HEADS):
            s_ref[at, cells[h]] = dot_halves(feat, [half[feats[h], :] for half in u])
        v_ref[:, at] = split_heads(dot_halves(wv, split(feat_ref[at, :].T)))
        return carry

    over_chunks(count, step, 0)
    tops, totals, sums = [], [], []
    for h in range(HEADS):

        def highest(start, size, top, h=h):
            part = jnp.max(s_ref[pl.ds(start, size), cells[h]], axis=0, keepdims=True)
            return part if top is None else jnp.maximum(top, part)

        least = None if count <= CHUNK else jnp.full((1, rows), -jnp.inf, F32)
        tops.append(over_chunks(count, highest, least))
    for h in range(HEADS):

        def weigh(start, size, state, h=h):
            total, acc = state
            at = pl.ds(start, size)
            expo = jnp.exp2(s_ref[at, cells[h]] - tops[h])
            top, low = split(expo)
            value = v_ref[of_head(h, 2), at]
            total = total + jnp.sum(expo, axis=0, keepdims=True)
            both = dot_bf(value, top)
            return total, acc + (both[:DH] + (both[DH:] + dot_bf(value[:DH], low)))

        start = (jnp.zeros((1, rows), F32), jnp.zeros((DH, rows), F32))
        total, acc = over_chunks(count, weigh, start)
        totals.append(total)
        sums.append(acc)
    place = pl.ds(pl.multiple_of(head_ref[0] * mine, mine), mine)
    s_mine_ref[...] = s_ref[place, :]
    feat = split(feat_ref[place, :])
    for h in range(HEADS):
        dp_ref[:, cells[h]] = dot_halves(feat, [half[feats[h], :] for half in t])
    return tops, totals, sums


def backward(s_mine_ref, dp_ref, tops, inverses, deltas, u_back, t_back):
    rows = tops[0].shape[1]
    probs, d_scores = [], []
    for h in range(HEADS):
        cells = slice(h * rows, (h + 1) * rows)
        prob = jnp.exp2(s_mine_ref[:, cells] - tops[h]) * inverses[h]
        probs.append(prob)
        d_scores.append(prob * (dp_ref[:, cells] - deltas[h]))
    return dot_halves(split(jnp.concatenate(d_scores, axis=1)), u_back) + dot_halves(
        split(jnp.concatenate(probs, axis=1)), t_back
    )


def halves_of(refs):
    return [ref[...] for ref in refs]


def first_half_kernel(
    head_ref, feat_ref, u_top_ref, u_low_ref, t_top_ref, t_low_ref, v_top_ref, v_low_ref,
    s_mine_ref, dp_ref, sums_ref, state_ref, s_ref, v_ref,
):
    tops, totals, sums = forward(
        head_ref, feat_ref, (u_top_ref, u_low_ref), (t_top_ref, t_low_ref),
        halves_of((v_top_ref, v_low_ref)), s_ref, v_ref, s_mine_ref, dp_ref,
    )
    for h in range(HEADS):
        sums_ref[of_head(h, 1), :] = sums[h]
        state_ref[h : h + 1, :] = tops[h]
        state_ref[HEADS + h : HEADS + h + 1, :] = totals[h]


def second_half_kernel(
    head_ref, sums_ref, state_ref, feat_ref, d_t_ref, u_top_ref, u_low_ref, t_top_ref,
    t_low_ref, v_top_ref, v_low_ref, u_back_top_ref, u_back_low_ref, t_back_top_ref,
    t_back_low_ref, att_t_ref, give_ref, out_state_ref, s_ref, v_ref, s_mine_ref, dp_ref,
):
    tops, totals, sums = forward(
        head_ref, feat_ref, (u_top_ref, u_low_ref), (t_top_ref, t_low_ref),
        halves_of((v_top_ref, v_low_ref)), s_ref, v_ref, s_mine_ref, dp_ref,
    )
    inverses, deltas = [], []
    for h in range(HEADS):
        other_top = state_ref[h : h + 1, :]
        other_total = state_ref[HEADS + h : HEADS + h + 1, :]
        top = jnp.maximum(tops[h], other_top)
        factor, other = jnp.exp2(tops[h] - top), jnp.exp2(other_top - top)
        inverse = 1.0 / (totals[h] * factor + other_total * other)
        att = (sums[h] * factor + sums_ref[of_head(h, 1), :] * other) * inverse
        att_t_ref[of_head(h, 1), :] = att
        tops[h] = top
        inverses.append(inverse)
        deltas.append(jnp.sum(d_t_ref[of_head(h, 1), :] * att, axis=0, keepdims=True))
    for i, row in enumerate(tops + inverses + deltas):
        out_state_ref[i : i + 1, :] = row
    give_ref[...] = backward(
        s_mine_ref, dp_ref, tops, inverses, deltas,
        halves_of((u_back_top_ref, u_back_low_ref)), halves_of((t_back_top_ref, t_back_low_ref)),
    )


def keep_kernel(
    s_mine_ref, dp_ref, state_ref, u_back_top_ref, u_back_low_ref, t_back_top_ref,
    t_back_low_ref, keep_ref,
):
    rows = [state_ref[i : i + 1, :] for i in range(3 * HEADS)]
    keep_ref[...] = backward(
        s_mine_ref, dp_ref, rows[:HEADS], rows[HEADS : 2 * HEADS], rows[2 * HEADS :],
        halves_of((u_back_top_ref, u_back_low_ref)), halves_of((t_back_top_ref, t_back_low_ref)),
    )


def add_kernel(own, keep_ref, recv_ref, *outs):
    for i, out in enumerate(outs):
        rows = pl.ds(i * own, own)
        out[...] = dense(keep_ref[rows, :] + recv_ref[rows, :])


def output_kernel(mixed_t_ref, att_t_ref, w_ref, out_t_ref):
    out_t_ref[...] = mixed_t_ref[...] + dot(w_ref[...].T, att_t_ref[...])


def sum_kernel(*refs):
    total = refs[0][...]
    for ref in refs[1:-1]:
        total = total + ref[...]
    refs[-1][...] = undense(total, refs[-1].shape[1])


def shards(
    features,
    face_weight,
    faces,
    face_live,
    send_index,
    anchor_index,
    w_in,
    w_out,
    w_query,
    w_key,
    w_value,
    w_attn_out,
    out_grad,
):
    rows, width = features.shape
    halos = send_index.shape[1]
    units = w_in.shape[1]
    own = anchor_index.shape[0]
    n_dom, n_head, n_aux = (lax.axis_size(a) for a in ("dom", "head", "aux"))
    assert n_aux == 2
    anchors = own * n_head
    mine = own * n_dom
    count = anchors * n_dom
    head = lax.axis_index("head").astype(I32).reshape(1)
    swap = [(0, 1), (1, 0)]

    def along(value, step):
        return lax.ppermute(value, "dom", [(i, (i + step) % n_dom) for i in range(n_dom)])

    def head_sum(part):
        if n_head == 2:
            return part, lax.ppermute(part, "head", swap)
        return lax.psum(part, "head"), jnp.zeros_like(part)

    x_t, g_t, w_out_t = features.T, out_grad.T, w_out.T
    to_lower, to_upper, index, faces, x_t, w_in = call(
        outgoing_kernel,
        [
            dense_shape(halos, width), dense_shape(halos, width), (1, own, I32), (*faces.shape, I32), (width, rows),
            w_in.shape,
        ],
        [send_index, anchor_index.reshape(1, own), faces, x_t, w_in],
        hbm=range(5),
        scratch=[pltpu.VMEM((2, halos), I32), pltpu.SemaphoreType.DMA((5,))],
    )
    from_upper = along(to_lower, n_dom - 1)
    from_lower = along(to_upper, 1)
    if n_head == 2:
        other_index = lax.ppermute(index, "head", swap)
    else:
        other_index = lax.all_gather(index, "head").reshape(1, anchors)
    pre_t, halo_mat, w_top, w_low = call(
        own_faces_kernel,
        [(units, rows), (2 * halos, rows)] + [(units, width, BF)] * 2,
        [face_live.reshape(1, 1), x_t, faces, face_weight.reshape(1, -1), w_in],
        flops=2 * 10**9,
    )
    pre_pick, halo_pick, anchor_x = call(
        pick_kernel,
        [(units, anchors), (2 * halos, anchors), (anchors, width)],
        [head, index, other_index, pre_t, halo_mat, x_t],
        smem=(0,),
    )
    anchor_part, top, low = call(
        anchor_part_kernel,
        [dense_shape(anchors, width)] + [(width, 2 * halos, BF)] * 2,
        [from_lower, from_upper, pre_pick, halo_pick, w_top, w_low, w_out_t],
        flops=10**9,
    )
    anchor_part, anchor_recv = head_sum(anchor_part)
    (part,) = call(
        rest_kernel,
        [(width, rows)],
        [top, low, halo_mat, pre_t, w_top, w_low, w_out_t],
        flops=10**9,
    )
    front = [(HEADS * width, rows, BF)] * 2
    back = [(HEADS * rows, width, BF)] * 2
    d_t, v_top, v_low, t_top, t_low, *t_back = call(
        cotangent_kernel,
        [(width, rows)] + [(width, width, BF)] * 2 + front + back,
        [g_t, w_attn_out, w_value, top],
        flops=10**9,
    )
    part, recv = head_sum(part)
    feats = call(
        anchor_kernel,
        [dense_shape(anchors, width)] * n_dom,
        [anchor_x, anchor_part, anchor_recv, d_t],
        flops=5 * 10**9,
    )
    feats = [feats[0]] + [along(feats[s], s) for s in range(1, n_dom)]
    mixed, u_top, u_low, *u_back = call(
        query_kernel,
        [(width, rows)] + front + back,
        [x_t, part, recv, w_query, w_key],
        flops=10**9,
    )
    fronts = [u_top, u_low, t_top, t_low, v_top, v_low]
    (feat_a,) = call(functools.partial(join_kernel, own), [(count, width)], [mixed] + feats)
    feat_b = lax.ppermute(feat_a, "aux", swap)
    in_mine = (mine, HEADS * rows)
    work = [pltpu.VMEM((count, HEADS * rows), F32), pltpu.VMEM((2 * width, count), BF)]
    s_mine, dp, sums, state = call(
        first_half_kernel,
        [in_mine, in_mine, (width, rows), (8, rows)],
        [head, feat_a, *fronts],
        smem=(0,),
        scratch=work,
        flops=2 * 10**9,
    )
    att, give, state = call(
        second_half_kernel,
        [(width, rows), (mine, width), (16, rows)],
        [head, sums, state, feat_b, d_t, *fronts, *u_back, *t_back],
        smem=(0,),
        scratch=work + [pltpu.VMEM(in_mine, F32)] * 2,
        flops=2 * 10**9,
    )
    recv = lax.ppermute(give, "aux", swap)
    (keep,) = call(
        keep_kernel,
        [(mine, width)],
        [s_mine, dp, state, *u_back, *t_back],
        flops=10**9,
    )
    sums = call(
        functools.partial(add_kernel, own), [dense_shape(own, width)] * n_dom, [keep, recv]
    )
    sums = [sums[0]] + [along(sums[s], n_dom - s) for s in reversed(range(1, n_dom))]
    (output_t,) = call(output_kernel, [(width, rows)], [mixed, att, w_attn_out])
    (anchor_grad,) = call(sum_kernel, [(own, width)], sums)
    return output_t.T, anchor_grad


def solution(mesh):
    placed = (
        P(("groups", "dom", "aux"), None),
        P(("groups", "dom", "aux")),
        P(None, ("groups", "dom", "aux")),
        P(("groups", "dom", "aux")),
        P(None, ("groups", "dom", "aux")),
        P(("groups", "dom", "head", "aux")),
        P(None, "head"),
        P("head", None),
        P(),
        P(),
        P(),
        P(),
        P(("groups", "dom", "aux"), None),
    )
    return jax.shard_map(
        shards,
        mesh=mesh,
        in_specs=placed,
        out_specs=(P(("groups", "dom", "aux"), None), P(("groups", "dom", "head", "aux"), None)),
        check_vma=False,
    )
```

time: 40.7 us -> 38.4 us (0.943)
  waiting for transfers between devices: 10.3 us -> 6.39 us
  Pallas kernels: 10.6 us -> 12.9 us
  starting transfers between devices: 18.2 us -> 17.1 us
    ppermute x6 -> x0, starting transfers between devices: 8.9 us -> none  [across(): return lax.ppermute(value, 'dom', [(i, i ^ step) for i in range(n_dom)])]
    ppermute x2 -> x8, starting transfers between devices: 3.82 us -> 11.7 us  [along(): lax.ppermute(value, 'dom', [(i, (i + step) % n_dom) for i in range(n_dom)])]
    ppermute x6 -> x0, waiting for transfers between devices: 6.34 us -> none  [across(): return lax.ppermute(value, 'dom', [(i, i ^ step) for i in range(n_dom)])]
    ppermute x2 -> x8, waiting for transfers between devices: 0.01 us -> 4.53 us  [along(): lax.ppermute(value, 'dom', [(i, (i + step) % n_dom) for i in range(n_dom)])]
    pallas_call x12 -> x15, Pallas kernels: 10.6 us -> 12.9 us  [call(): pl.pallas_call(body, out_shape=[jax.ShapeDtypeStruct(o[:2], o[2] if len(o...]
    ppermute x2, waiting for transfers between devices: 1.98 us -> 0.59 us  [head_sum(): return (part, lax.ppermute(part, 'head', swap))]
    ppermute x1, waiting for transfers between devices: 1.21 us -> 0.71 us  [shards(): recv = lax.ppermute(give, 'aux', swap)]
  transfers between devices with their start and end apart: 13 -> 13, of which waited for: 7 -> 8; matrix products, arithmetic and copies ran while one was open for 0% -> 0% of each run, Pallas kernels for 12% -> 20%
where the time goes in v3:
time: 38.4 us; the launch traced here: 38.2 us
  starting transfers between devices  17.1 us (45%)
  Pallas kernels  12.9 us (34%)
  waiting for transfers between devices  6.39 us (17%)
  between operations  1.44 us (4%)
  local copies, waits for them, and re-layouts  0.4 us (1%)
    pallas_call x15, Pallas kernels, call(): pl.pallas_call(body, out_shape=[jax.ShapeDtypeStruct(o[:2], o[2] if len(o...  12.9 us
    ppermute x8, starting transfers between devices, along(): lax.ppermute(value, 'dom', [(i, (i + step) % n_dom) for i in range(n_dom)])  11.7 us
    ppermute x8, waiting for transfers between devices, along(): lax.ppermute(value, 'dom', [(i, (i + step) % n_dom) for i in range(n_dom)])  4.53 us
    ppermute x1, starting transfers between devices, shards(): other_index = lax.ppermute(index, 'head', swap)  3 us
    ppermute x2, starting transfers between devices, head_sum(): return (part, lax.ppermute(part, 'head', swap))  2.16 us
  transfers between devices with their start and end apart: 13, of which 8 were waited for; matrix products, arithmetic and copies ran while one was open for 0% of the time, Pallas kernels for 20%

profile of v3, /device:TPU:0, one launch (start us, length us, event | category | flops | bytes accessed | tf_op | source)
XLA Modules:
  0.0 38.2 jit_solution(15866707402162895234)
XLA Ops:
  0.6 1.5 %shard_map.140 = (f32[48,128]{1,0:T(8,128)S(1)}, f32[48,128]{1,0:T(8,128)S(1)}, s32[1,32]{1,0:T(1,128)S(1)}, s32[3,1536]{1,0:T(4,128)S(1)}, f32[192,256]{1,0:T(8,128)S(1)}, /*index=5*/f32[384,384]{1,0:T(8,128)S(1)}) custom-call(s32[2,32]{1,0:T(2,128)} %send_hbm.1, s32[1,32]{1,0:T(1,128)} %bitcast.13, s32[3,1536]{1,0:T(4,128)} %faces_hbm.1, ...), custom_call_target="tpu_custom_call" | custom-call | flops 100000000 | bytes 1000000 | tf_op jit(solution)/shard_map/pallas_call | solution.py:73
  2.2 3.0 %collective-permute-start.2 = (s32[1,32]{1,0:T(1,128)S(1)}, s32[1,32]{1,0:T(1,128)S(1)}, u32[]{:S(2)}, u32[]{:S(2)}) collective-permute-start(s32[1,32]{1,0:T(1,128)S(1)} %get-tuple-element.48.own_ref), channel_id=1, source_target_pairs={{0,2},{2,0},{1,3},{3,1},{4,6},{6,4},{5,7},{7,5},{8,10},{10,8},{9,1... | collective-permute-start | bytes 392 | tf_op jit(solution)/shard_map/ppermute | solution.py:494
  5.2 1.6 %collective-permute-start = (f32[48,128]{1,0:T(8,128)S(1)}, f32[48,128]{1,0:T(8,128)S(1)}, u32[]{:S(2)}, u32[]{:S(2)}) collective-permute-start(f32[48,128]{1,0:T(8,128)S(1)} %get-tuple-element.46), channel_id=1, source_target_pairs={{0,4},{4,8},{8,12},{12,0},{1,5},{5,9},{9,13},{13,1},{2,6},{6,10},{... | collective-permute-start | bytes 73736 | tf_op jit(solution)/shard_map/ppermute | solution.py:473
  6.7 2.2 %collective-permute-start.1 = (f32[48,128]{1,0:T(8,128)S(1)}, f32[48,128]{1,0:T(8,128)S(1)}, u32[]{:S(2)}, u32[]{:S(2)}) collective-permute-start(f32[48,128]{1,0:T(8,128)S(1)} %get-tuple-element.47), channel_id=1, source_target_pairs={{0,12},{4,0},{8,4},{12,8},{1,13},{5,1},{9,5},{13,9},{2,14},{6,2},{... | collective-permute-start | bytes 73736 | tf_op jit(solution)/shard_map/ppermute | solution.py:473
  9.7 1.6 %shard_map.141 = (f32[384,256]{1,0:T(8,128)S(1)}, f32[64,256]{1,0:T(8,128)S(1)}, bf16[384,192]{1,0:T(8,128)(2,1)S(1)}, bf16[384,192]{1,0:T(8,128)(2,1)S(1)}) custom-call(s32[1,1]{1,0:T(1,128)} %bitcast.7.live_ref, f32[192,256]{1,0:T(8,128)S(1)} %get-tuple-element.45.x_t_ref, s32[3,1536]{1,0:T(4,128)S(1)} %get-tuple-element.49.faces_ref, ...), custom_call_target="tpu_custom_call" | custom-call | flops 2000000000 | bytes 1000000 | tf_op jit(solution)/shard_map/pallas_call | solution.py:73
  12.3 1.0 %shard_map.143 = (f32[96,128]{1,0:T(8,128)S(1)}, bf16[192,64]{1,0:T(8,128)(2,1)S(1)}, bf16[192,64]{1,0:T(8,128)(2,1)S(1)}) custom-call(f32[48,128]{1,0:T(8,128)S(1)} %collective-permute-done.lower_ref, f32[48,128]{1,0:T(8,128)S(1)} %collective-permute-done.1.upper_ref, f32[384,64]{1,0:T(8,128)S(1)} %get-tuple-element.53.pre_pick_ref, ...), custom_call_target="tpu_custom_call" | custom-call | flops 1000000000 | bytes 1000000 | tf_op jit(solution)/shard_map/pallas_call | solution.py:73
  13.7 1.0 %shard_map.144.part_ref = f32[192,256]{1,0:T(8,128)S(1)} custom-call(bf16[192,64]{1,0:T(8,128)(2,1)S(1)} %get-tuple-element.57.top_ref._, bf16[192,64]{1,0:T(8,128)(2,1)S(1)} %get-tuple-element.58.low_ref, f32[64,256]{1,0:T(8,128)S(1)} %get-tuple-element.52.halo_mat_ref, f32[384,256]{1,0:T(8,128)S(1)} %get-tuple-element.51.pre_t_ref, ...), custom_call_target="tpu_custom_call" | custom-call | flops 1000000000 | bytes 1000000 | tf_op jit(solution)/shard_map/pallas_call | solution.py:73
  14.7 1.8 %collective-permute-start.3 = (f32[192,256]{1,0:T(8,128)S(1)}, f32[192,256]{1,0:T(8,128)S(1)}, u32[]{:S(2)}, u32[]{:S(2)}) collective-permute-start(f32[192,256]{1,0:T(8,128)S(1)} %shard_map.144.part_ref), channel_id=1, source_target_pairs={{0,2},{2,0},{1,3},{3,1},{4,6},{6,4},{5,7},{7,5},{8,10},{10,8},{9,1... | collective-permute-start | bytes 589832 | tf_op jit(solution)/shard_map/ppermute | solution.py:477
  16.5 0.8 %shard_map.146 = (f32[192,256]{1,0:T(8,128)S(1)}, bf16[192,192]{1,0:T(8,128)(2,1)S(1)}, bf16[192,192]{1,0:T(8,128)(2,1)S(1)}, bf16[576,256]{1,0:T(8,128)(2,1)S(1...) custom-call(f32[192,256]{1,0:T(8,128)S(1)} %bitcast.10, ...), custom_call_target="tpu_custom_call" | custom-call | flops 1000000000 | bytes 1000000 | tf_op jit(solution)/shard_map/pallas_call | solution.py:73
  18.2 3.0 %collective-permute-start.6 = (f32[96,128]{1,0:T(8,128)S(1)}, f32[96,128]{1,0:T(8,128)S(1)}, u32[]{:S(2)}, u32[]{:S(2)}) collective-permute-start(f32[96,128]{1,0:T(8,128)S(1)} %get-tuple-element.65), channel_id=1, source_target_pairs={{0,8},{4,12},{8,0},{12,4},{1,9},{5,13},{9,1},{13,5},{2,10},{6,14},... | collective-permute-start | bytes 147464 | tf_op jit(solution)/shard_map/ppermute | solution.py:473
  21.3 0.9 %collective-permute-start.7 = (f32[96,128]{1,0:T(8,128)S(1)}, f32[96,128]{1,0:T(8,128)S(1)}, u32[]{:S(2)}, u32[]{:S(2)}) collective-permute-start(f32[96,128]{1,0:T(8,128)S(1)} %get-tuple-element.66), channel_id=1, source_target_pairs={{0,12},{4,0},{8,4},{12,8},{1,13},{5,1},{9,5},{13,9},{2,14},{6,2},{... | collective-permute-start | bytes 147464 | tf_op jit(solution)/shard_map/ppermute | solution.py:473
  22.1 0.9 %shard_map.145 = (f32[192,256]{1,0:T(8,128)S(1)}, bf16[576,256]{1,0:T(8,128)(2,1)S(1)}, bf16[576,256]{1,0:T(8,128)(2,1)S(1)}, bf16[768,192]{1,0:T(8,128)(2,1)S(1)}, bf16[768,192]{1,0:T(8,128)(2,1)S(1)}) custom-call(f32[192,256]{1,0:T(8,128)S(1)} %get-tuple-element.45.x_t_ref, f32[192,256]{1,0:T(8,128)S(1)} %shard_map.144.part_ref, ...), custom_call_target="tpu_custom_call" | custom-call | flops 1000000000 | bytes 1000000 | tf_op jit(solution)/shard_map/pallas_call | solution.py:73
  23.1 1.1 %collective-permute-done.5.refs_1_ = f32[96,128]{1,0:T(8,128)S(1)} collective-permute-done((f32[96,128]{1,0:T(8,128)S(1)}, f32[96,128]{1,0:T(8,128)S(1)}, u32[]{:S(2)}, u32[]{:S(2)}) %collective-permute-start.5) | collective-permute-done | bytes 49184 | tf_op jit(solution)/shard_map/ppermute | solution.py:473
  24.1 1.2 %collective-permute-done.7.refs_3_ = f32[96,128]{1,0:T(8,128)S(1)} collective-permute-done((f32[96,128]{1,0:T(8,128)S(1)}, f32[96,128]{1,0:T(8,128)S(1)}, u32[]{:S(2)}, u32[]{:S(2)}) %collective-permute-start.7) | collective-permute-done | bytes 49184 | tf_op jit(solution)/shard_map/ppermute | solution.py:473
  25.5 1.0 %shard_map.149 = (f32[128,768]{1,0:T(8,128)S(1)}, f32[128,768]{1,0:T(8,128)S(1)}, f32[192,256]{1,0:T(8,128)S(1)}, f32[8,256]{1,0:T(8,128)S(1)}) custom-call(s32[1]{0:T(128)} %bitcast.2.head_ref, f32[256,192]{1,0:T(8,128)S(1)} %shard_map.148.feat_ref, bf16[576,256]{1,0:T(8,128)(2,1)S(1)} %get-tuple-element.67.u_top_ref, ...), custom_call_target="tpu_custom_call" | custom-call | flops 2000000000 | bytes 1000000 | tf_op jit(solution)/shard_map/pallas_call | solution.py:73
  27.0 1.8 %shard_map.150 = (f32[192,256]{1,0:T(8,128)S(1)}, f32[128,192]{1,0:T(8,128)S(1)}, f32[16,256]{1,0:T(8,128)S(1)}) custom-call(s32[1]{0:T(128)} %bitcast.2.head_ref, f32[192,256]{1,0:T(8,128)S(1)} %get-tuple-element.73.sums_ref, f32[8,256]{1,0:T(8,128)S(1)} %get-tuple-element.74.state_ref, f32[256,192]{1,0:T(8,128)S(1)} %collective-permute-done.8.feat_ref, ...), custom_call_target="tpu_custom_call" | custom-call | flops 2000000000 | bytes 1000000 | tf_op jit(solution)/shard_map/pallas_call | solution.py:73
  29.6 0.7 %collective-permute-done.9.recv_ref = f32[128,192]{1,0:T(8,128)S(1)} collective-permute-done((f32[128,192]{1,0:T(8,128)S(1)}, f32[128,192]{1,0:T(8,128)S(1)}, u32[]{:S(2)}, u32[]{:S(2)}) %collective-permute-start.9) | collective-permute-done | bytes 98336 | tf_op jit(solution)/shard_map/ppermute | solution.py:565
  30.4 1.4 %collective-permute-start.10 = (f32[48,128]{1,0:T(8,128)S(1)}, f32[48,128]{1,0:T(8,128)S(1)}, u32[]{:S(2)}, u32[]{:S(2)}) collective-permute-start(f32[48,128]{1,0:T(8,128)S(1)} %get-tuple-element.85), channel_id=1, source_target_pairs={{0,4},{4,8},{8,12},{12,0},{1,5},{5,9},{9,13},{13,1},{2,6},{6,10},{... | collective-permute-start | bytes 73736 | tf_op jit(solution)/shard_map/ppermute | solution.py:473
  31.8 2.0 %collective-permute-start.11 = (f32[48,128]{1,0:T(8,128)S(1)}, f32[48,128]{1,0:T(8,128)S(1)}, u32[]{:S(2)}, u32[]{:S(2)}) collective-permute-start(f32[48,128]{1,0:T(8,128)S(1)} %get-tuple-element.86), channel_id=1, source_target_pairs={{0,8},{4,12},{8,0},{12,4},{1,9},{5,13},{9,1},{13,5},{2,10},{6,14},... | collective-permute-start | bytes 73736 | tf_op jit(solution)/shard_map/ppermute | solution.py:473
  34.3 1.0 %shard_map.151 = f32[192,256]{1,0:T(8,128)} custom-call(f32[192,256]{1,0:T(8,128)S(1)} %get-tuple-element.59._.mixed_t_ref, f32[192,256]{1,0:T(8,128)S(1)} %get-tuple-element.79.att_t_ref, f32[192,192]{1,0:T(8,128)S(1)} %copy-done), custom_call_target="tpu_custom_call" | custom-call | flops 100000000 | bytes 1000000 | tf_op jit(solution)/shard_map/pallas_call | solution.py:73
  35.3 0.7 %collective-permute-done.10.refs_1_ = f32[48,128]{1,0:T(8,128)S(1)} collective-permute-done((f32[48,128]{1,0:T(8,128)S(1)}, f32[48,128]{1,0:T(8,128)S(1)}, u32[]{:S(2)}, u32[]{:S(2)}) %collective-permute-start.10) | collective-permute-done | bytes 24608 | tf_op jit(solution)/shard_map/ppermute | solution.py:473
  36.0 0.7 %collective-permute-done.11.refs_2_ = f32[48,128]{1,0:T(8,128)S(1)} collective-permute-done((f32[48,128]{1,0:T(8,128)S(1)}, f32[48,128]{1,0:T(8,128)S(1)}, u32[]{:S(2)}, u32[]{:S(2)}) %collective-permute-start.11) | collective-permute-done | bytes 24608 | tf_op jit(solution)/shard_map/ppermute | solution.py:473
  36.7 0.9 %collective-permute-done.12.refs_3_ = f32[48,128]{1,0:T(8,128)S(1)} collective-permute-done((f32[48,128]{1,0:T(8,128)S(1)}, f32[48,128]{1,0:T(8,128)S(1)}, u32[]{:S(2)}, u32[]{:S(2)}) %collective-permute-start.12) | collective-permute-done | bytes 24608 | tf_op jit(solution)/shard_map/ppermute | solution.py:473
  37.5 0.7 %shard_map.154 = f32[32,192]{1,0:T(8,128)} custom-call(f32[48,128]{1,0:T(8,128)S(1)} %get-tuple-element.84.refs_0_, f32[48,128]{1,0:T(8,128)S(1)} %collective-permute-done.10.refs_1_, f32[48,128]{1,0:T(8,128)S(1)} %collective-permute-done.11.refs_2_, f32[48,128]{1,0:T(8,128)S(1)} %collective-permute-done.12.refs_3_), custom_call_target="tpu_custom_call" | custom-call | flops 100000000 | bytes 1000000 | tf_op jit(solution)/shard_map/pallas_call | solution.py:73
  (32 shorter events, 4.4 us)
Async XLA Ops:
  0.6 9.0 %copy-start.6 = (f32[1536]{0:T(1024)S(1)}, f32[1536]{0:T(1024)}, u32[]{:S(2)}) copy-start(f32[1536]{0:T(1024)} %param.14) | copy-start | bytes 18436
  2.2 9.1 %collective-permute-start.2 = (s32[1,32]{1,0:T(1,128)S(1)}, s32[1,32]{1,0:T(1,128)S(1)}, u32[]{:S(2)}, u32[]{:S(2)}) collective-permute-start(s32[1,32]{1,0:T(1,128)S(1)} %get-tuple-element.48.own_ref), channel_id=1, source_target_pairs={{0,2},{2,0},{1,3},{3,1},{4,6},{6,4},{5,7},{7,5},{8,10},{10,8},{9,1... | collective-permute-start | bytes 392 | tf_op jit(solution)/shard_map/ppermute | solution.py:494
  5.2 6.7 %collective-permute-start = (f32[48,128]{1,0:T(8,128)S(1)}, f32[48,128]{1,0:T(8,128)S(1)}, u32[]{:S(2)}, u32[]{:S(2)}) collective-permute-start(f32[48,128]{1,0:T(8,128)S(1)} %get-tuple-element.46), channel_id=1, source_target_pairs={{0,4},{4,8},{8,12},{12,0},{1,5},{5,9},{9,13},{13,1},{2,6},{6,10},{... | collective-permute-start | bytes 73736 | tf_op jit(solution)/shard_map/ppermute | solution.py:473
  6.7 5.1 %collective-permute-start.1 = (f32[48,128]{1,0:T(8,128)S(1)}, f32[48,128]{1,0:T(8,128)S(1)}, u32[]{:S(2)}, u32[]{:S(2)}) collective-permute-start(f32[48,128]{1,0:T(8,128)S(1)} %get-tuple-element.47), channel_id=1, source_target_pairs={{0,12},{4,0},{8,4},{12,8},{1,13},{5,1},{9,5},{13,9},{2,14},{6,2},{... | collective-permute-start | bytes 73736 | tf_op jit(solution)/shard_map/ppermute | solution.py:473
  11.3 1.0 %copy-start.1 = (f32[384,192]{0,1:T(8,128)S(1)}, f32[384,192]{0,1:T(8,128)}, u32[]{:S(2)}) copy-start(f32[384,192]{0,1:T(8,128)} %param.20) | copy-start | bytes 884740
  13.3 4.6 %collective-permute-start.4 = (f32[96,128]{1,0:T(8,128)S(1)}, f32[96,128]{1,0:T(8,128)S(1)}, u32[]{:S(2)}, u32[]{:S(2)}) collective-permute-start(f32[96,128]{1,0:T(8,128)S(1)} %get-tuple-element.61.part_ref), channel_id=1, source_target_pairs={{0,2},{2,0},{1,3},{3,1},{4,6},{6,4},{5,7},{7,5},{8,10},{10,8},{9,1... | collective-permute-start | bytes 147464 | tf_op jit(solution)/shard_map/ppermute | solution.py:477
  13.7 2.8 %copy-start = (f32[192,192]{1,0:T(8,128)S(1)}, f32[192,192]{1,0:T(8,128)}, u32[]{:S(2)}) copy-start(f32[192,192]{1,0:T(8,128)} %w_ref.5) | copy-start | bytes 442372
  13.7 2.8 %copy-start.2 = (f32[256,192]{0,1:T(8,128)S(1)}, f32[256,192]{0,1:T(8,128)}, u32[]{:S(2)}) copy-start(f32[256,192]{0,1:T(8,128)} %param.25) | copy-start | bytes 589828
  13.7 2.8 %copy-start.3 = (f32[192,192]{1,0:T(8,128)S(1)}, f32[192,192]{1,0:T(8,128)}, u32[]{:S(2)}) copy-start(f32[192,192]{1,0:T(8,128)} %wv_ref.1) | copy-start | bytes 442372
  14.7 7.4 %collective-permute-start.3 = (f32[192,256]{1,0:T(8,128)S(1)}, f32[192,256]{1,0:T(8,128)S(1)}, u32[]{:S(2)}, u32[]{:S(2)}) collective-permute-start(f32[192,256]{1,0:T(8,128)S(1)} %shard_map.144.part_ref), channel_id=1, source_target_pairs={{0,2},{2,0},{1,3},{3,1},{4,6},{6,4},{5,7},{7,5},{8,10},{10,8},{9,1... | collective-permute-start | bytes 589832 | tf_op jit(solution)/shard_map/ppermute | solution.py:477
  17.9 4.2 %copy-start.4 = (f32[192,192]{1,0:T(8,128)S(1)}, f32[192,192]{1,0:T(8,128)}, u32[]{:S(2)}) copy-start(f32[192,192]{1,0:T(8,128)} %w_ref.3) | copy-start | bytes 442372
  17.9 4.2 %copy-start.5 = (f32[192,192]{1,0:T(8,128)S(1)}, f32[192,192]{1,0:T(8,128)}, u32[]{:S(2)}) copy-start(f32[192,192]{1,0:T(8,128)} %wk_ref.1) | copy-start | bytes 442372
  18.2 5.9 %collective-permute-start.5 = (f32[96,128]{1,0:T(8,128)S(1)}, f32[96,128]{1,0:T(8,128)S(1)}, u32[]{:S(2)}, u32[]{:S(2)}) collective-permute-start(f32[96,128]{1,0:T(8,128)S(1)} %get-tuple-element.64), channel_id=1, source_target_pairs={{0,4},{4,8},{8,12},{12,0},{1,5},{5,9},{9,13},{13,1},{2,6},{6,10},{... | collective-permute-start | bytes 147464 | tf_op jit(solution)/shard_map/ppermute | solution.py:473
  18.2 5.9 %collective-permute-start.6 = (f32[96,128]{1,0:T(8,128)S(1)}, f32[96,128]{1,0:T(8,128)S(1)}, u32[]{:S(2)}, u32[]{:S(2)}) collective-permute-start(f32[96,128]{1,0:T(8,128)S(1)} %get-tuple-element.65), channel_id=1, source_target_pairs={{0,8},{4,12},{8,0},{12,4},{1,9},{5,13},{9,1},{13,5},{2,10},{6,14},... | collective-permute-start | bytes 147464 | tf_op jit(solution)/shard_map/ppermute | solution.py:473
  21.3 4.1 %collective-permute-start.7 = (f32[96,128]{1,0:T(8,128)S(1)}, f32[96,128]{1,0:T(8,128)S(1)}, u32[]{:S(2)}, u32[]{:S(2)}) collective-permute-start(f32[96,128]{1,0:T(8,128)S(1)} %get-tuple-element.66), channel_id=1, source_target_pairs={{0,12},{4,0},{8,4},{12,8},{1,13},{5,1},{9,5},{13,9},{2,14},{6,2},{... | collective-permute-start | bytes 147464 | tf_op jit(solution)/shard_map/ppermute | solution.py:473
  25.4 1.6 %collective-permute-start.8 = (f32[256,192]{1,0:T(8,128)S(1)}, f32[256,192]{1,0:T(8,128)S(1)}, u32[]{:S(2)}, u32[]{:S(2)}) collective-permute-start(f32[256,192]{1,0:T(8,128)S(1)} %shard_map.148.feat_ref), channel_id=1, source_target_pairs={{0,1},{1,0},{2,3},{3,2},{4,5},{5,4},{6,7},{7,6},{8,9},{9,8},{10,11... | collective-permute-start | bytes 589832 | tf_op jit(solution)/shard_map/ppermute | solution.py:546
  28.9 1.4 %collective-permute-start.9 = (f32[128,192]{1,0:T(8,128)S(1)}, f32[128,192]{1,0:T(8,128)S(1)}, u32[]{:S(2)}, u32[]{:S(2)}) collective-permute-start(f32[128,192]{1,0:T(8,128)S(1)} %get-tuple-element.83), channel_id=1, source_target_pairs={{0,1},{1,0},{2,3},{3,2},{4,5},{5,4},{6,7},{7,6},{8,9},{9,8},{10,11... | collective-permute-start | bytes 294920 | tf_op jit(solution)/shard_map/ppermute | solution.py:565
  30.4 5.7 %collective-permute-start.10 = (f32[48,128]{1,0:T(8,128)S(1)}, f32[48,128]{1,0:T(8,128)S(1)}, u32[]{:S(2)}, u32[]{:S(2)}) collective-permute-start(f32[48,128]{1,0:T(8,128)S(1)} %get-tuple-element.85), channel_id=1, source_target_pairs={{0,4},{4,8},{8,12},{12,0},{1,5},{5,9},{9,13},{13,1},{2,6},{6,10},{... | collective-permute-start | bytes 73736 | tf_op jit(solution)/shard_map/ppermute | solution.py:473
  31.8 4.9 %collective-permute-start.11 = (f32[48,128]{1,0:T(8,128)S(1)}, f32[48,128]{1,0:T(8,128)S(1)}, u32[]{:S(2)}, u32[]{:S(2)}) collective-permute-start(f32[48,128]{1,0:T(8,128)S(1)} %get-tuple-element.86), channel_id=1, source_target_pairs={{0,8},{4,12},{8,0},{12,4},{1,9},{5,13},{9,1},{13,5},{2,10},{6,14},... | collective-permute-start | bytes 73736 | tf_op jit(solution)/shard_map/ppermute | solution.py:473
  33.7 3.8 %collective-permute-start.12 = (f32[48,128]{1,0:T(8,128)S(1)}, f32[48,128]{1,0:T(8,128)S(1)}, u32[]{:S(2)}, u32[]{:S(2)}) collective-permute-start(f32[48,128]{1,0:T(8,128)S(1)} %get-tuple-element.87), channel_id=1, source_target_pairs={{0,12},{4,0},{8,4},{12,8},{1,13},{5,1},{9,5},{13,9},{2,14},{6,2},{... | collective-permute-start | bytes 73736 | tf_op jit(solution)/shard_map/ppermute | solution.py:473

commit v4 on v3

--- a/solution.py
+++ b/solution.py
@@ -96,7 +96,7 @@
 
 def outgoing_kernel(
     send_hbm, index_hbm, faces_hbm, x_t_hbm, w_in_hbm,
-    lower_ref, upper_ref, index_ref, faces_ref, x_t_ref, w_in_ref, send_ref, sems,
+    lower_ref, upper_ref, index_ref, index_out_ref, faces_ref, x_t_ref, w_in_ref, send_ref, sems,
 ):
     copies = [
         pltpu.make_async_copy(source, target, sems.at[i])
@@ -120,6 +120,8 @@
     upper_ref[...] = dense(sent[halos:])
     for copy in copies[2:]:
         copy.wait()
+    index_out_ref[...] = jnp.zeros_like(index_out_ref)
+    index_out_ref[0:1, 0 : index_ref.shape[1]] = index_ref[...]
 
 
 def small_chosen(index, rows, value):
@@ -166,9 +168,10 @@
 
 def every_index(head_ref, own_ref, other_ref):
     own = own_ref.shape[1]
-    if other_ref.shape[1] > own:
+    if other_ref.shape[0] == 1:
         return other_ref[...]
     first = head_ref[0] == 0
+    other_ref = other_ref.at[0:1, 0:own]
     return jnp.concatenate(
         [
             jnp.where(first, own_ref[...], other_ref[...]),
@@ -178,53 +181,23 @@
     )
 
 
-def take(value, pick):
-    rows = value.shape[0]
-    taken = dot_bf(jnp.concatenate(exact_parts(value), axis=0), pick)
-    return taken[:rows] + (taken[rows : 2 * rows] + taken[2 * rows :])
-
-
-def pick_kernel(
-    head_ref, own_ref, other_ref, pre_t_ref, halo_mat_ref, x_t_ref,
-    pre_pick_ref, halo_pick_ref, anchor_x_ref,
-):
-    pick = chosen(every_index(head_ref, own_ref, other_ref), pre_t_ref.shape[1])
-    pre_pick_ref[...] = take(pre_t_ref[...], pick)
-    halo_pick_ref[...] = take(halo_mat_ref[...], pick)
-    anchor_x_ref[...] = take(x_t_ref[...], pick).T
-
-
-def hidden_part(halo_t, halo_mat, pre_t, w_in_halves, w_out_t):
-    halo_agg = dot_halves(halo_t, split(halo_mat))
-    pre = pre_t + dot_halves(w_in_halves, split(halo_agg))
-    hidden = 0.5 * pre * (1.0 + lax.erf(pre * math.sqrt(0.5)))
-    return dot(w_out_t, hidden)
-
-
-def anchor_part_kernel(
-    lower_ref, upper_ref, pre_pick_ref, halo_pick_ref, w_top_ref, w_low_ref, w_out_t_ref,
-    part_ref, top_ref, low_ref,
+def hidden_kernel(
+    head_ref, lower_ref, upper_ref, own_ref, other_ref, pre_t_ref, halo_mat_ref, w_top_ref,
+    w_low_ref, w_out_t_ref, top_ref, low_ref, anchor_ref,
 ):
     width = w_top_ref.shape[1]
-    halo = jnp.concatenate(
+    halo_t = jnp.concatenate(
         [undense(lower_ref[...], width), undense(upper_ref[...], width)], axis=0
-    )
-    halo_t = split(halo.T)
-    part = hidden_part(
-        halo_t, halo_pick_ref[...], pre_pick_ref[...], (w_top_ref[...], w_low_ref[...]),
-        w_out_t_ref[...],
-    )
-    part_ref[...] = dense(part.T)
-    top_ref[...], low_ref[...] = halo_t
-
-
-def rest_kernel(
-    top_ref, low_ref, halo_mat_ref, pre_t_ref, w_top_ref, w_low_ref, w_out_t_ref, part_t_ref
-):
-    part_t_ref[...] = hidden_part(
-        (top_ref[...], low_ref[...]), halo_mat_ref[...], pre_t_ref[...],
-        (w_top_ref[...], w_low_ref[...]), w_out_t_ref[...],
-    )
+    ).T
+    halo_agg = dot(halo_t, halo_mat_ref[...])
+    pre = pre_t_ref[...] + dot_halves((w_top_ref[...], w_low_ref[...]), split(halo_agg))
+    units, rows = pre.shape
+    halves = split(0.5 * pre * (1.0 + lax.erf(pre * math.sqrt(0.5))))
+    pick = chosen(every_index(head_ref, own_ref, other_ref), rows)
+    anchors = dot_bf(jnp.concatenate(halves, axis=0), pick).astype(BF)
+    part = dot_halves(split(w_out_t_ref[...]), (anchors[:units], anchors[units:]))
+    anchor_ref[...] = dense(part.T)
+    top_ref[...], low_ref[...] = halves
 
 
 def split_heads(value_t):
@@ -232,6 +205,18 @@
     for h in range(HEADS):
         out += split(value_t[h * DH : (h + 1) * DH])
     return jnp.concatenate(out, axis=0)
+
+
+def rest_kernel(
+    head_ref, own_ref, other_ref, top_ref, low_ref, w_out_t_ref, x_t_ref, part_t_ref,
+    anchor_x_ref,
+):
+    part_t_ref[...] = dot_halves(split(w_out_t_ref[...]), (top_ref[...], low_ref[...]))
+    pick = chosen(every_index(head_ref, own_ref, other_ref), x_t_ref.shape[1])
+    width = x_t_ref.shape[0]
+    taken = dot_bf(jnp.concatenate(exact_parts(x_t_ref[...]), axis=0), pick)
+    taken = taken[:width] + (taken[width : 2 * width] + taken[2 * width :])
+    anchor_x_ref[...] = taken.T
 
 
 def through(w, value_t, front_refs, back_refs, back_scale):
@@ -478,10 +463,11 @@
         return lax.psum(part, "head"), jnp.zeros_like(part)
 
     x_t, g_t, w_out_t = features.T, out_grad.T, w_out.T
-    to_lower, to_upper, index, faces, x_t, w_in = call(
+    to_lower, to_upper, index, index_out, faces, x_t, w_in = call(
         outgoing_kernel,
         [
-            dense_shape(halos, width), dense_shape(halos, width), (1, own, I32), (*faces.shape, I32), (width, rows),
+            dense_shape(halos, width), dense_shape(halos, width), (1, own, I32),
+            (56, 128, I32), (*faces.shape, I32), (width, rows),
             w_in.shape,
         ],
         [send_index, anchor_index.reshape(1, own), faces, x_t, w_in],
@@ -491,32 +477,31 @@
     from_upper = along(to_lower, n_dom - 1)
     from_lower = along(to_upper, 1)
     if n_head == 2:
-        other_index = lax.ppermute(index, "head", swap)
+        other_index = lax.ppermute(index_out, "head", swap)
     else:
         other_index = lax.all_gather(index, "head").reshape(1, anchors)
     pre_t, halo_mat, w_top, w_low = call(
         own_faces_kernel,
         [(units, rows), (2 * halos, rows)] + [(units, width, BF)] * 2,
         [face_live.reshape(1, 1), x_t, faces, face_weight.reshape(1, -1), w_in],
-        flops=2 * 10**9,
-    )
-    pre_pick, halo_pick, anchor_x = call(
-        pick_kernel,
-        [(units, anchors), (2 * halos, anchors), (anchors, width)],
-        [head, index, other_index, pre_t, halo_mat, x_t],
+        flops=2*10**9,
+    )
+    top, low, anchor_part = call(
+        hidden_kernel,
+        [(units, rows, BF), (units, rows, BF), dense_shape(anchors, width)],
+        [
+            head, from_lower, from_upper, index, other_index, pre_t, halo_mat, w_top, w_low,
+            w_out_t,
+        ],
         smem=(0,),
-    )
-    anchor_part, top, low = call(
-        anchor_part_kernel,
-        [dense_shape(anchors, width)] + [(width, 2 * halos, BF)] * 2,
-        [from_lower, from_upper, pre_pick, halo_pick, w_top, w_low, w_out_t],
         flops=10**9,
     )
     anchor_part, anchor_recv = head_sum(anchor_part)
-    (part,) = call(
+    part, anchor_x = call(
         rest_kernel,
-        [(width, rows)],
-        [top, low, halo_mat, pre_t, w_top, w_low, w_out_t],
+        [(width, rows), (anchors, width)],
+        [head, index, other_index, top, low, w_out_t, x_t],
+        smem=(0,),
         flops=10**9,
     )
     front = [(HEADS * width, rows, BF)] * 2

time: 38.4 us -> 37.7 us (0.982)
  Pallas kernels: 12.9 us -> 12.1 us
  starting transfers between devices: 17.1 us -> 17.5 us
    ppermute x8, starting transfers between devices: 11.7 us -> 13.5 us  [along(): lax.ppermute(value, 'dom', [(i, (i + step) % n_dom) for i in range(n_dom)])]
    ppermute x1, starting transfers between devices: 3 us -> 1.64 us  [shards(): other_index = lax.ppermute(index_out, 'head', swap)]
    pallas_call x15 -> x14, Pallas kernels: 12.9 us -> 12.1 us  [call(): pl.pallas_call(body, out_shape=[jax.ShapeDtypeStruct(o[:2], o[2] if len(o...]
    ppermute x8, waiting for transfers between devices: 4.53 us -> 3.91 us  [along(): lax.ppermute(value, 'dom', [(i, (i + step) % n_dom) for i in range(n_dom)])]
    ppermute x2, waiting for transfers between devices: 0.59 us -> 1.12 us  [head_sum(): return (part, lax.ppermute(part, 'head', swap))]
  transfers between devices with their start and end apart: 13 -> 13, of which waited for: 8 -> 8; matrix products, arithmetic and copies ran while one was open for 0% -> 0% of each run, Pallas kernels for 20% -> 17%
where the time goes in v4:
time: 37.7 us; the launch traced here: 37.5 us
  starting transfers between devices  17.5 us (46%)
  Pallas kernels  12.1 us (32%)
  waiting for transfers between devices  6.3 us (17%)
  between operations  1.44 us (4%)
    ppermute x8, starting transfers between devices, along(): lax.ppermute(value, 'dom', [(i, (i + step) % n_dom) for i in range(n_dom)])  13.5 us
    pallas_call x14, Pallas kernels, call(): pl.pallas_call(body, out_shape=[jax.ShapeDtypeStruct(o[:2], o[2] if len(o...  12.1 us
    ppermute x8, waiting for transfers between devices, along(): lax.ppermute(value, 'dom', [(i, (i + step) % n_dom) for i in range(n_dom)])  3.91 us
    ppermute x2, starting transfers between devices, head_sum(): return (part, lax.ppermute(part, 'head', swap))  2.15 us
    ppermute x1, starting transfers between devices, shards(): other_index = lax.ppermute(index_out, 'head', swap)  1.64 us
    ppermute x2, waiting for transfers between devices, head_sum(): return (part, lax.ppermute(part, 'head', swap))  1.12 us
  transfers between devices with their start and end apart: 13, of which 8 were waited for; matrix products, arithmetic and copies ran while one was open for 0% of the time, Pallas kernels for 17%

profile of v4, /device:TPU:0, one launch (start us, length us, event | category | flops | bytes accessed | tf_op | source)
XLA Modules:
  0.0 37.5 jit_solution(10598270980055481074)
XLA Ops:
  0.6 1.5 %shard_map.140 = (f32[48,128]{1,0:T(8,128)S(1)}, f32[48,128]{1,0:T(8,128)S(1)}, s32[1,32]{1,0:T(1,128)S(1)}, s32[56,128]{1,0:T(8,128)S(1)}, s32[3,1536]{1,0:T(4,...) custom-call(s32[2,32]{1,0:T(2,128)} %send_hbm.1, s32[1,32]{1,0:T(1,128)} %bitcast.13, s32[3,1536]{1,0:T(4,128)} %faces_hbm.1, ...), custom_call_target="tpu_custom_call" | custom-call | flops 100000000 | bytes 1000000 | tf_op jit(solution)/shard_map/pallas_call | solution.py:73
  2.2 3.1 %collective-permute-start.1 = (f32[48,128]{1,0:T(8,128)S(1)}, f32[48,128]{1,0:T(8,128)S(1)}, u32[]{:S(2)}, u32[]{:S(2)}) collective-permute-start(f32[48,128]{1,0:T(8,128)S(1)} %get-tuple-element.48), channel_id=1, source_target_pairs={{0,4},{4,8},{8,12},{12,0},{1,5},{5,9},{9,13},{13,1},{2,6},{6,10},{... | collective-permute-start | bytes 73736 | tf_op jit(solution)/shard_map/ppermute | solution.py:458
  5.3 2.1 %collective-permute-start.2 = (f32[48,128]{1,0:T(8,128)S(1)}, f32[48,128]{1,0:T(8,128)S(1)}, u32[]{:S(2)}, u32[]{:S(2)}) collective-permute-start(f32[48,128]{1,0:T(8,128)S(1)} %get-tuple-element.49), channel_id=1, source_target_pairs={{0,12},{4,0},{8,4},{12,8},{1,13},{5,1},{9,5},{13,9},{2,14},{6,2},{... | collective-permute-start | bytes 73736 | tf_op jit(solution)/shard_map/ppermute | solution.py:458
  7.3 1.6 %collective-permute-start = (s32[56,128]{1,0:T(8,128)S(1)}, s32[56,128]{1,0:T(8,128)S(1)}, u32[]{:S(2)}, u32[]{:S(2)}) collective-permute-start(s32[56,128]{1,0:T(8,128)S(1)} %get-tuple-element.47), channel_id=1, source_target_pairs={{0,2},{2,0},{1,3},{3,1},{4,6},{6,4},{5,7},{7,5},{8,10},{10,8},{9,1... | collective-permute-start | bytes 86024 | tf_op jit(solution)/shard_map/ppermute | solution.py:480
  9.7 1.6 %shard_map.141 = (f32[384,256]{1,0:T(8,128)S(1)}, f32[64,256]{1,0:T(8,128)S(1)}, bf16[384,192]{1,0:T(8,128)(2,1)S(1)}, bf16[384,192]{1,0:T(8,128)(2,1)S(1)}) custom-call(s32[1,1]{1,0:T(1,128)} %bitcast.7.live_ref, f32[192,256]{1,0:T(8,128)S(1)} %get-tuple-element.45.x_t_ref, s32[3,1536]{1,0:T(4,128)S(1)} %get-tuple-element.50.faces_ref, ...), custom_call_target="tpu_custom_call" | custom-call | flops 2000000000 | bytes 1000000 | tf_op jit(solution)/shard_map/pallas_call | solution.py:73
  11.3 1.3 %shard_map.142 = (bf16[384,256]{1,0:T(8,128)(2,1)S(1)}, bf16[384,256]{1,0:T(8,128)(2,1)S(1)}, f32[96,128]{1,0:T(8,128)S(1)}) custom-call(s32[1]{0:T(128)} %bitcast.2.head_ref, f32[48,128]{1,0:T(8,128)S(1)} %collective-permute-done.1.lower_ref, f32[48,128]{1,0:T(8,128)S(1)} %collective-permute-done.2.upper_ref, s32[1,32]{1,0:T(1,128)S(1)} %get-tuple-element.46.own_ref, ...), custom_call_target="tpu_custom_call" | custom-call | flops 1000000000 | bytes 1000000 | tf_op jit(solution)/shard_map/pallas_call | solution.py:73
  12.7 1.6 %collective-permute-start.4 = (f32[96,128]{1,0:T(8,128)S(1)}, f32[96,128]{1,0:T(8,128)S(1)}, u32[]{:S(2)}, u32[]{:S(2)}) collective-permute-start(f32[96,128]{1,0:T(8,128)S(1)} %get-tuple-element.61.part_ref), channel_id=1, source_target_pairs={{0,2},{2,0},{1,3},{3,1},{4,6},{6,4},{5,7},{7,5},{8,10},{10,8},{9,1... | collective-permute-start | bytes 147464 | tf_op jit(solution)/shard_map/ppermute | solution.py:462
  15.4 0.8 %shard_map.145 = (f32[192,256]{1,0:T(8,128)S(1)}, bf16[192,192]{1,0:T(8,128)(2,1)S(1)}, bf16[192,192]{1,0:T(8,128)(2,1)S(1)}, bf16[576,256]{1,0:T(8,128)(2,1)S(1...) custom-call(f32[192,256]{1,0:T(8,128)S(1)} %bitcast.10, ...), custom_call_target="tpu_custom_call" | custom-call | flops 1000000000 | bytes 1000000 | tf_op jit(solution)/shard_map/pallas_call | solution.py:73
  16.2 1.1 %collective-permute-done.4.recv_ref = f32[96,128]{1,0:T(8,128)S(1)} collective-permute-done((f32[96,128]{1,0:T(8,128)S(1)}, f32[96,128]{1,0:T(8,128)S(1)}, u32[]{:S(2)}, u32[]{:S(2)}) %collective-permute-start.4) | collective-permute-done | bytes 49184 | tf_op jit(solution)/shard_map/ppermute | solution.py:462
  17.7 2.4 %collective-permute-start.6 = (f32[96,128]{1,0:T(8,128)S(1)}, f32[96,128]{1,0:T(8,128)S(1)}, u32[]{:S(2)}, u32[]{:S(2)}) collective-permute-start(f32[96,128]{1,0:T(8,128)S(1)} %get-tuple-element.65), channel_id=1, source_target_pairs={{0,8},{4,12},{8,0},{12,4},{1,9},{5,13},{9,1},{13,5},{2,10},{6,14},... | collective-permute-start | bytes 147464 | tf_op jit(solution)/shard_map/ppermute | solution.py:458
  20.0 1.4 %collective-permute-start.7 = (f32[96,128]{1,0:T(8,128)S(1)}, f32[96,128]{1,0:T(8,128)S(1)}, u32[]{:S(2)}, u32[]{:S(2)}) collective-permute-start(f32[96,128]{1,0:T(8,128)S(1)} %get-tuple-element.66), channel_id=1, source_target_pairs={{0,12},{4,0},{8,4},{12,8},{1,13},{5,1},{9,5},{13,9},{2,14},{6,2},{... | collective-permute-start | bytes 147464 | tf_op jit(solution)/shard_map/ppermute | solution.py:458
  21.5 0.9 %shard_map.144 = (f32[192,256]{1,0:T(8,128)S(1)}, bf16[576,256]{1,0:T(8,128)(2,1)S(1)}, bf16[576,256]{1,0:T(8,128)(2,1)S(1)}, bf16[768,192]{1,0:T(8,128)(2,1)S(1)}, bf16[768,192]{1,0:T(8,128)(2,1)S(1)}) custom-call(f32[192,256]{1,0:T(8,128)S(1)} %get-tuple-element.45.x_t_ref, f32[192,256]{1,0:T(8,128)S(1)} %get-tuple-element.58.part_ref, ...), custom_call_target="tpu_custom_call" | custom-call | flops 1000000000 | bytes 1000000 | tf_op jit(solution)/shard_map/pallas_call | solution.py:73
  22.4 1.1 %collective-permute-done.5.refs_1_ = f32[96,128]{1,0:T(8,128)S(1)} collective-permute-done((f32[96,128]{1,0:T(8,128)S(1)}, f32[96,128]{1,0:T(8,128)S(1)}, u32[]{:S(2)}, u32[]{:S(2)}) %collective-permute-start.5) | collective-permute-done | bytes 49184 | tf_op jit(solution)/shard_map/ppermute | solution.py:458
  23.5 0.6 %collective-permute-done.7.refs_3_ = f32[96,128]{1,0:T(8,128)S(1)} collective-permute-done((f32[96,128]{1,0:T(8,128)S(1)}, f32[96,128]{1,0:T(8,128)S(1)}, u32[]{:S(2)}, u32[]{:S(2)}) %collective-permute-start.7) | collective-permute-done | bytes 49184 | tf_op jit(solution)/shard_map/ppermute | solution.py:458
  24.3 1.0 %shard_map.148 = (f32[128,768]{1,0:T(8,128)S(1)}, f32[128,768]{1,0:T(8,128)S(1)}, f32[192,256]{1,0:T(8,128)S(1)}, f32[8,256]{1,0:T(8,128)S(1)}) custom-call(s32[1]{0:T(128)} %bitcast.2.head_ref, f32[256,192]{1,0:T(8,128)S(1)} %shard_map.147.feat_ref, bf16[576,256]{1,0:T(8,128)(2,1)S(1)} %get-tuple-element.67.u_top_ref, ...), custom_call_target="tpu_custom_call" | custom-call | flops 2000000000 | bytes 1000000 | tf_op jit(solution)/shard_map/pallas_call | solution.py:73
  25.8 1.8 %shard_map.149 = (f32[192,256]{1,0:T(8,128)S(1)}, f32[128,192]{1,0:T(8,128)S(1)}, f32[16,256]{1,0:T(8,128)S(1)}) custom-call(s32[1]{0:T(128)} %bitcast.2.head_ref, f32[192,256]{1,0:T(8,128)S(1)} %get-tuple-element.73.sums_ref, f32[8,256]{1,0:T(8,128)S(1)} %get-tuple-element.74.state_ref, f32[256,192]{1,0:T(8,128)S(1)} %collective-permute-done.8.feat_ref, ...), custom_call_target="tpu_custom_call" | custom-call | flops 2000000000 | bytes 1000000 | tf_op jit(solution)/shard_map/pallas_call | solution.py:73
  28.3 0.7 %collective-permute-done.9.recv_ref = f32[128,192]{1,0:T(8,128)S(1)} collective-permute-done((f32[128,192]{1,0:T(8,128)S(1)}, f32[128,192]{1,0:T(8,128)S(1)}, u32[]{:S(2)}, u32[]{:S(2)}) %collective-permute-start.9) | collective-permute-done | bytes 98336 | tf_op jit(solution)/shard_map/ppermute | solution.py:550
  29.1 2.0 %collective-permute-start.10 = (f32[48,128]{1,0:T(8,128)S(1)}, f32[48,128]{1,0:T(8,128)S(1)}, u32[]{:S(2)}, u32[]{:S(2)}) collective-permute-start(f32[48,128]{1,0:T(8,128)S(1)} %get-tuple-element.85), channel_id=1, source_target_pairs={{0,4},{4,8},{8,12},{12,0},{1,5},{5,9},{9,13},{13,1},{2,6},{6,10},{... | collective-permute-start | bytes 73736 | tf_op jit(solution)/shard_map/ppermute | solution.py:458
  31.2 1.8 %collective-permute-start.11 = (f32[48,128]{1,0:T(8,128)S(1)}, f32[48,128]{1,0:T(8,128)S(1)}, u32[]{:S(2)}, u32[]{:S(2)}) collective-permute-start(f32[48,128]{1,0:T(8,128)S(1)} %get-tuple-element.86), channel_id=1, source_target_pairs={{0,8},{4,12},{8,0},{12,4},{1,9},{5,13},{9,1},{13,5},{2,10},{6,14},... | collective-permute-start | bytes 73736 | tf_op jit(solution)/shard_map/ppermute | solution.py:458
  33.0 0.6 %collective-permute-start.12 = (f32[48,128]{1,0:T(8,128)S(1)}, f32[48,128]{1,0:T(8,128)S(1)}, u32[]{:S(2)}, u32[]{:S(2)}) collective-permute-start(f32[48,128]{1,0:T(8,128)S(1)} %get-tuple-element.87), channel_id=1, source_target_pairs={{0,12},{4,0},{8,4},{12,8},{1,13},{5,1},{9,5},{13,9},{2,14},{6,2},{... | collective-permute-start | bytes 73736 | tf_op jit(solution)/shard_map/ppermute | solution.py:458
  33.6 1.0 %shard_map.150 = f32[192,256]{1,0:T(8,128)} custom-call(f32[192,256]{1,0:T(8,128)S(1)} %get-tuple-element.59._.mixed_t_ref, f32[192,256]{1,0:T(8,128)S(1)} %get-tuple-element.79.att_t_ref, f32[192,192]{1,0:T(8,128)S(1)} %copy-done), custom_call_target="tpu_custom_call" | custom-call | flops 100000000 | bytes 1000000 | tf_op jit(solution)/shard_map/pallas_call | solution.py:73
  34.9 1.1 %collective-permute-done.11.refs_2_ = f32[48,128]{1,0:T(8,128)S(1)} collective-permute-done((f32[48,128]{1,0:T(8,128)S(1)}, f32[48,128]{1,0:T(8,128)S(1)}, u32[]{:S(2)}, u32[]{:S(2)}) %collective-permute-start.11) | collective-permute-done | bytes 24608 | tf_op jit(solution)/shard_map/ppermute | solution.py:458
  35.9 0.9 %collective-permute-done.12.refs_3_ = f32[48,128]{1,0:T(8,128)S(1)} collective-permute-done((f32[48,128]{1,0:T(8,128)S(1)}, f32[48,128]{1,0:T(8,128)S(1)}, u32[]{:S(2)}, u32[]{:S(2)}) %collective-permute-start.12) | collective-permute-done | bytes 24608 | tf_op jit(solution)/shard_map/ppermute | solution.py:458
  36.8 0.7 %shard_map.153 = f32[32,192]{1,0:T(8,128)} custom-call(f32[48,128]{1,0:T(8,128)S(1)} %get-tuple-element.84.refs_0_, f32[48,128]{1,0:T(8,128)S(1)} %collective-permute-done.10.refs_1_, f32[48,128]{1,0:T(8,128)S(1)} %collective-permute-done.11.refs_2_, f32[48,128]{1,0:T(8,128)S(1)} %collective-permute-done.12.refs_3_), custom_call_target="tpu_custom_call" | custom-call | flops 100000000 | bytes 1000000 | tf_op jit(solution)/shard_map/pallas_call | solution.py:73
  (31 shorter events, 3.3 us)
Async XLA Ops:
  0.6 9.0 %copy-start.6 = (f32[1536]{0:T(1024)S(1)}, f32[1536]{0:T(1024)}, u32[]{:S(2)}) copy-start(f32[1536]{0:T(1024)} %param.14) | copy-start | bytes 18436
  2.2 9.1 %collective-permute-start.1 = (f32[48,128]{1,0:T(8,128)S(1)}, f32[48,128]{1,0:T(8,128)S(1)}, u32[]{:S(2)}, u32[]{:S(2)}) collective-permute-start(f32[48,128]{1,0:T(8,128)S(1)} %get-tuple-element.48), channel_id=1, source_target_pairs={{0,4},{4,8},{8,12},{12,0},{1,5},{5,9},{9,13},{13,1},{2,6},{6,10},{... | collective-permute-start | bytes 73736 | tf_op jit(solution)/shard_map/ppermute | solution.py:458
  5.3 6.0 %collective-permute-start.2 = (f32[48,128]{1,0:T(8,128)S(1)}, f32[48,128]{1,0:T(8,128)S(1)}, u32[]{:S(2)}, u32[]{:S(2)}) collective-permute-start(f32[48,128]{1,0:T(8,128)S(1)} %get-tuple-element.49), channel_id=1, source_target_pairs={{0,12},{4,0},{8,4},{12,8},{1,13},{5,1},{9,5},{13,9},{2,14},{6,2},{... | collective-permute-start | bytes 73736 | tf_op jit(solution)/shard_map/ppermute | solution.py:458
  7.3 4.0 %collective-permute-start = (s32[56,128]{1,0:T(8,128)S(1)}, s32[56,128]{1,0:T(8,128)S(1)}, u32[]{:S(2)}, u32[]{:S(2)}) collective-permute-start(s32[56,128]{1,0:T(8,128)S(1)} %get-tuple-element.47), channel_id=1, source_target_pairs={{0,2},{2,0},{1,3},{3,1},{4,6},{6,4},{5,7},{7,5},{8,10},{10,8},{9,1... | collective-permute-start | bytes 86024 | tf_op jit(solution)/shard_map/ppermute | solution.py:480
  9.7 1.6 %copy-start.1 = (f32[384,192]{0,1:T(8,128)S(1)}, f32[384,192]{0,1:T(8,128)}, u32[]{:S(2)}) copy-start(f32[384,192]{0,1:T(8,128)} %param.20) | copy-start | bytes 884740
  12.7 4.7 %collective-permute-start.4 = (f32[96,128]{1,0:T(8,128)S(1)}, f32[96,128]{1,0:T(8,128)S(1)}, u32[]{:S(2)}, u32[]{:S(2)}) collective-permute-start(f32[96,128]{1,0:T(8,128)S(1)} %get-tuple-element.61.part_ref), channel_id=1, source_target_pairs={{0,2},{2,0},{1,3},{3,1},{4,6},{6,4},{5,7},{7,5},{8,10},{10,8},{9,1... | collective-permute-start | bytes 147464 | tf_op jit(solution)/shard_map/ppermute | solution.py:462
  14.3 1.0 %copy-start = (f32[192,192]{1,0:T(8,128)S(1)}, f32[192,192]{1,0:T(8,128)}, u32[]{:S(2)}) copy-start(f32[192,192]{1,0:T(8,128)} %w_ref.5) | copy-start | bytes 442372
  14.3 1.0 %copy-start.2 = (f32[256,192]{0,1:T(8,128)S(1)}, f32[256,192]{0,1:T(8,128)}, u32[]{:S(2)}) copy-start(f32[256,192]{0,1:T(8,128)} %param.25) | copy-start | bytes 589828
  14.3 1.1 %copy-start.3 = (f32[192,192]{1,0:T(8,128)S(1)}, f32[192,192]{1,0:T(8,128)}, u32[]{:S(2)}) copy-start(f32[192,192]{1,0:T(8,128)} %wv_ref.1) | copy-start | bytes 442372
  14.7 6.7 %collective-permute-start.3 = (f32[192,256]{1,0:T(8,128)S(1)}, f32[192,256]{1,0:T(8,128)S(1)}, u32[]{:S(2)}, u32[]{:S(2)}) collective-permute-start(f32[192,256]{1,0:T(8,128)S(1)} %get-tuple-element.58.part_ref), channel_id=1, source_target_pairs={{0,2},{2,0},{1,3},{3,1},{4,6},{6,4},{5,7},{7,5},{8,10},{10,8},{9,1... | collective-permute-start | bytes 589832 | tf_op jit(solution)/shard_map/ppermute | solution.py:462
  17.3 4.2 %copy-start.4 = (f32[192,192]{1,0:T(8,128)S(1)}, f32[192,192]{1,0:T(8,128)}, u32[]{:S(2)}) copy-start(f32[192,192]{1,0:T(8,128)} %w_ref.3) | copy-start | bytes 442372
  17.3 4.2 %copy-start.5 = (f32[192,192]{1,0:T(8,128)S(1)}, f32[192,192]{1,0:T(8,128)}, u32[]{:S(2)}) copy-start(f32[192,192]{1,0:T(8,128)} %wk_ref.1) | copy-start | bytes 442372
  17.6 5.9 %collective-permute-start.5 = (f32[96,128]{1,0:T(8,128)S(1)}, f32[96,128]{1,0:T(8,128)S(1)}, u32[]{:S(2)}, u32[]{:S(2)}) collective-permute-start(f32[96,128]{1,0:T(8,128)S(1)} %get-tuple-element.64), channel_id=1, source_target_pairs={{0,4},{4,8},{8,12},{12,0},{1,5},{5,9},{9,13},{13,1},{2,6},{6,10},{... | collective-permute-start | bytes 147464 | tf_op jit(solution)/shard_map/ppermute | solution.py:458
  17.7 5.9 %collective-permute-start.6 = (f32[96,128]{1,0:T(8,128)S(1)}, f32[96,128]{1,0:T(8,128)S(1)}, u32[]{:S(2)}, u32[]{:S(2)}) collective-permute-start(f32[96,128]{1,0:T(8,128)S(1)} %get-tuple-element.65), channel_id=1, source_target_pairs={{0,8},{4,12},{8,0},{12,4},{1,9},{5,13},{9,1},{13,5},{2,10},{6,14},... | collective-permute-start | bytes 147464 | tf_op jit(solution)/shard_map/ppermute | solution.py:458
  20.0 4.1 %collective-permute-start.7 = (f32[96,128]{1,0:T(8,128)S(1)}, f32[96,128]{1,0:T(8,128)S(1)}, u32[]{:S(2)}, u32[]{:S(2)}) collective-permute-start(f32[96,128]{1,0:T(8,128)S(1)} %get-tuple-element.66), channel_id=1, source_target_pairs={{0,12},{4,0},{8,4},{12,8},{1,13},{5,1},{9,5},{13,9},{2,14},{6,2},{... | collective-permute-start | bytes 147464 | tf_op jit(solution)/shard_map/ppermute | solution.py:458
  24.2 1.6 %collective-permute-start.8 = (f32[256,192]{1,0:T(8,128)S(1)}, f32[256,192]{1,0:T(8,128)S(1)}, u32[]{:S(2)}, u32[]{:S(2)}) collective-permute-start(f32[256,192]{1,0:T(8,128)S(1)} %shard_map.147.feat_ref), channel_id=1, source_target_pairs={{0,1},{1,0},{2,3},{3,2},{4,5},{5,4},{6,7},{7,6},{8,9},{9,8},{10,11... | collective-permute-start | bytes 589832 | tf_op jit(solution)/shard_map/ppermute | solution.py:531
  27.6 1.4 %collective-permute-start.9 = (f32[128,192]{1,0:T(8,128)S(1)}, f32[128,192]{1,0:T(8,128)S(1)}, u32[]{:S(2)}, u32[]{:S(2)}) collective-permute-start(f32[128,192]{1,0:T(8,128)S(1)} %get-tuple-element.83), channel_id=1, source_target_pairs={{0,1},{1,0},{2,3},{3,2},{4,5},{5,4},{6,7},{7,6},{8,9},{9,8},{10,11... | collective-permute-start | bytes 294920 | tf_op jit(solution)/shard_map/ppermute | solution.py:550
  29.1 5.7 %collective-permute-start.10 = (f32[48,128]{1,0:T(8,128)S(1)}, f32[48,128]{1,0:T(8,128)S(1)}, u32[]{:S(2)}, u32[]{:S(2)}) collective-permute-start(f32[48,128]{1,0:T(8,128)S(1)} %get-tuple-element.85), channel_id=1, source_target_pairs={{0,4},{4,8},{8,12},{12,0},{1,5},{5,9},{9,13},{13,1},{2,6},{6,10},{... | collective-permute-start | bytes 73736 | tf_op jit(solution)/shard_map/ppermute | solution.py:458
  31.2 4.8 %collective-permute-start.11 = (f32[48,128]{1,0:T(8,128)S(1)}, f32[48,128]{1,0:T(8,128)S(1)}, u32[]{:S(2)}, u32[]{:S(2)}) collective-permute-start(f32[48,128]{1,0:T(8,128)S(1)} %get-tuple-element.86), channel_id=1, source_target_pairs={{0,8},{4,12},{8,0},{12,4},{1,9},{5,13},{9,1},{13,5},{2,10},{6,14},... | collective-permute-start | bytes 73736 | tf_op jit(solution)/shard_map/ppermute | solution.py:458
  33.0 3.8 %collective-permute-start.12 = (f32[48,128]{1,0:T(8,128)S(1)}, f32[48,128]{1,0:T(8,128)S(1)}, u32[]{:S(2)}, u32[]{:S(2)}) collective-permute-start(f32[48,128]{1,0:T(8,128)S(1)} %get-tuple-element.87), channel_id=1, source_target_pairs={{0,12},{4,0},{8,4},{12,8},{1,13},{5,1},{9,5},{13,9},{2,14},{6,2},{... | collective-permute-start | bytes 73736 | tf_op jit(solution)/shard_map/ppermute | solution.py:458

commit v5 on v4

--- a/solution.py
+++ b/solution.py
@@ -53,6 +53,25 @@
     rows = value.shape[0] * 2 // 3
     tails = jnp.concatenate([value[rows:, :64], value[rows:, 64:]], axis=0)
     return jnp.concatenate([value[:rows], tails], axis=1)
+
+
+def side_by_side(value):
+    rows, columns = value.shape
+    parts = max(128 // columns, 1)
+    size = rows // parts
+    return jnp.concatenate([value[i * size : (i + 1) * size] for i in range(parts)], axis=1)
+
+
+def below_each_other(value, columns):
+    parts = max(128 // columns, 1)
+    return jnp.concatenate(
+        [value[:, i * columns : (i + 1) * columns] for i in range(parts)], axis=0
+    )
+
+
+def side_shape(rows, columns):
+    parts = max(128 // columns, 1)
+    return rows // parts, columns * parts
 
 
 def dense_shape(rows, width):
@@ -92,6 +111,12 @@
 def exact_parts(value):
     top, mid = split(value)
     return top, mid, (value - top.astype(F32) - mid.astype(F32)).astype(BF)
+
+
+def take(value, pick):
+    rows = value.shape[0]
+    taken = dot_bf(jnp.concatenate(exact_parts(value), axis=0), pick)
+    return taken[:rows] + (taken[rows : 2 * rows] + taken[2 * rows :])
 
 
 def outgoing_kernel(
@@ -114,10 +139,9 @@
     index = jnp.concatenate([send_ref[0:1, :], send_ref[1:2, :]], axis=1)
     pick = chosen(index, x_t_ref.shape[1])
     copies[1].wait()
-    top, mid, low = exact_parts(x_t_ref[...])
-    sent = layer_norm((dot_bf(top, pick) + dot_bf(mid, pick) + dot_bf(low, pick)).T)
-    lower_ref[...] = dense(sent[:halos])
-    upper_ref[...] = dense(sent[halos:])
+    sent = layer_norm(take(x_t_ref[...], pick), axis=0)
+    lower_ref[...] = side_by_side(sent[:, :halos])
+    upper_ref[...] = side_by_side(sent[:, halos:])
     for copy in copies[2:]:
         copy.wait()
     index_out_ref[...] = jnp.zeros_like(index_out_ref)
@@ -185,10 +209,11 @@
     head_ref, lower_ref, upper_ref, own_ref, other_ref, pre_t_ref, halo_mat_ref, w_top_ref,
     w_low_ref, w_out_t_ref, top_ref, low_ref, anchor_ref,
 ):
-    width = w_top_ref.shape[1]
+    halos = halo_mat_ref.shape[0] // 2
     halo_t = jnp.concatenate(
-        [undense(lower_ref[...], width), undense(upper_ref[...], width)], axis=0
-    ).T
+        [below_each_other(lower_ref[...], halos), below_each_other(upper_ref[...], halos)],
+        axis=1,
+    )
     halo_agg = dot(halo_t, halo_mat_ref[...])
     pre = pre_t_ref[...] + dot_halves((w_top_ref[...], w_low_ref[...]), split(halo_agg))
     units, rows = pre.shape
@@ -196,7 +221,7 @@
     pick = chosen(every_index(head_ref, own_ref, other_ref), rows)
     anchors = dot_bf(jnp.concatenate(halves, axis=0), pick).astype(BF)
     part = dot_halves(split(w_out_t_ref[...]), (anchors[:units], anchors[units:]))
-    anchor_ref[...] = dense(part.T)
+    anchor_ref[...] = side_by_side(part)
     top_ref[...], low_ref[...] = halves
 
 
@@ -213,10 +238,7 @@
 ):
     part_t_ref[...] = dot_halves(split(w_out_t_ref[...]), (top_ref[...], low_ref[...]))
     pick = chosen(every_index(head_ref, own_ref, other_ref), x_t_ref.shape[1])
-    width = x_t_ref.shape[0]
-    taken = dot_bf(jnp.concatenate(exact_parts(x_t_ref[...]), axis=0), pick)
-    taken = taken[:width] + (taken[width : 2 * width] + taken[2 * width :])
-    anchor_x_ref[...] = taken.T
+    anchor_x_ref[...] = take(x_t_ref[...], pick)
 
 
 def through(w, value_t, front_refs, back_refs, back_scale):
@@ -229,7 +251,7 @@
         halves = split(front)
         backs = split(front.T * back_scale)
         for i in range(2):
-            front_refs[i][h * width : (h + 1) * width, :] = halves[i]
+            front_refs[i][:, h * rows : (h + 1) * rows] = halves[i]
             back_refs[i][h * rows : (h + 1) * rows, :] = backs[i]
 
 
@@ -246,8 +268,8 @@
 
 
 def anchor_kernel(x_ref, part_ref, recv_ref, _, *outs):
-    part = undense(part_ref[...] + recv_ref[...], x_ref.shape[1])
-    feat = dense(layer_norm(x_ref[...] + part))
+    part = below_each_other(part_ref[...] + recv_ref[...], x_ref.shape[1])
+    feat = dense(layer_norm(x_ref[...] + part, axis=0).T)
     for out in outs:
         out[...] = feat
 
@@ -290,66 +312,56 @@
 
 
 def forward(head_ref, feat_ref, u, t, wv, s_ref, v_ref, s_mine_ref, dp_ref):
-    width = feat_ref.shape[1]
     count = feat_ref.shape[0]
-    rows = u[0].shape[1]
+    rows = u[0].shape[1] // HEADS
     mine = dp_ref.shape[0]
     cells = [slice(h * rows, (h + 1) * rows) for h in range(HEADS)]
-    feats = [slice(h * width, (h + 1) * width) for h in range(HEADS)]
 
     def step(start, size, carry):
         at = pl.ds(start, size)
         feat = split(feat_ref[at, :])
-        for h in range(HEADS):
-            s_ref[at, cells[h]] = dot_halves(feat, [half[feats[h], :] for half in u])
+        s_ref[at, :] = dot_halves(feat, halves_of(u))
         v_ref[:, at] = split_heads(dot_halves(wv, split(feat_ref[at, :].T)))
         return carry
 
     over_chunks(count, step, 0)
-    tops, totals, sums = [], [], []
-    for h in range(HEADS):
-
-        def highest(start, size, top, h=h):
-            part = jnp.max(s_ref[pl.ds(start, size), cells[h]], axis=0, keepdims=True)
-            return part if top is None else jnp.maximum(top, part)
-
-        least = None if count <= CHUNK else jnp.full((1, rows), -jnp.inf, F32)
-        tops.append(over_chunks(count, highest, least))
-    for h in range(HEADS):
-
-        def weigh(start, size, state, h=h):
-            total, acc = state
-            at = pl.ds(start, size)
-            expo = jnp.exp2(s_ref[at, cells[h]] - tops[h])
-            top, low = split(expo)
+    place = pl.ds(pl.multiple_of(head_ref[0] * mine, mine), mine)
+    dp_ref[...] = dot_halves(split(feat_ref[place, :]), halves_of(t))
+
+    def highest(start, size, top):
+        part = jnp.max(s_ref[pl.ds(start, size), :], axis=0, keepdims=True)
+        return part if top is None else jnp.maximum(top, part)
+
+    least = None if count <= CHUNK else jnp.full((1, HEADS * rows), -jnp.inf, F32)
+    top = over_chunks(count, highest, least)
+
+    def weigh(start, size, state):
+        total, sums = state
+        at = pl.ds(start, size)
+        expo = jnp.exp2(s_ref[at, :] - top)
+        high, low = split(expo)
+        total = total + jnp.sum(expo, axis=0, keepdims=True)
+        added = []
+        for h in range(HEADS):
             value = v_ref[of_head(h, 2), at]
-            total = total + jnp.sum(expo, axis=0, keepdims=True)
-            both = dot_bf(value, top)
-            return total, acc + (both[:DH] + (both[DH:] + dot_bf(value[:DH], low)))
-
-        start = (jnp.zeros((1, rows), F32), jnp.zeros((DH, rows), F32))
-        total, acc = over_chunks(count, weigh, start)
-        totals.append(total)
-        sums.append(acc)
-    place = pl.ds(pl.multiple_of(head_ref[0] * mine, mine), mine)
+            both = dot_bf(value, high[:, cells[h]])
+            low_part = dot_bf(value[:DH], low[:, cells[h]])
+            added.append(sums[h] + (both[:DH] + (both[DH:] + low_part)))
+        return total, tuple(added)
+
+    start = (
+        jnp.zeros((1, HEADS * rows), F32),
+        tuple(jnp.zeros((DH, rows), F32) for _ in range(HEADS)),
+    )
+    total, sums = over_chunks(count, weigh, start)
     s_mine_ref[...] = s_ref[place, :]
-    feat = split(feat_ref[place, :])
-    for h in range(HEADS):
-        dp_ref[:, cells[h]] = dot_halves(feat, [half[feats[h], :] for half in t])
-    return tops, totals, sums
-
-
-def backward(s_mine_ref, dp_ref, tops, inverses, deltas, u_back, t_back):
-    rows = tops[0].shape[1]
-    probs, d_scores = [], []
-    for h in range(HEADS):
-        cells = slice(h * rows, (h + 1) * rows)
-        prob = jnp.exp2(s_mine_ref[:, cells] - tops[h]) * inverses[h]
-        probs.append(prob)
-        d_scores.append(prob * (dp_ref[:, cells] - deltas[h]))
-    return dot_halves(split(jnp.concatenate(d_scores, axis=1)), u_back) + dot_halves(
-        split(jnp.concatenate(probs, axis=1)), t_back
-    )
+    return top, total, sums
+
+
+def backward(s_mine_ref, dp_ref, top, inverse, delta, u_back, t_back):
+    probs = jnp.exp2(s_mine_ref[...] - top) * inverse
+    d_scores = probs * (dp_ref[...] - delta)
+    return dot_halves(split(d_scores), u_back) + dot_halves(split(probs), t_back)
 
 
 def halves_of(refs):
@@ -360,14 +372,14 @@
     head_ref, feat_ref, u_top_ref, u_low_ref, t_top_ref, t_low_ref, v_top_ref, v_low_ref,
     s_mine_ref, dp_ref, sums_ref, state_ref, s_ref, v_ref,
 ):
-    tops, totals, sums = forward(
+    top, total, sums = forward(
         head_ref, feat_ref, (u_top_ref, u_low_ref), (t_top_ref, t_low_ref),
         halves_of((v_top_ref, v_low_ref)), s_ref, v_ref, s_mine_ref, dp_ref,
     )
     for h in range(HEADS):
         sums_ref[of_head(h, 1), :] = sums[h]
-        state_ref[h : h + 1, :] = tops[h]
-        state_ref[HEADS + h : HEADS + h + 1, :] = totals[h]
+    state_ref[0:1, :] = top
+    state_ref[1:2, :] = total
 
 
 def second_half_kernel(
@@ -375,26 +387,27 @@
     t_low_ref, v_top_ref, v_low_ref, u_back_top_ref, u_back_low_ref, t_back_top_ref,
     t_back_low_ref, att_t_ref, give_ref, out_state_ref, s_ref, v_ref, s_mine_ref, dp_ref,
 ):
-    tops, totals, sums = forward(
+    top, total, sums = forward(
         head_ref, feat_ref, (u_top_ref, u_low_ref), (t_top_ref, t_low_ref),
         halves_of((v_top_ref, v_low_ref)), s_ref, v_ref, s_mine_ref, dp_ref,
     )
-    inverses, deltas = [], []
+    rows = d_t_ref.shape[1]
+    other_top, other_total = state_ref[0:1, :], state_ref[1:2, :]
+    new = jnp.maximum(top, other_top)
+    factor, other = jnp.exp2(top - new), jnp.exp2(other_top - new)
+    inverse = 1.0 / (total * factor + other_total * other)
+    deltas = []
     for h in range(HEADS):
-        other_top = state_ref[h : h + 1, :]
-        other_total = state_ref[HEADS + h : HEADS + h + 1, :]
-        top = jnp.maximum(tops[h], other_top)
-        factor, other = jnp.exp2(tops[h] - top), jnp.exp2(other_top - top)
-        inverse = 1.0 / (totals[h] * factor + other_total * other)
-        att = (sums[h] * factor + sums_ref[of_head(h, 1), :] * other) * inverse
-        att_t_ref[of_head(h, 1), :] = att
-        tops[h] = top
-        inverses.append(inverse)
-        deltas.append(jnp.sum(d_t_ref[of_head(h, 1), :] * att, axis=0, keepdims=True))
-    for i, row in enumerate(tops + inverses + deltas):
+        at, cells = of_head(h, 1), slice(h * rows, (h + 1) * rows)
+        att = sums[h] * factor[:, cells] + sums_ref[at, :] * other[:, cells]
+        att = att * inverse[:, cells]
+        att_t_ref[at, :] = att
+        deltas.append(jnp.sum(d_t_ref[at, :] * att, axis=0, keepdims=True))
+    delta = jnp.concatenate(deltas, axis=1)
+    for i, row in enumerate((new, inverse, delta)):
         out_state_ref[i : i + 1, :] = row
     give_ref[...] = backward(
-        s_mine_ref, dp_ref, tops, inverses, deltas,
+        s_mine_ref, dp_ref, new, inverse, delta,
         halves_of((u_back_top_ref, u_back_low_ref)), halves_of((t_back_top_ref, t_back_low_ref)),
     )
 
@@ -403,9 +416,8 @@
     s_mine_ref, dp_ref, state_ref, u_back_top_ref, u_back_low_ref, t_back_top_ref,
     t_back_low_ref, keep_ref,
 ):
-    rows = [state_ref[i : i + 1, :] for i in range(3 * HEADS)]
     keep_ref[...] = backward(
-        s_mine_ref, dp_ref, rows[:HEADS], rows[HEADS : 2 * HEADS], rows[2 * HEADS :],
+        s_mine_ref, dp_ref, state_ref[0:1, :], state_ref[1:2, :], state_ref[2:3, :],
         halves_of((u_back_top_ref, u_back_low_ref)), halves_of((t_back_top_ref, t_back_low_ref)),
     )
 
@@ -466,7 +478,7 @@
     to_lower, to_upper, index, index_out, faces, x_t, w_in = call(
         outgoing_kernel,
         [
-            dense_shape(halos, width), dense_shape(halos, width), (1, own, I32),
+            side_shape(width, halos), side_shape(width, halos), (1, own, I32),
             (56, 128, I32), (*faces.shape, I32), (width, rows),
             w_in.shape,
         ],
@@ -488,7 +500,7 @@
     )
     top, low, anchor_part = call(
         hidden_kernel,
-        [(units, rows, BF), (units, rows, BF), dense_shape(anchors, width)],
+        [(units, rows, BF), (units, rows, BF), side_shape(width, anchors)],
         [
             head, from_lower, from_upper, index, other_index, pre_t, halo_mat, w_top, w_low,
             w_out_t,
@@ -499,12 +511,12 @@
     anchor_part, anchor_recv = head_sum(anchor_part)
     part, anchor_x = call(
         rest_kernel,
-        [(width, rows), (anchors, width)],
+        [(width, rows), (width, anchors)],
         [head, index, other_index, top, low, w_out_t, x_t],
         smem=(0,),
         flops=10**9,
     )
-    front = [(HEADS * width, rows, BF)] * 2
+    front = [(width, HEADS * rows, BF)] * 2
     back = [(HEADS * rows, width, BF)] * 2
     d_t, v_top, v_low, t_top, t_low, *t_back = call(
         cotangent_kernel,
@@ -533,7 +545,7 @@
     work = [pltpu.VMEM((count, HEADS * rows), F32), pltpu.VMEM((2 * width, count), BF)]
     s_mine, dp, sums, state = call(
         first_half_kernel,
-        [in_mine, in_mine, (width, rows), (8, rows)],
+        [in_mine, in_mine, (width, rows), (8, HEADS * rows)],
         [head, feat_a, *fronts],
         smem=(0,),
         scratch=work,
@@ -541,7 +553,7 @@
     )
     att, give, state = call(
         second_half_kernel,
-        [(width, rows), (mine, width), (16, rows)],
+        [(width, rows), (mine, width), (8, HEADS * rows)],
         [head, sums, state, feat_b, d_t, *fronts, *u_back, *t_back],
         smem=(0,),
         scratch=work + [pltpu.VMEM(in_mine, F32)] * 2,

time: 37.7 us -> 37.5 us (level)
  no operation moved by 1% of the time
where the time goes in v5:
time: 37.5 us; the launch traced here: 37.4 us
  starting transfers between devices  17.6 us (47%)
  Pallas kernels  11.8 us (31%)
  waiting for transfers between devices  6.39 us (17%)
  between operations  1.46 us (4%)
    ppermute x8, starting transfers between devices, along(): lax.ppermute(value, 'dom', [(i, (i + step) % n_dom) for i in range(n_dom)])  13.5 us
    pallas_call x14, Pallas kernels, call(): pl.pallas_call(body, out_shape=[jax.ShapeDtypeStruct(o[:2], o[2] if len(o...  11.8 us
    ppermute x8, waiting for transfers between devices, along(): lax.ppermute(value, 'dom', [(i, (i + step) % n_dom) for i in range(n_dom)])  3.9 us
    ppermute x2, starting transfers between devices, head_sum(): return (part, lax.ppermute(part, 'head', swap))  2.16 us
    ppermute x1, starting transfers between devices, shards(): other_index = lax.ppermute(index_out, 'head', swap)  1.65 us
    ppermute x2, waiting for transfers between devices, head_sum(): return (part, lax.ppermute(part, 'head', swap))  1.13 us
  transfers between devices with their start and end apart: 13, of which 8 were waited for; matrix products, arithmetic and copies ran while one was open for 0% of the time, Pallas kernels for 17%

profile of v5, /device:TPU:0, one launch (start us, length us, event | category | flops | bytes accessed | tf_op | source)
XLA Modules:
  0.0 37.4 jit_solution(16986583617278395524)
XLA Ops:
  0.6 1.4 %shard_map.140 = (f32[48,128]{1,0:T(8,128)S(1)}, f32[48,128]{1,0:T(8,128)S(1)}, s32[1,32]{1,0:T(1,128)S(1)}, s32[56,128]{1,0:T(8,128)S(1)}, s32[3,1536]{1,0:T(4,...) custom-call(s32[2,32]{1,0:T(2,128)} %send_hbm.1, s32[1,32]{1,0:T(1,128)} %bitcast.13, s32[3,1536]{1,0:T(4,128)} %faces_hbm.1, ...), custom_call_target="tpu_custom_call" | custom-call | flops 100000000 | bytes 1000000 | tf_op jit(solution)/shard_map/pallas_call | solution.py:92
  2.1 3.1 %collective-permute-start.1 = (f32[48,128]{1,0:T(8,128)S(1)}, f32[48,128]{1,0:T(8,128)S(1)}, u32[]{:S(2)}, u32[]{:S(2)}) collective-permute-start(f32[48,128]{1,0:T(8,128)S(1)} %get-tuple-element.48), channel_id=1, source_target_pairs={{0,4},{4,8},{8,12},{12,0},{1,5},{5,9},{9,13},{13,1},{2,6},{6,10},{... | collective-permute-start | bytes 73736 | tf_op jit(solution)/shard_map/ppermute | solution.py:470
  5.1 2.1 %collective-permute-start.2 = (f32[48,128]{1,0:T(8,128)S(1)}, f32[48,128]{1,0:T(8,128)S(1)}, u32[]{:S(2)}, u32[]{:S(2)}) collective-permute-start(f32[48,128]{1,0:T(8,128)S(1)} %get-tuple-element.49), channel_id=1, source_target_pairs={{0,12},{4,0},{8,4},{12,8},{1,13},{5,1},{9,5},{13,9},{2,14},{6,2},{... | collective-permute-start | bytes 73736 | tf_op jit(solution)/shard_map/ppermute | solution.py:470
  7.2 1.6 %collective-permute-start = (s32[56,128]{1,0:T(8,128)S(1)}, s32[56,128]{1,0:T(8,128)S(1)}, u32[]{:S(2)}, u32[]{:S(2)}) collective-permute-start(s32[56,128]{1,0:T(8,128)S(1)} %get-tuple-element.47), channel_id=1, source_target_pairs={{0,2},{2,0},{1,3},{3,1},{4,6},{6,4},{5,7},{7,5},{8,10},{10,8},{9,1... | collective-permute-start | bytes 86024 | tf_op jit(solution)/shard_map/ppermute | solution.py:492
  9.6 1.6 %shard_map.141 = (f32[384,256]{1,0:T(8,128)S(1)}, f32[64,256]{1,0:T(8,128)S(1)}, bf16[384,192]{1,0:T(8,128)(2,1)S(1)}, bf16[384,192]{1,0:T(8,128)(2,1)S(1)}) custom-call(s32[1,1]{1,0:T(1,128)} %bitcast.7.live_ref, f32[192,256]{1,0:T(8,128)S(1)} %get-tuple-element.45.x_t_ref, s32[3,1536]{1,0:T(4,128)S(1)} %get-tuple-element.50.faces_ref, ...), custom_call_target="tpu_custom_call" | custom-call | flops 2000000000 | bytes 1000000 | tf_op jit(solution)/shard_map/pallas_call | solution.py:92
  11.2 1.3 %shard_map.142 = (bf16[384,256]{1,0:T(8,128)(2,1)S(1)}, bf16[384,256]{1,0:T(8,128)(2,1)S(1)}, f32[96,128]{1,0:T(8,128)S(1)}) custom-call(s32[1]{0:T(128)} %bitcast.2.head_ref, f32[48,128]{1,0:T(8,128)S(1)} %collective-permute-done.1.lower_ref, f32[48,128]{1,0:T(8,128)S(1)} %collective-permute-done.2.upper_ref, s32[1,32]{1,0:T(1,128)S(1)} %get-tuple-element.46.own_ref, ...), custom_call_target="tpu_custom_call" | custom-call | flops 1000000000 | bytes 1000000 | tf_op jit(solution)/shard_map/pallas_call | solution.py:92
  12.5 1.6 %collective-permute-start.4 = (f32[96,128]{1,0:T(8,128)S(1)}, f32[96,128]{1,0:T(8,128)S(1)}, u32[]{:S(2)}, u32[]{:S(2)}) collective-permute-start(f32[96,128]{1,0:T(8,128)S(1)} %get-tuple-element.61.part_ref), channel_id=1, source_target_pairs={{0,2},{2,0},{1,3},{3,1},{4,6},{6,4},{5,7},{7,5},{8,10},{10,8},{9,1... | collective-permute-start | bytes 147464 | tf_op jit(solution)/shard_map/ppermute | solution.py:474
  15.2 0.8 %shard_map.145 = (f32[192,256]{1,0:T(8,128)S(1)}, bf16[192,192]{1,0:T(8,128)(2,1)S(1)}, bf16[192,192]{1,0:T(8,128)(2,1)S(1)}, bf16[192,768]{1,0:T(8,128)(2,1)S(1...) custom-call(f32[192,256]{1,0:T(8,128)S(1)} %bitcast.10, ...), custom_call_target="tpu_custom_call" | custom-call | flops 1000000000 | bytes 1000000 | tf_op jit(solution)/shard_map/pallas_call | solution.py:92
  16.0 1.1 %collective-permute-done.4.recv_ref = f32[96,128]{1,0:T(8,128)S(1)} collective-permute-done((f32[96,128]{1,0:T(8,128)S(1)}, f32[96,128]{1,0:T(8,128)S(1)}, u32[]{:S(2)}, u32[]{:S(2)}) %collective-permute-start.4) | collective-permute-done | bytes 49184 | tf_op jit(solution)/shard_map/ppermute | solution.py:474
  17.5 2.4 %collective-permute-start.6 = (f32[96,128]{1,0:T(8,128)S(1)}, f32[96,128]{1,0:T(8,128)S(1)}, u32[]{:S(2)}, u32[]{:S(2)}) collective-permute-start(f32[96,128]{1,0:T(8,128)S(1)} %get-tuple-element.65), channel_id=1, source_target_pairs={{0,8},{4,12},{8,0},{12,4},{1,9},{5,13},{9,1},{13,5},{2,10},{6,14},... | collective-permute-start | bytes 147464 | tf_op jit(solution)/shard_map/ppermute | solution.py:470
  19.9 1.4 %collective-permute-start.7 = (f32[96,128]{1,0:T(8,128)S(1)}, f32[96,128]{1,0:T(8,128)S(1)}, u32[]{:S(2)}, u32[]{:S(2)}) collective-permute-start(f32[96,128]{1,0:T(8,128)S(1)} %get-tuple-element.66), channel_id=1, source_target_pairs={{0,12},{4,0},{8,4},{12,8},{1,13},{5,1},{9,5},{13,9},{2,14},{6,2},{... | collective-permute-start | bytes 147464 | tf_op jit(solution)/shard_map/ppermute | solution.py:470
  21.4 0.9 %shard_map.144 = (f32[192,256]{1,0:T(8,128)S(1)}, bf16[192,768]{1,0:T(8,128)(2,1)S(1)}, bf16[192,768]{1,0:T(8,128)(2,1)S(1)}, bf16[768,192]{1,0:T(8,128)(2,1)S(1)}, bf16[768,192]{1,0:T(8,128)(2,1)S(1)}) custom-call(f32[192,256]{1,0:T(8,128)S(1)} %get-tuple-element.45.x_t_ref, f32[192,256]{1,0:T(8,128)S(1)} %get-tuple-element.58.part_ref, ...), custom_call_target="tpu_custom_call" | custom-call | flops 1000000000 | bytes 1000000 | tf_op jit(solution)/shard_map/pallas_call | solution.py:92
  22.3 1.1 %collective-permute-done.5.refs_1_ = f32[96,128]{1,0:T(8,128)S(1)} collective-permute-done((f32[96,128]{1,0:T(8,128)S(1)}, f32[96,128]{1,0:T(8,128)S(1)}, u32[]{:S(2)}, u32[]{:S(2)}) %collective-permute-start.5) | collective-permute-done | bytes 49184 | tf_op jit(solution)/shard_map/ppermute | solution.py:470
  24.2 0.9 %shard_map.148 = (f32[128,768]{1,0:T(8,128)S(1)}, f32[128,768]{1,0:T(8,128)S(1)}, f32[192,256]{1,0:T(8,128)S(1)}, f32[8,768]{1,0:T(8,128)S(1)}) custom-call(s32[1]{0:T(128)} %bitcast.2.head_ref, f32[256,192]{1,0:T(8,128)S(1)} %shard_map.147.feat_ref, bf16[192,768]{1,0:T(8,128)(2,1)S(1)} %get-tuple-element.67.u_top_ref, ...), custom_call_target="tpu_custom_call" | custom-call | flops 2000000000 | bytes 1000000 | tf_op jit(solution)/shard_map/pallas_call | solution.py:92
  25.1 0.7 %collective-permute-done.8.feat_ref = f32[256,192]{1,0:T(8,128)S(1)} collective-permute-done((f32[256,192]{1,0:T(8,128)S(1)}, f32[256,192]{1,0:T(8,128)S(1)}, u32[]{:S(2)}, u32[]{:S(2)}) %collective-permute-start.8) | collective-permute-done | bytes 196640 | tf_op jit(solution)/shard_map/ppermute | solution.py:543
  25.7 1.8 %shard_map.149 = (f32[192,256]{1,0:T(8,128)S(1)}, f32[128,192]{1,0:T(8,128)S(1)}, f32[8,768]{1,0:T(8,128)S(1)}) custom-call(s32[1]{0:T(128)} %bitcast.2.head_ref, f32[192,256]{1,0:T(8,128)S(1)} %get-tuple-element.73.sums_ref, f32[8,768]{1,0:T(8,128)S(1)} %get-tuple-element.74.state_ref, f32[256,192]{1,0:T(8,128)S(1)} %collective-permute-done.8.feat_ref, ...), custom_call_target="tpu_custom_call" | custom-call | flops 2000000000 | bytes 1000000 | tf_op jit(solution)/shard_map/pallas_call | solution.py:92
  28.2 0.7 %collective-permute-done.9.recv_ref = f32[128,192]{1,0:T(8,128)S(1)} collective-permute-done((f32[128,192]{1,0:T(8,128)S(1)}, f32[128,192]{1,0:T(8,128)S(1)}, u32[]{:S(2)}, u32[]{:S(2)}) %collective-permute-start.9) | collective-permute-done | bytes 98336 | tf_op jit(solution)/shard_map/ppermute | solution.py:562
  29.0 2.0 %collective-permute-start.10 = (f32[48,128]{1,0:T(8,128)S(1)}, f32[48,128]{1,0:T(8,128)S(1)}, u32[]{:S(2)}, u32[]{:S(2)}) collective-permute-start(f32[48,128]{1,0:T(8,128)S(1)} %get-tuple-element.85), channel_id=1, source_target_pairs={{0,4},{4,8},{8,12},{12,0},{1,5},{5,9},{9,13},{13,1},{2,6},{6,10},{... | collective-permute-start | bytes 73736 | tf_op jit(solution)/shard_map/ppermute | solution.py:470
  31.1 1.8 %collective-permute-start.11 = (f32[48,128]{1,0:T(8,128)S(1)}, f32[48,128]{1,0:T(8,128)S(1)}, u32[]{:S(2)}, u32[]{:S(2)}) collective-permute-start(f32[48,128]{1,0:T(8,128)S(1)} %get-tuple-element.86), channel_id=1, source_target_pairs={{0,8},{4,12},{8,0},{12,4},{1,9},{5,13},{9,1},{13,5},{2,10},{6,14},... | collective-permute-start | bytes 73736 | tf_op jit(solution)/shard_map/ppermute | solution.py:470
  32.9 0.6 %collective-permute-start.12 = (f32[48,128]{1,0:T(8,128)S(1)}, f32[48,128]{1,0:T(8,128)S(1)}, u32[]{:S(2)}, u32[]{:S(2)}) collective-permute-start(f32[48,128]{1,0:T(8,128)S(1)} %get-tuple-element.87), channel_id=1, source_target_pairs={{0,12},{4,0},{8,4},{12,8},{1,13},{5,1},{9,5},{13,9},{2,14},{6,2},{... | collective-permute-start | bytes 73736 | tf_op jit(solution)/shard_map/ppermute | solution.py:470
  33.5 1.0 %shard_map.150 = f32[192,256]{1,0:T(8,128)} custom-call(f32[192,256]{1,0:T(8,128)S(1)} %get-tuple-element.59._.mixed_t_ref, f32[192,256]{1,0:T(8,128)S(1)} %get-tuple-element.79.att_t_ref, f32[192,192]{1,0:T(8,128)S(1)} %copy-done), custom_call_target="tpu_custom_call" | custom-call | flops 100000000 | bytes 1000000 | tf_op jit(solution)/shard_map/pallas_call | solution.py:92
  34.8 1.1 %collective-permute-done.11.refs_2_ = f32[48,128]{1,0:T(8,128)S(1)} collective-permute-done((f32[48,128]{1,0:T(8,128)S(1)}, f32[48,128]{1,0:T(8,128)S(1)}, u32[]{:S(2)}, u32[]{:S(2)}) %collective-permute-start.11) | collective-permute-done | bytes 24608 | tf_op jit(solution)/shard_map/ppermute | solution.py:470
  35.8 0.9 %collective-permute-done.12.refs_3_ = f32[48,128]{1,0:T(8,128)S(1)} collective-permute-done((f32[48,128]{1,0:T(8,128)S(1)}, f32[48,128]{1,0:T(8,128)S(1)}, u32[]{:S(2)}, u32[]{:S(2)}) %collective-permute-start.12) | collective-permute-done | bytes 24608 | tf_op jit(solution)/shard_map/ppermute | solution.py:470
  36.7 0.7 %shard_map.153 = f32[32,192]{1,0:T(8,128)} custom-call(f32[48,128]{1,0:T(8,128)S(1)} %get-tuple-element.84.refs_0_, f32[48,128]{1,0:T(8,128)S(1)} %collective-permute-done.10.refs_1_, f32[48,128]{1,0:T(8,128)S(1)} %collective-permute-done.11.refs_2_, f32[48,128]{1,0:T(8,128)S(1)} %collective-permute-done.12.refs_3_), custom_call_target="tpu_custom_call" | custom-call | flops 100000000 | bytes 1000000 | tf_op jit(solution)/shard_map/pallas_call | solution.py:92
  (31 shorter events, 3.3 us)
Async XLA Ops:
  0.6 8.9 %copy-start.6 = (f32[1536]{0:T(1024)S(1)}, f32[1536]{0:T(1024)}, u32[]{:S(2)}) copy-start(f32[1536]{0:T(1024)} %param.14) | copy-start | bytes 18436
  2.1 9.1 %collective-permute-start.1 = (f32[48,128]{1,0:T(8,128)S(1)}, f32[48,128]{1,0:T(8,128)S(1)}, u32[]{:S(2)}, u32[]{:S(2)}) collective-permute-start(f32[48,128]{1,0:T(8,128)S(1)} %get-tuple-element.48), channel_id=1, source_target_pairs={{0,4},{4,8},{8,12},{12,0},{1,5},{5,9},{9,13},{13,1},{2,6},{6,10},{... | collective-permute-start | bytes 73736 | tf_op jit(solution)/shard_map/ppermute | solution.py:470
  5.1 6.0 %collective-permute-start.2 = (f32[48,128]{1,0:T(8,128)S(1)}, f32[48,128]{1,0:T(8,128)S(1)}, u32[]{:S(2)}, u32[]{:S(2)}) collective-permute-start(f32[48,128]{1,0:T(8,128)S(1)} %get-tuple-element.49), channel_id=1, source_target_pairs={{0,12},{4,0},{8,4},{12,8},{1,13},{5,1},{9,5},{13,9},{2,14},{6,2},{... | collective-permute-start | bytes 73736 | tf_op jit(solution)/shard_map/ppermute | solution.py:470
  7.2 4.0 %collective-permute-start = (s32[56,128]{1,0:T(8,128)S(1)}, s32[56,128]{1,0:T(8,128)S(1)}, u32[]{:S(2)}, u32[]{:S(2)}) collective-permute-start(s32[56,128]{1,0:T(8,128)S(1)} %get-tuple-element.47), channel_id=1, source_target_pairs={{0,2},{2,0},{1,3},{3,1},{4,6},{6,4},{5,7},{7,5},{8,10},{10,8},{9,1... | collective-permute-start | bytes 86024 | tf_op jit(solution)/shard_map/ppermute | solution.py:492
  9.5 1.6 %copy-start.1 = (f32[384,192]{0,1:T(8,128)S(1)}, f32[384,192]{0,1:T(8,128)}, u32[]{:S(2)}) copy-start(f32[384,192]{0,1:T(8,128)} %param.20) | copy-start | bytes 884740
  12.5 4.7 %collective-permute-start.4 = (f32[96,128]{1,0:T(8,128)S(1)}, f32[96,128]{1,0:T(8,128)S(1)}, u32[]{:S(2)}, u32[]{:S(2)}) collective-permute-start(f32[96,128]{1,0:T(8,128)S(1)} %get-tuple-element.61.part_ref), channel_id=1, source_target_pairs={{0,2},{2,0},{1,3},{3,1},{4,6},{6,4},{5,7},{7,5},{8,10},{10,8},{9,1... | collective-permute-start | bytes 147464 | tf_op jit(solution)/shard_map/ppermute | solution.py:474
  14.1 1.0 %copy-start = (f32[192,192]{1,0:T(8,128)S(1)}, f32[192,192]{1,0:T(8,128)}, u32[]{:S(2)}) copy-start(f32[192,192]{1,0:T(8,128)} %w_ref.5) | copy-start | bytes 442372
  14.1 1.0 %copy-start.2 = (f32[256,192]{0,1:T(8,128)S(1)}, f32[256,192]{0,1:T(8,128)}, u32[]{:S(2)}) copy-start(f32[256,192]{0,1:T(8,128)} %param.25) | copy-start | bytes 589828
  14.1 1.1 %copy-start.3 = (f32[192,192]{1,0:T(8,128)S(1)}, f32[192,192]{1,0:T(8,128)}, u32[]{:S(2)}) copy-start(f32[192,192]{1,0:T(8,128)} %wv_ref.1) | copy-start | bytes 442372
  14.5 6.9 %collective-permute-start.3 = (f32[192,256]{1,0:T(8,128)S(1)}, f32[192,256]{1,0:T(8,128)S(1)}, u32[]{:S(2)}, u32[]{:S(2)}) collective-permute-start(f32[192,256]{1,0:T(8,128)S(1)} %get-tuple-element.58.part_ref), channel_id=1, source_target_pairs={{0,2},{2,0},{1,3},{3,1},{4,6},{6,4},{5,7},{7,5},{8,10},{10,8},{9,1... | collective-permute-start | bytes 589832 | tf_op jit(solution)/shard_map/ppermute | solution.py:474
  17.2 4.2 %copy-start.4 = (f32[192,192]{1,0:T(8,128)S(1)}, f32[192,192]{1,0:T(8,128)}, u32[]{:S(2)}) copy-start(f32[192,192]{1,0:T(8,128)} %w_ref.3) | copy-start | bytes 442372
  17.2 4.2 %copy-start.5 = (f32[192,192]{1,0:T(8,128)S(1)}, f32[192,192]{1,0:T(8,128)}, u32[]{:S(2)}) copy-start(f32[192,192]{1,0:T(8,128)} %wk_ref.1) | copy-start | bytes 442372
  17.5 5.9 %collective-permute-start.5 = (f32[96,128]{1,0:T(8,128)S(1)}, f32[96,128]{1,0:T(8,128)S(1)}, u32[]{:S(2)}, u32[]{:S(2)}) collective-permute-start(f32[96,128]{1,0:T(8,128)S(1)} %get-tuple-element.64), channel_id=1, source_target_pairs={{0,4},{4,8},{8,12},{12,0},{1,5},{5,9},{9,13},{13,1},{2,6},{6,10},{... | collective-permute-start | bytes 147464 | tf_op jit(solution)/shard_map/ppermute | solution.py:470
  17.5 5.9 %collective-permute-start.6 = (f32[96,128]{1,0:T(8,128)S(1)}, f32[96,128]{1,0:T(8,128)S(1)}, u32[]{:S(2)}, u32[]{:S(2)}) collective-permute-start(f32[96,128]{1,0:T(8,128)S(1)} %get-tuple-element.65), channel_id=1, source_target_pairs={{0,8},{4,12},{8,0},{12,4},{1,9},{5,13},{9,1},{13,5},{2,10},{6,14},... | collective-permute-start | bytes 147464 | tf_op jit(solution)/shard_map/ppermute | solution.py:470
  19.9 4.1 %collective-permute-start.7 = (f32[96,128]{1,0:T(8,128)S(1)}, f32[96,128]{1,0:T(8,128)S(1)}, u32[]{:S(2)}, u32[]{:S(2)}) collective-permute-start(f32[96,128]{1,0:T(8,128)S(1)} %get-tuple-element.66), channel_id=1, source_target_pairs={{0,12},{4,0},{8,4},{12,8},{1,13},{5,1},{9,5},{13,9},{2,14},{6,2},{... | collective-permute-start | bytes 147464 | tf_op jit(solution)/shard_map/ppermute | solution.py:470
  24.1 1.6 %collective-permute-start.8 = (f32[256,192]{1,0:T(8,128)S(1)}, f32[256,192]{1,0:T(8,128)S(1)}, u32[]{:S(2)}, u32[]{:S(2)}) collective-permute-start(f32[256,192]{1,0:T(8,128)S(1)} %shard_map.147.feat_ref), channel_id=1, source_target_pairs={{0,1},{1,0},{2,3},{3,2},{4,5},{5,4},{6,7},{7,6},{8,9},{9,8},{10,11... | collective-permute-start | bytes 589832 | tf_op jit(solution)/shard_map/ppermute | solution.py:543
  27.5 1.4 %collective-permute-start.9 = (f32[128,192]{1,0:T(8,128)S(1)}, f32[128,192]{1,0:T(8,128)S(1)}, u32[]{:S(2)}, u32[]{:S(2)}) collective-permute-start(f32[128,192]{1,0:T(8,128)S(1)} %get-tuple-element.83), channel_id=1, source_target_pairs={{0,1},{1,0},{2,3},{3,2},{4,5},{5,4},{6,7},{7,6},{8,9},{9,8},{10,11... | collective-permute-start | bytes 294920 | tf_op jit(solution)/shard_map/ppermute | solution.py:562
  29.0 5.7 %collective-permute-start.10 = (f32[48,128]{1,0:T(8,128)S(1)}, f32[48,128]{1,0:T(8,128)S(1)}, u32[]{:S(2)}, u32[]{:S(2)}) collective-permute-start(f32[48,128]{1,0:T(8,128)S(1)} %get-tuple-element.85), channel_id=1, source_target_pairs={{0,4},{4,8},{8,12},{12,0},{1,5},{5,9},{9,13},{13,1},{2,6},{6,10},{... | collective-permute-start | bytes 73736 | tf_op jit(solution)/shard_map/ppermute | solution.py:470
  31.1 4.8 %collective-permute-start.11 = (f32[48,128]{1,0:T(8,128)S(1)}, f32[48,128]{1,0:T(8,128)S(1)}, u32[]{:S(2)}, u32[]{:S(2)}) collective-permute-start(f32[48,128]{1,0:T(8,128)S(1)} %get-tuple-element.86), channel_id=1, source_target_pairs={{0,8},{4,12},{8,0},{12,4},{1,9},{5,13},{9,1},{13,5},{2,10},{6,14},... | collective-permute-start | bytes 73736 | tf_op jit(solution)/shard_map/ppermute | solution.py:470
  32.9 3.8 %collective-permute-start.12 = (f32[48,128]{1,0:T(8,128)S(1)}, f32[48,128]{1,0:T(8,128)S(1)}, u32[]{:S(2)}, u32[]{:S(2)}) collective-permute-start(f32[48,128]{1,0:T(8,128)S(1)} %get-tuple-element.87), channel_id=1, source_target_pairs={{0,12},{4,0},{8,4},{12,8},{1,13},{5,1},{9,5},{13,9},{2,14},{6,2},{... | collective-permute-start | bytes 73736 | tf_op jit(solution)/shard_map/ppermute | solution.py:470

commit v6 on v5

--- a/solution.py
+++ b/solution.py
@@ -216,11 +216,11 @@
     )
     halo_agg = dot(halo_t, halo_mat_ref[...])
     pre = pre_t_ref[...] + dot_halves((w_top_ref[...], w_low_ref[...]), split(halo_agg))
-    units, rows = pre.shape
+    rows = pre.shape[1]
     halves = split(0.5 * pre * (1.0 + lax.erf(pre * math.sqrt(0.5))))
     pick = chosen(every_index(head_ref, own_ref, other_ref), rows)
-    anchors = dot_bf(jnp.concatenate(halves, axis=0), pick).astype(BF)
-    part = dot_halves(split(w_out_t_ref[...]), (anchors[:units], anchors[units:]))
+    anchors = [dot_bf(half, pick).astype(BF) for half in halves]
+    part = dot_halves(split(w_out_t_ref[...]), anchors)
     anchor_ref[...] = side_by_side(part)
     top_ref[...], low_ref[...] = halves
 
@@ -364,6 +364,12 @@
     return dot_halves(split(d_scores), u_back) + dot_halves(split(probs), t_back)
 
 
+def put_blocks(own, value, out):
+    size = dense_shape(own, value.shape[1])[0]
+    for i in range(value.shape[0] // own):
+        out[i * size : (i + 1) * size, :] = dense(value[i * own : (i + 1) * own])
+
+
 def halves_of(refs):
     return [ref[...] for ref in refs]
 
@@ -383,7 +389,7 @@
 
 
 def second_half_kernel(
-    head_ref, sums_ref, state_ref, feat_ref, d_t_ref, u_top_ref, u_low_ref, t_top_ref,
+    own, head_ref, sums_ref, state_ref, feat_ref, d_t_ref, u_top_ref, u_low_ref, t_top_ref,
     t_low_ref, v_top_ref, v_low_ref, u_back_top_ref, u_back_low_ref, t_back_top_ref,
     t_back_low_ref, att_t_ref, give_ref, out_state_ref, s_ref, v_ref, s_mine_ref, dp_ref,
 ):
@@ -406,26 +412,28 @@
     delta = jnp.concatenate(deltas, axis=1)
     for i, row in enumerate((new, inverse, delta)):
         out_state_ref[i : i + 1, :] = row
-    give_ref[...] = backward(
+    grad = backward(
         s_mine_ref, dp_ref, new, inverse, delta,
         halves_of((u_back_top_ref, u_back_low_ref)), halves_of((t_back_top_ref, t_back_low_ref)),
     )
+    put_blocks(own, grad, give_ref)
 
 
 def keep_kernel(
-    s_mine_ref, dp_ref, state_ref, u_back_top_ref, u_back_low_ref, t_back_top_ref,
+    own, s_mine_ref, dp_ref, state_ref, u_back_top_ref, u_back_low_ref, t_back_top_ref,
     t_back_low_ref, keep_ref,
 ):
-    keep_ref[...] = backward(
+    grad = backward(
         s_mine_ref, dp_ref, state_ref[0:1, :], state_ref[1:2, :], state_ref[2:3, :],
         halves_of((u_back_top_ref, u_back_low_ref)), halves_of((t_back_top_ref, t_back_low_ref)),
     )
-
-
-def add_kernel(own, keep_ref, recv_ref, *outs):
+    put_blocks(own, grad, keep_ref)
+
+
+def add_kernel(keep_ref, recv_ref, *outs):
     for i, out in enumerate(outs):
-        rows = pl.ds(i * own, own)
-        out[...] = dense(keep_ref[rows, :] + recv_ref[rows, :])
+        rows = pl.ds(i * out.shape[0], out.shape[0])
+        out[...] = keep_ref[rows, :] + recv_ref[rows, :]
 
 
 def output_kernel(mixed_t_ref, att_t_ref, w_ref, out_t_ref):
@@ -552,8 +560,8 @@
         flops=2 * 10**9,
     )
     att, give, state = call(
-        second_half_kernel,
-        [(width, rows), (mine, width), (8, HEADS * rows)],
+        functools.partial(second_half_kernel, own),
+        [(width, rows), dense_shape(mine, width), (8, HEADS * rows)],
         [head, sums, state, feat_b, d_t, *fronts, *u_back, *t_back],
         smem=(0,),
         scratch=work + [pltpu.VMEM(in_mine, F32)] * 2,
@@ -561,13 +569,13 @@
     )
     recv = lax.ppermute(give, "aux", swap)
     (keep,) = call(
-        keep_kernel,
-        [(mine, width)],
+        functools.partial(keep_kernel, own),
+        [dense_shape(mine, width)],
         [s_mine, dp, state, *u_back, *t_back],
         flops=10**9,
     )
     sums = call(
-        functools.partial(add_kernel, own), [dense_shape(own, width)] * n_dom, [keep, recv]
+        add_kernel, [dense_shape(own, width)] * n_dom, [keep, recv]
     )
     sums = [sums[0]] + [along(sums[s], n_dom - s) for s in reversed(range(1, n_dom))]
     (output_t,) = call(output_kernel, [(width, rows)], [mixed, att, w_attn_out])

time: 37.5 us -> 37.5 us (level)
  no operation moved by 1% of the time
where the time goes in v6:
time: 37.5 us; the launch traced here: 37.3 us
  starting transfers between devices  17.6 us (47%)
  Pallas kernels  11.8 us (31%)
  waiting for transfers between devices  6.29 us (17%)
  between operations  1.45 us (4%)
    ppermute x8, starting transfers between devices, along(): lax.ppermute(value, 'dom', [(i, (i + step) % n_dom) for i in range(n_dom)])  13.5 us
    pallas_call x14, Pallas kernels, call(): pl.pallas_call(body, out_shape=[jax.ShapeDtypeStruct(o[:2], o[2] if len(o...  11.8 us
    ppermute x8, waiting for transfers between devices, along(): lax.ppermute(value, 'dom', [(i, (i + step) % n_dom) for i in range(n_dom)])  3.9 us
    ppermute x2, starting transfers between devices, head_sum(): return (part, lax.ppermute(part, 'head', swap))  2.16 us
    ppermute x1, starting transfers between devices, shards(): other_index = lax.ppermute(index_out, 'head', swap)  1.65 us
    ppermute x2, waiting for transfers between devices, head_sum(): return (part, lax.ppermute(part, 'head', swap))  1.13 us
  transfers between devices with their start and end apart: 13, of which 8 were waited for; matrix products, arithmetic and copies ran while one was open for 0% of the time, Pallas kernels for 17%

profile of v6, /device:TPU:0, one launch (start us, length us, event | category | flops | bytes accessed | tf_op | source)
XLA Modules:
  0.0 37.3 jit_solution(2921551729783692497)
XLA Ops:
  0.6 1.4 %shard_map.140 = (f32[48,128]{1,0:T(8,128)S(1)}, f32[48,128]{1,0:T(8,128)S(1)}, s32[1,32]{1,0:T(1,128)S(1)}, s32[56,128]{1,0:T(8,128)S(1)}, s32[3,1536]{1,0:T(4,...) custom-call(s32[2,32]{1,0:T(2,128)} %send_hbm.1, s32[1,32]{1,0:T(1,128)} %bitcast.13, s32[3,1536]{1,0:T(4,128)} %faces_hbm.1, ...), custom_call_target="tpu_custom_call" | custom-call | flops 100000000 | bytes 1000000 | tf_op jit(solution)/shard_map/pallas_call | solution.py:92
  2.1 3.1 %collective-permute-start.1 = (f32[48,128]{1,0:T(8,128)S(1)}, f32[48,128]{1,0:T(8,128)S(1)}, u32[]{:S(2)}, u32[]{:S(2)}) collective-permute-start(f32[48,128]{1,0:T(8,128)S(1)} %get-tuple-element.48), channel_id=1, source_target_pairs={{0,4},{4,8},{8,12},{12,0},{1,5},{5,9},{9,13},{13,1},{2,6},{6,10},{... | collective-permute-start | bytes 73736 | tf_op jit(solution)/shard_map/ppermute | solution.py:478
  5.1 2.1 %collective-permute-start.2 = (f32[48,128]{1,0:T(8,128)S(1)}, f32[48,128]{1,0:T(8,128)S(1)}, u32[]{:S(2)}, u32[]{:S(2)}) collective-permute-start(f32[48,128]{1,0:T(8,128)S(1)} %get-tuple-element.49), channel_id=1, source_target_pairs={{0,12},{4,0},{8,4},{12,8},{1,13},{5,1},{9,5},{13,9},{2,14},{6,2},{... | collective-permute-start | bytes 73736 | tf_op jit(solution)/shard_map/ppermute | solution.py:478
  7.2 1.6 %collective-permute-start = (s32[56,128]{1,0:T(8,128)S(1)}, s32[56,128]{1,0:T(8,128)S(1)}, u32[]{:S(2)}, u32[]{:S(2)}) collective-permute-start(s32[56,128]{1,0:T(8,128)S(1)} %get-tuple-element.47), channel_id=1, source_target_pairs={{0,2},{2,0},{1,3},{3,1},{4,6},{6,4},{5,7},{7,5},{8,10},{10,8},{9,1... | collective-permute-start | bytes 86024 | tf_op jit(solution)/shard_map/ppermute | solution.py:500
  9.6 1.6 %shard_map.141 = (f32[384,256]{1,0:T(8,128)S(1)}, f32[64,256]{1,0:T(8,128)S(1)}, bf16[384,192]{1,0:T(8,128)(2,1)S(1)}, bf16[384,192]{1,0:T(8,128)(2,1)S(1)}) custom-call(s32[1,1]{1,0:T(1,128)} %bitcast.7.live_ref, f32[192,256]{1,0:T(8,128)S(1)} %get-tuple-element.45.x_t_ref, s32[3,1536]{1,0:T(4,128)S(1)} %get-tuple-element.50.faces_ref, ...), custom_call_target="tpu_custom_call" | custom-call | flops 2000000000 | bytes 1000000 | tf_op jit(solution)/shard_map/pallas_call | solution.py:92
  11.2 1.3 %shard_map.142 = (bf16[384,256]{1,0:T(8,128)(2,1)S(1)}, bf16[384,256]{1,0:T(8,128)(2,1)S(1)}, f32[96,128]{1,0:T(8,128)S(1)}) custom-call(s32[1]{0:T(128)} %bitcast.2.head_ref, f32[48,128]{1,0:T(8,128)S(1)} %collective-permute-done.1.lower_ref, f32[48,128]{1,0:T(8,128)S(1)} %collective-permute-done.2.upper_ref, s32[1,32]{1,0:T(1,128)S(1)} %get-tuple-element.46.own_ref, ...), custom_call_target="tpu_custom_call" | custom-call | flops 1000000000 | bytes 1000000 | tf_op jit(solution)/shard_map/pallas_call | solution.py:92
  12.5 1.6 %collective-permute-start.4 = (f32[96,128]{1,0:T(8,128)S(1)}, f32[96,128]{1,0:T(8,128)S(1)}, u32[]{:S(2)}, u32[]{:S(2)}) collective-permute-start(f32[96,128]{1,0:T(8,128)S(1)} %get-tuple-element.61.part_ref), channel_id=1, source_target_pairs={{0,2},{2,0},{1,3},{3,1},{4,6},{6,4},{5,7},{7,5},{8,10},{10,8},{9,1... | collective-permute-start | bytes 147464 | tf_op jit(solution)/shard_map/ppermute | solution.py:482
  15.2 0.8 %shard_map.145 = (f32[192,256]{1,0:T(8,128)S(1)}, bf16[192,192]{1,0:T(8,128)(2,1)S(1)}, bf16[192,192]{1,0:T(8,128)(2,1)S(1)}, bf16[192,768]{1,0:T(8,128)(2,1)S(1...) custom-call(f32[192,256]{1,0:T(8,128)S(1)} %bitcast.10, ...), custom_call_target="tpu_custom_call" | custom-call | flops 1000000000 | bytes 1000000 | tf_op jit(solution)/shard_map/pallas_call | solution.py:92
  16.0 1.1 %collective-permute-done.4.recv_ref = f32[96,128]{1,0:T(8,128)S(1)} collective-permute-done((f32[96,128]{1,0:T(8,128)S(1)}, f32[96,128]{1,0:T(8,128)S(1)}, u32[]{:S(2)}, u32[]{:S(2)}) %collective-permute-start.4) | collective-permute-done | bytes 49184 | tf_op jit(solution)/shard_map/ppermute | solution.py:482
  17.6 2.4 %collective-permute-start.6 = (f32[96,128]{1,0:T(8,128)S(1)}, f32[96,128]{1,0:T(8,128)S(1)}, u32[]{:S(2)}, u32[]{:S(2)}) collective-permute-start(f32[96,128]{1,0:T(8,128)S(1)} %get-tuple-element.65), channel_id=1, source_target_pairs={{0,8},{4,12},{8,0},{12,4},{1,9},{5,13},{9,1},{13,5},{2,10},{6,14},... | collective-permute-start | bytes 147464 | tf_op jit(solution)/shard_map/ppermute | solution.py:478
  19.9 1.4 %collective-permute-start.7 = (f32[96,128]{1,0:T(8,128)S(1)}, f32[96,128]{1,0:T(8,128)S(1)}, u32[]{:S(2)}, u32[]{:S(2)}) collective-permute-start(f32[96,128]{1,0:T(8,128)S(1)} %get-tuple-element.66), channel_id=1, source_target_pairs={{0,12},{4,0},{8,4},{12,8},{1,13},{5,1},{9,5},{13,9},{2,14},{6,2},{... | collective-permute-start | bytes 147464 | tf_op jit(solution)/shard_map/ppermute | solution.py:478
  21.4 0.9 %shard_map.144 = (f32[192,256]{1,0:T(8,128)S(1)}, bf16[192,768]{1,0:T(8,128)(2,1)S(1)}, bf16[192,768]{1,0:T(8,128)(2,1)S(1)}, bf16[768,192]{1,0:T(8,128)(2,1)S(1)}, bf16[768,192]{1,0:T(8,128)(2,1)S(1)}) custom-call(f32[192,256]{1,0:T(8,128)S(1)} %get-tuple-element.45.x_t_ref, f32[192,256]{1,0:T(8,128)S(1)} %get-tuple-element.58.part_ref, ...), custom_call_target="tpu_custom_call" | custom-call | flops 1000000000 | bytes 1000000 | tf_op jit(solution)/shard_map/pallas_call | solution.py:92
  22.3 1.1 %collective-permute-done.5.refs_1_ = f32[96,128]{1,0:T(8,128)S(1)} collective-permute-done((f32[96,128]{1,0:T(8,128)S(1)}, f32[96,128]{1,0:T(8,128)S(1)}, u32[]{:S(2)}, u32[]{:S(2)}) %collective-permute-start.5) | collective-permute-done | bytes 49184 | tf_op jit(solution)/shard_map/ppermute | solution.py:478
  24.2 0.9 %shard_map.148 = (f32[128,768]{1,0:T(8,128)S(1)}, f32[128,768]{1,0:T(8,128)S(1)}, f32[192,256]{1,0:T(8,128)S(1)}, f32[8,768]{1,0:T(8,128)S(1)}) custom-call(s32[1]{0:T(128)} %bitcast.2.head_ref, f32[256,192]{1,0:T(8,128)S(1)} %shard_map.147.feat_ref, bf16[192,768]{1,0:T(8,128)(2,1)S(1)} %get-tuple-element.67.u_top_ref, ...), custom_call_target="tpu_custom_call" | custom-call | flops 2000000000 | bytes 1000000 | tf_op jit(solution)/shard_map/pallas_call | solution.py:92
  25.1 0.7 %collective-permute-done.8.feat_ref = f32[256,192]{1,0:T(8,128)S(1)} collective-permute-done((f32[256,192]{1,0:T(8,128)S(1)}, f32[256,192]{1,0:T(8,128)S(1)}, u32[]{:S(2)}, u32[]{:S(2)}) %collective-permute-start.8) | collective-permute-done | bytes 196640 | tf_op jit(solution)/shard_map/ppermute | solution.py:551
  25.7 1.9 %shard_map.149 = (f32[192,256]{1,0:T(8,128)S(1)}, f32[192,128]{1,0:T(8,128)S(1)}, f32[8,768]{1,0:T(8,128)S(1)}) custom-call(s32[1]{0:T(128)} %bitcast.2.head_ref, f32[192,256]{1,0:T(8,128)S(1)} %get-tuple-element.73.sums_ref, f32[8,768]{1,0:T(8,128)S(1)} %get-tuple-element.74.state_ref, f32[256,192]{1,0:T(8,128)S(1)} %collective-permute-done.8.feat_ref, ...), custom_call_target="tpu_custom_call" | custom-call | flops 2000000000 | bytes 1000000 | tf_op jit(solution)/shard_map/pallas_call | solution.py:92
  28.4 0.6 %collective-permute-done.9.recv_ref = f32[192,128]{1,0:T(8,128)S(1)} collective-permute-done((f32[192,128]{1,0:T(8,128)S(1)}, f32[192,128]{1,0:T(8,128)S(1)}, u32[]{:S(2)}, u32[]{:S(2)}) %collective-permute-start.9) | collective-permute-done | bytes 98336 | tf_op jit(solution)/shard_map/ppermute | solution.py:570
  29.0 2.1 %collective-permute-start.10 = (f32[48,128]{1,0:T(8,128)S(1)}, f32[48,128]{1,0:T(8,128)S(1)}, u32[]{:S(2)}, u32[]{:S(2)}) collective-permute-start(f32[48,128]{1,0:T(8,128)S(1)} %get-tuple-element.85), channel_id=1, source_target_pairs={{0,4},{4,8},{8,12},{12,0},{1,5},{5,9},{9,13},{13,1},{2,6},{6,10},{... | collective-permute-start | bytes 73736 | tf_op jit(solution)/shard_map/ppermute | solution.py:478
  31.0 1.8 %collective-permute-start.11 = (f32[48,128]{1,0:T(8,128)S(1)}, f32[48,128]{1,0:T(8,128)S(1)}, u32[]{:S(2)}, u32[]{:S(2)}) collective-permute-start(f32[48,128]{1,0:T(8,128)S(1)} %get-tuple-element.86), channel_id=1, source_target_pairs={{0,8},{4,12},{8,0},{12,4},{1,9},{5,13},{9,1},{13,5},{2,10},{6,14},... | collective-permute-start | bytes 73736 | tf_op jit(solution)/shard_map/ppermute | solution.py:478
  32.8 0.6 %collective-permute-start.12 = (f32[48,128]{1,0:T(8,128)S(1)}, f32[48,128]{1,0:T(8,128)S(1)}, u32[]{:S(2)}, u32[]{:S(2)}) collective-permute-start(f32[48,128]{1,0:T(8,128)S(1)} %get-tuple-element.87), channel_id=1, source_target_pairs={{0,12},{4,0},{8,4},{12,8},{1,13},{5,1},{9,5},{13,9},{2,14},{6,2},{... | collective-permute-start | bytes 73736 | tf_op jit(solution)/shard_map/ppermute | solution.py:478
  33.5 1.0 %shard_map.150 = f32[192,256]{1,0:T(8,128)} custom-call(f32[192,256]{1,0:T(8,128)S(1)} %get-tuple-element.59._.mixed_t_ref, f32[192,256]{1,0:T(8,128)S(1)} %get-tuple-element.79.att_t_ref, f32[192,192]{1,0:T(8,128)S(1)} %copy-done), custom_call_target="tpu_custom_call" | custom-call | flops 100000000 | bytes 1000000 | tf_op jit(solution)/shard_map/pallas_call | solution.py:92
  34.7 1.0 %collective-permute-done.11.refs_2_ = f32[48,128]{1,0:T(8,128)S(1)} collective-permute-done((f32[48,128]{1,0:T(8,128)S(1)}, f32[48,128]{1,0:T(8,128)S(1)}, u32[]{:S(2)}, u32[]{:S(2)}) %collective-permute-start.11) | collective-permute-done | bytes 24608 | tf_op jit(solution)/shard_map/ppermute | solution.py:478
  35.8 0.9 %collective-permute-done.12.refs_3_ = f32[48,128]{1,0:T(8,128)S(1)} collective-permute-done((f32[48,128]{1,0:T(8,128)S(1)}, f32[48,128]{1,0:T(8,128)S(1)}, u32[]{:S(2)}, u32[]{:S(2)}) %collective-permute-start.12) | collective-permute-done | bytes 24608 | tf_op jit(solution)/shard_map/ppermute | solution.py:478
  36.6 0.7 %shard_map.153 = f32[32,192]{1,0:T(8,128)} custom-call(f32[48,128]{1,0:T(8,128)S(1)} %get-tuple-element.84.refs_0_, f32[48,128]{1,0:T(8,128)S(1)} %collective-permute-done.10.refs_1_, f32[48,128]{1,0:T(8,128)S(1)} %collective-permute-done.11.refs_2_, f32[48,128]{1,0:T(8,128)S(1)} %collective-permute-done.12.refs_3_), custom_call_target="tpu_custom_call" | custom-call | flops 100000000 | bytes 1000000 | tf_op jit(solution)/shard_map/pallas_call | solution.py:92
  (31 shorter events, 3.3 us)
Async XLA Ops:
  0.6 8.9 %copy-start.6 = (f32[1536]{0:T(1024)S(1)}, f32[1536]{0:T(1024)}, u32[]{:S(2)}) copy-start(f32[1536]{0:T(1024)} %param.14) | copy-start | bytes 18436
  2.1 9.1 %collective-permute-start.1 = (f32[48,128]{1,0:T(8,128)S(1)}, f32[48,128]{1,0:T(8,128)S(1)}, u32[]{:S(2)}, u32[]{:S(2)}) collective-permute-start(f32[48,128]{1,0:T(8,128)S(1)} %get-tuple-element.48), channel_id=1, source_target_pairs={{0,4},{4,8},{8,12},{12,0},{1,5},{5,9},{9,13},{13,1},{2,6},{6,10},{... | collective-permute-start | bytes 73736 | tf_op jit(solution)/shard_map/ppermute | solution.py:478
  5.1 6.0 %collective-permute-start.2 = (f32[48,128]{1,0:T(8,128)S(1)}, f32[48,128]{1,0:T(8,128)S(1)}, u32[]{:S(2)}, u32[]{:S(2)}) collective-permute-start(f32[48,128]{1,0:T(8,128)S(1)} %get-tuple-element.49), channel_id=1, source_target_pairs={{0,12},{4,0},{8,4},{12,8},{1,13},{5,1},{9,5},{13,9},{2,14},{6,2},{... | collective-permute-start | bytes 73736 | tf_op jit(solution)/shard_map/ppermute | solution.py:478
  7.2 4.0 %collective-permute-start = (s32[56,128]{1,0:T(8,128)S(1)}, s32[56,128]{1,0:T(8,128)S(1)}, u32[]{:S(2)}, u32[]{:S(2)}) collective-permute-start(s32[56,128]{1,0:T(8,128)S(1)} %get-tuple-element.47), channel_id=1, source_target_pairs={{0,2},{2,0},{1,3},{3,1},{4,6},{6,4},{5,7},{7,5},{8,10},{10,8},{9,1... | collective-permute-start | bytes 86024 | tf_op jit(solution)/shard_map/ppermute | solution.py:500
  9.5 1.6 %copy-start.1 = (f32[384,192]{0,1:T(8,128)S(1)}, f32[384,192]{0,1:T(8,128)}, u32[]{:S(2)}) copy-start(f32[384,192]{0,1:T(8,128)} %param.20) | copy-start | bytes 884740
  12.5 4.7 %collective-permute-start.4 = (f32[96,128]{1,0:T(8,128)S(1)}, f32[96,128]{1,0:T(8,128)S(1)}, u32[]{:S(2)}, u32[]{:S(2)}) collective-permute-start(f32[96,128]{1,0:T(8,128)S(1)} %get-tuple-element.61.part_ref), channel_id=1, source_target_pairs={{0,2},{2,0},{1,3},{3,1},{4,6},{6,4},{5,7},{7,5},{8,10},{10,8},{9,1... | collective-permute-start | bytes 147464 | tf_op jit(solution)/shard_map/ppermute | solution.py:482
  14.1 1.0 %copy-start = (f32[192,192]{1,0:T(8,128)S(1)}, f32[192,192]{1,0:T(8,128)}, u32[]{:S(2)}) copy-start(f32[192,192]{1,0:T(8,128)} %w_ref.5) | copy-start | bytes 442372
  14.1 1.0 %copy-start.2 = (f32[256,192]{0,1:T(8,128)S(1)}, f32[256,192]{0,1:T(8,128)}, u32[]{:S(2)}) copy-start(f32[256,192]{0,1:T(8,128)} %param.25) | copy-start | bytes 589828
  14.1 1.1 %copy-start.3 = (f32[192,192]{1,0:T(8,128)S(1)}, f32[192,192]{1,0:T(8,128)}, u32[]{:S(2)}) copy-start(f32[192,192]{1,0:T(8,128)} %wv_ref.1) | copy-start | bytes 442372
  14.5 6.9 %collective-permute-start.3 = (f32[192,256]{1,0:T(8,128)S(1)}, f32[192,256]{1,0:T(8,128)S(1)}, u32[]{:S(2)}, u32[]{:S(2)}) collective-permute-start(f32[192,256]{1,0:T(8,128)S(1)} %get-tuple-element.58.part_ref), channel_id=1, source_target_pairs={{0,2},{2,0},{1,3},{3,1},{4,6},{6,4},{5,7},{7,5},{8,10},{10,8},{9,1... | collective-permute-start | bytes 589832 | tf_op jit(solution)/shard_map/ppermute | solution.py:482
  17.2 4.2 %copy-start.4 = (f32[192,192]{1,0:T(8,128)S(1)}, f32[192,192]{1,0:T(8,128)}, u32[]{:S(2)}) copy-start(f32[192,192]{1,0:T(8,128)} %w_ref.3) | copy-start | bytes 442372
  17.2 4.2 %copy-start.5 = (f32[192,192]{1,0:T(8,128)S(1)}, f32[192,192]{1,0:T(8,128)}, u32[]{:S(2)}) copy-start(f32[192,192]{1,0:T(8,128)} %wk_ref.1) | copy-start | bytes 442372
  17.5 5.9 %collective-permute-start.5 = (f32[96,128]{1,0:T(8,128)S(1)}, f32[96,128]{1,0:T(8,128)S(1)}, u32[]{:S(2)}, u32[]{:S(2)}) collective-permute-start(f32[96,128]{1,0:T(8,128)S(1)} %get-tuple-element.64), channel_id=1, source_target_pairs={{0,4},{4,8},{8,12},{12,0},{1,5},{5,9},{9,13},{13,1},{2,6},{6,10},{... | collective-permute-start | bytes 147464 | tf_op jit(solution)/shard_map/ppermute | solution.py:478
  17.6 5.9 %collective-permute-start.6 = (f32[96,128]{1,0:T(8,128)S(1)}, f32[96,128]{1,0:T(8,128)S(1)}, u32[]{:S(2)}, u32[]{:S(2)}) collective-permute-start(f32[96,128]{1,0:T(8,128)S(1)} %get-tuple-element.65), channel_id=1, source_target_pairs={{0,8},{4,12},{8,0},{12,4},{1,9},{5,13},{9,1},{13,5},{2,10},{6,14},... | collective-permute-start | bytes 147464 | tf_op jit(solution)/shard_map/ppermute | solution.py:478
  19.9 4.1 %collective-permute-start.7 = (f32[96,128]{1,0:T(8,128)S(1)}, f32[96,128]{1,0:T(8,128)S(1)}, u32[]{:S(2)}, u32[]{:S(2)}) collective-permute-start(f32[96,128]{1,0:T(8,128)S(1)} %get-tuple-element.66), channel_id=1, source_target_pairs={{0,12},{4,0},{8,4},{12,8},{1,13},{5,1},{9,5},{13,9},{2,14},{6,2},{... | collective-permute-start | bytes 147464 | tf_op jit(solution)/shard_map/ppermute | solution.py:478
  24.1 1.6 %collective-permute-start.8 = (f32[256,192]{1,0:T(8,128)S(1)}, f32[256,192]{1,0:T(8,128)S(1)}, u32[]{:S(2)}, u32[]{:S(2)}) collective-permute-start(f32[256,192]{1,0:T(8,128)S(1)} %shard_map.147.feat_ref), channel_id=1, source_target_pairs={{0,1},{1,0},{2,3},{3,2},{4,5},{5,4},{6,7},{7,6},{8,9},{9,8},{10,11... | collective-permute-start | bytes 589832 | tf_op jit(solution)/shard_map/ppermute | solution.py:551
  27.6 1.4 %collective-permute-start.9 = (f32[192,128]{1,0:T(8,128)S(1)}, f32[192,128]{1,0:T(8,128)S(1)}, u32[]{:S(2)}, u32[]{:S(2)}) collective-permute-start(f32[192,128]{1,0:T(8,128)S(1)} %get-tuple-element.83), channel_id=1, source_target_pairs={{0,1},{1,0},{2,3},{3,2},{4,5},{5,4},{6,7},{7,6},{8,9},{9,8},{10,11... | collective-permute-start | bytes 294920 | tf_op jit(solution)/shard_map/ppermute | solution.py:570
  29.0 5.8 %collective-permute-start.10 = (f32[48,128]{1,0:T(8,128)S(1)}, f32[48,128]{1,0:T(8,128)S(1)}, u32[]{:S(2)}, u32[]{:S(2)}) collective-permute-start(f32[48,128]{1,0:T(8,128)S(1)} %get-tuple-element.85), channel_id=1, source_target_pairs={{0,4},{4,8},{8,12},{12,0},{1,5},{5,9},{9,13},{13,1},{2,6},{6,10},{... | collective-permute-start | bytes 73736 | tf_op jit(solution)/shard_map/ppermute | solution.py:478
  31.0 4.8 %collective-permute-start.11 = (f32[48,128]{1,0:T(8,128)S(1)}, f32[48,128]{1,0:T(8,128)S(1)}, u32[]{:S(2)}, u32[]{:S(2)}) collective-permute-start(f32[48,128]{1,0:T(8,128)S(1)} %get-tuple-element.86), channel_id=1, source_target_pairs={{0,8},{4,12},{8,0},{12,4},{1,9},{5,13},{9,1},{13,5},{2,10},{6,14},... | collective-permute-start | bytes 73736 | tf_op jit(solution)/shard_map/ppermute | solution.py:478
  32.8 3.8 %collective-permute-start.12 = (f32[48,128]{1,0:T(8,128)S(1)}, f32[48,128]{1,0:T(8,128)S(1)}, u32[]{:S(2)}, u32[]{:S(2)}) collective-permute-start(f32[48,128]{1,0:T(8,128)S(1)} %get-tuple-element.87), channel_id=1, source_target_pairs={{0,12},{4,0},{8,4},{12,8},{1,13},{5,1},{9,5},{13,9},{2,14},{6,2},{... | collective-permute-start | bytes 73736 | tf_op jit(solution)/shard_map/ppermute | solution.py:478

commit v7 on v6

--- a/solution.py
+++ b/solution.py
@@ -287,12 +287,13 @@
 
 
 def join_kernel(own, _, *refs):
-    out = refs[-1]
-    blocks = len(refs) - 1
-    for i, ref in enumerate(refs[:-1]):
+    out, message = refs[-2:]
+    blocks = len(refs) - 2
+    for i, ref in enumerate(refs[:-2]):
         value = undense(ref[...], out.shape[1])
         for place in range(value.shape[0] // own):
             out[pl.ds((place * blocks + i) * own, own), :] = value[place * own : (place + 1) * own]
+    message[...] = dense(out[...])
 
 
 CHUNK = 512
@@ -389,10 +390,12 @@
 
 
 def second_half_kernel(
-    own, head_ref, sums_ref, state_ref, feat_ref, d_t_ref, u_top_ref, u_low_ref, t_top_ref,
+    own, head_ref, sums_ref, state_ref, message_ref, d_t_ref, u_top_ref, u_low_ref, t_top_ref,
     t_low_ref, v_top_ref, v_low_ref, u_back_top_ref, u_back_low_ref, t_back_top_ref,
     t_back_low_ref, att_t_ref, give_ref, out_state_ref, s_ref, v_ref, s_mine_ref, dp_ref,
-):
+    feat_ref,
+):
+    feat_ref[...] = undense(message_ref[...], feat_ref.shape[1])
     top, total, sums = forward(
         head_ref, feat_ref, (u_top_ref, u_low_ref), (t_top_ref, t_low_ref),
         halves_of((v_top_ref, v_low_ref)), s_ref, v_ref, s_mine_ref, dp_ref,
@@ -547,8 +550,12 @@
         flops=10**9,
     )
     fronts = [u_top, u_low, t_top, t_low, v_top, v_low]
-    (feat_a,) = call(functools.partial(join_kernel, own), [(count, width)], [mixed] + feats)
-    feat_b = lax.ppermute(feat_a, "aux", swap)
+    feat_a, feat_b = call(
+        functools.partial(join_kernel, own),
+        [(count, width), dense_shape(count, width)],
+        [mixed] + feats,
+    )
+    feat_b = lax.ppermute(feat_b, "aux", swap)
     in_mine = (mine, HEADS * rows)
     work = [pltpu.VMEM((count, HEADS * rows), F32), pltpu.VMEM((2 * width, count), BF)]
     s_mine, dp, sums, state = call(
@@ -564,7 +571,7 @@
         [(width, rows), dense_shape(mine, width), (8, HEADS * rows)],
         [head, sums, state, feat_b, d_t, *fronts, *u_back, *t_back],
         smem=(0,),
-        scratch=work + [pltpu.VMEM(in_mine, F32)] * 2,
+        scratch=work + [pltpu.VMEM(in_mine, F32)] * 2 + [pltpu.VMEM((count, width), F32)],
         flops=2 * 10**9,
     )
     recv = lax.ppermute(give, "aux", swap)

time: 37.5 us -> 37.5 us (level)
  no operation moved by 1% of the time
where the time goes in v7:
time: 37.5 us; the launch traced here: 37.3 us
  starting transfers between devices  17.6 us (47%)
  Pallas kernels  11.9 us (32%)
  waiting for transfers between devices  6.21 us (17%)
  between operations  1.45 us (4%)
    ppermute x8, starting transfers between devices, along(): lax.ppermute(value, 'dom', [(i, (i + step) % n_dom) for i in range(n_dom)])  13.5 us
    pallas_call x14, Pallas kernels, call(): pl.pallas_call(body, out_shape=[jax.ShapeDtypeStruct(o[:2], o[2] if len(o...  11.9 us
    ppermute x8, waiting for transfers between devices, along(): lax.ppermute(value, 'dom', [(i, (i + step) % n_dom) for i in range(n_dom)])  3.91 us
    ppermute x2, starting transfers between devices, head_sum(): return (part, lax.ppermute(part, 'head', swap))  2.16 us
    ppermute x1, starting transfers between devices, shards(): other_index = lax.ppermute(index_out, 'head', swap)  1.65 us
    ppermute x2, waiting for transfers between devices, head_sum(): return (part, lax.ppermute(part, 'head', swap))  1.13 us
  transfers between devices with their start and end apart: 13, of which 8 were waited for; matrix products, arithmetic and copies ran while one was open for 0% of the time, Pallas kernels for 17%

profile of v7, /device:TPU:0, one launch (start us, length us, event | category | flops | bytes accessed | tf_op | source)
XLA Modules:
  0.0 37.3 jit_solution(4804067384211989768)
XLA Ops:
  0.6 1.4 %shard_map.140 = (f32[48,128]{1,0:T(8,128)S(1)}, f32[48,128]{1,0:T(8,128)S(1)}, s32[1,32]{1,0:T(1,128)S(1)}, s32[56,128]{1,0:T(8,128)S(1)}, s32[3,1536]{1,0:T(4,...) custom-call(s32[2,32]{1,0:T(2,128)} %send_hbm.1, s32[1,32]{1,0:T(1,128)} %bitcast.13, s32[3,1536]{1,0:T(4,128)} %faces_hbm.1, ...), custom_call_target="tpu_custom_call" | custom-call | flops 100000000 | bytes 1000000 | tf_op jit(solution)/shard_map/pallas_call | solution.py:92
  2.1 3.1 %collective-permute-start.1 = (f32[48,128]{1,0:T(8,128)S(1)}, f32[48,128]{1,0:T(8,128)S(1)}, u32[]{:S(2)}, u32[]{:S(2)}) collective-permute-start(f32[48,128]{1,0:T(8,128)S(1)} %get-tuple-element.50), channel_id=1, source_target_pairs={{0,4},{4,8},{8,12},{12,0},{1,5},{5,9},{9,13},{13,1},{2,6},{6,10},{... | collective-permute-start | bytes 73736 | tf_op jit(solution)/shard_map/ppermute | solution.py:481
  5.1 2.1 %collective-permute-start.2 = (f32[48,128]{1,0:T(8,128)S(1)}, f32[48,128]{1,0:T(8,128)S(1)}, u32[]{:S(2)}, u32[]{:S(2)}) collective-permute-start(f32[48,128]{1,0:T(8,128)S(1)} %get-tuple-element.51), channel_id=1, source_target_pairs={{0,12},{4,0},{8,4},{12,8},{1,13},{5,1},{9,5},{13,9},{2,14},{6,2},{... | collective-permute-start | bytes 73736 | tf_op jit(solution)/shard_map/ppermute | solution.py:481
  7.2 1.6 %collective-permute-start = (s32[56,128]{1,0:T(8,128)S(1)}, s32[56,128]{1,0:T(8,128)S(1)}, u32[]{:S(2)}, u32[]{:S(2)}) collective-permute-start(s32[56,128]{1,0:T(8,128)S(1)} %get-tuple-element.49), channel_id=1, source_target_pairs={{0,2},{2,0},{1,3},{3,1},{4,6},{6,4},{5,7},{7,5},{8,10},{10,8},{9,1... | collective-permute-start | bytes 86024 | tf_op jit(solution)/shard_map/ppermute | solution.py:503
  9.6 1.6 %shard_map.141 = (f32[384,256]{1,0:T(8,128)S(1)}, f32[64,256]{1,0:T(8,128)S(1)}, bf16[384,192]{1,0:T(8,128)(2,1)S(1)}, bf16[384,192]{1,0:T(8,128)(2,1)S(1)}) custom-call(s32[1,1]{1,0:T(1,128)} %bitcast.7.live_ref, f32[192,256]{1,0:T(8,128)S(1)} %get-tuple-element.47.x_t_ref, s32[3,1536]{1,0:T(4,128)S(1)} %get-tuple-element.52.faces_ref, ...), custom_call_target="tpu_custom_call" | custom-call | flops 2000000000 | bytes 1000000 | tf_op jit(solution)/shard_map/pallas_call | solution.py:92
  11.2 1.3 %shard_map.142 = (bf16[384,256]{1,0:T(8,128)(2,1)S(1)}, bf16[384,256]{1,0:T(8,128)(2,1)S(1)}, f32[96,128]{1,0:T(8,128)S(1)}) custom-call(s32[1]{0:T(128)} %bitcast.2.head_ref, f32[48,128]{1,0:T(8,128)S(1)} %collective-permute-done.1.lower_ref, f32[48,128]{1,0:T(8,128)S(1)} %collective-permute-done.2.upper_ref, s32[1,32]{1,0:T(1,128)S(1)} %get-tuple-element.48.own_ref, ...), custom_call_target="tpu_custom_call" | custom-call | flops 1000000000 | bytes 1000000 | tf_op jit(solution)/shard_map/pallas_call | solution.py:92
  12.5 1.6 %collective-permute-start.4 = (f32[96,128]{1,0:T(8,128)S(1)}, f32[96,128]{1,0:T(8,128)S(1)}, u32[]{:S(2)}, u32[]{:S(2)}) collective-permute-start(f32[96,128]{1,0:T(8,128)S(1)} %get-tuple-element.63.part_ref), channel_id=1, source_target_pairs={{0,2},{2,0},{1,3},{3,1},{4,6},{6,4},{5,7},{7,5},{8,10},{10,8},{9,1... | collective-permute-start | bytes 147464 | tf_op jit(solution)/shard_map/ppermute | solution.py:485
  15.2 0.8 %shard_map.145 = (f32[192,256]{1,0:T(8,128)S(1)}, bf16[192,192]{1,0:T(8,128)(2,1)S(1)}, bf16[192,192]{1,0:T(8,128)(2,1)S(1)}, bf16[192,768]{1,0:T(8,128)(2,1)S(1...) custom-call(f32[192,256]{1,0:T(8,128)S(1)} %bitcast.10, ...), custom_call_target="tpu_custom_call" | custom-call | flops 1000000000 | bytes 1000000 | tf_op jit(solution)/shard_map/pallas_call | solution.py:92
  16.0 1.1 %collective-permute-done.4.recv_ref = f32[96,128]{1,0:T(8,128)S(1)} collective-permute-done((f32[96,128]{1,0:T(8,128)S(1)}, f32[96,128]{1,0:T(8,128)S(1)}, u32[]{:S(2)}, u32[]{:S(2)}) %collective-permute-start.4) | collective-permute-done | bytes 49184 | tf_op jit(solution)/shard_map/ppermute | solution.py:485
  17.6 2.4 %collective-permute-start.6 = (f32[96,128]{1,0:T(8,128)S(1)}, f32[96,128]{1,0:T(8,128)S(1)}, u32[]{:S(2)}, u32[]{:S(2)}) collective-permute-start(f32[96,128]{1,0:T(8,128)S(1)} %get-tuple-element.67), channel_id=1, source_target_pairs={{0,8},{4,12},{8,0},{12,4},{1,9},{5,13},{9,1},{13,5},{2,10},{6,14},... | collective-permute-start | bytes 147464 | tf_op jit(solution)/shard_map/ppermute | solution.py:481
  19.9 1.4 %collective-permute-start.7 = (f32[96,128]{1,0:T(8,128)S(1)}, f32[96,128]{1,0:T(8,128)S(1)}, u32[]{:S(2)}, u32[]{:S(2)}) collective-permute-start(f32[96,128]{1,0:T(8,128)S(1)} %get-tuple-element.68), channel_id=1, source_target_pairs={{0,12},{4,0},{8,4},{12,8},{1,13},{5,1},{9,5},{13,9},{2,14},{6,2},{... | collective-permute-start | bytes 147464 | tf_op jit(solution)/shard_map/ppermute | solution.py:481
  21.4 0.9 %shard_map.144 = (f32[192,256]{1,0:T(8,128)S(1)}, bf16[192,768]{1,0:T(8,128)(2,1)S(1)}, bf16[192,768]{1,0:T(8,128)(2,1)S(1)}, bf16[768,192]{1,0:T(8,128)(2,1)S(1)}, bf16[768,192]{1,0:T(8,128)(2,1)S(1)}) custom-call(f32[192,256]{1,0:T(8,128)S(1)} %get-tuple-element.47.x_t_ref, f32[192,256]{1,0:T(8,128)S(1)} %get-tuple-element.60.part_ref, ...), custom_call_target="tpu_custom_call" | custom-call | flops 1000000000 | bytes 1000000 | tf_op jit(solution)/shard_map/pallas_call | solution.py:92
  22.3 1.1 %collective-permute-done.5.refs_1_ = f32[96,128]{1,0:T(8,128)S(1)} collective-permute-done((f32[96,128]{1,0:T(8,128)S(1)}, f32[96,128]{1,0:T(8,128)S(1)}, u32[]{:S(2)}, u32[]{:S(2)}) %collective-permute-start.5) | collective-permute-done | bytes 49184 | tf_op jit(solution)/shard_map/ppermute | solution.py:481
  23.4 0.6 %collective-permute-done.7.refs_3_ = f32[96,128]{1,0:T(8,128)S(1)} collective-permute-done((f32[96,128]{1,0:T(8,128)S(1)}, f32[96,128]{1,0:T(8,128)S(1)}, u32[]{:S(2)}, u32[]{:S(2)}) %collective-permute-start.7) | collective-permute-done | bytes 49184 | tf_op jit(solution)/shard_map/ppermute | solution.py:481
  24.3 0.8 %shard_map.148 = (f32[128,768]{1,0:T(8,128)S(1)}, f32[128,768]{1,0:T(8,128)S(1)}, f32[192,256]{1,0:T(8,128)S(1)}, f32[8,768]{1,0:T(8,128)S(1)}) custom-call(s32[1]{0:T(128)} %bitcast.2.head_ref, f32[256,192]{1,0:T(8,128)S(1)} %get-tuple-element.69.feat_ref, bf16[192,768]{1,0:T(8,128)(2,1)S(1)} %get-tuple-element.70.u_top_ref, ...), custom_call_target="tpu_custom_call" | custom-call | flops 2000000000 | bytes 1000000 | tf_op jit(solution)/shard_map/pallas_call | solution.py:92
  25.7 1.9 %shard_map.149 = (f32[192,256]{1,0:T(8,128)S(1)}, f32[192,128]{1,0:T(8,128)S(1)}, f32[8,768]{1,0:T(8,128)S(1)}) custom-call(s32[1]{0:T(128)} %bitcast.2.head_ref, f32[192,256]{1,0:T(8,128)S(1)} %get-tuple-element.76.sums_ref, f32[8,768]{1,0:T(8,128)S(1)} %get-tuple-element.77.state_ref, f32[384,128]{1,0:T(8,128)S(1)} %collective-permute-done.8.message_ref, ...), custom_call_target="tpu_custom_call" | custom-call | flops 2000000000 | bytes 1000000 | tf_op jit(solution)/shard_map/pallas_call | solution.py:92
  28.4 0.6 %collective-permute-done.9.recv_ref = f32[192,128]{1,0:T(8,128)S(1)} collective-permute-done((f32[192,128]{1,0:T(8,128)S(1)}, f32[192,128]{1,0:T(8,128)S(1)}, u32[]{:S(2)}, u32[]{:S(2)}) %collective-permute-start.9) | collective-permute-done | bytes 98336 | tf_op jit(solution)/shard_map/ppermute | solution.py:577
  29.0 2.1 %collective-permute-start.10 = (f32[48,128]{1,0:T(8,128)S(1)}, f32[48,128]{1,0:T(8,128)S(1)}, u32[]{:S(2)}, u32[]{:S(2)}) collective-permute-start(f32[48,128]{1,0:T(8,128)S(1)} %get-tuple-element.89), channel_id=1, source_target_pairs={{0,4},{4,8},{8,12},{12,0},{1,5},{5,9},{9,13},{13,1},{2,6},{6,10},{... | collective-permute-start | bytes 73736 | tf_op jit(solution)/shard_map/ppermute | solution.py:481
  31.0 1.8 %collective-permute-start.11 = (f32[48,128]{1,0:T(8,128)S(1)}, f32[48,128]{1,0:T(8,128)S(1)}, u32[]{:S(2)}, u32[]{:S(2)}) collective-permute-start(f32[48,128]{1,0:T(8,128)S(1)} %get-tuple-element.90), channel_id=1, source_target_pairs={{0,8},{4,12},{8,0},{12,4},{1,9},{5,13},{9,1},{13,5},{2,10},{6,14},... | collective-permute-start | bytes 73736 | tf_op jit(solution)/shard_map/ppermute | solution.py:481
  32.8 0.6 %collective-permute-start.12 = (f32[48,128]{1,0:T(8,128)S(1)}, f32[48,128]{1,0:T(8,128)S(1)}, u32[]{:S(2)}, u32[]{:S(2)}) collective-permute-start(f32[48,128]{1,0:T(8,128)S(1)} %get-tuple-element.91), channel_id=1, source_target_pairs={{0,12},{4,0},{8,4},{12,8},{1,13},{5,1},{9,5},{13,9},{2,14},{6,2},{... | collective-permute-start | bytes 73736 | tf_op jit(solution)/shard_map/ppermute | solution.py:481
  33.5 1.0 %shard_map.150 = f32[192,256]{1,0:T(8,128)} custom-call(f32[192,256]{1,0:T(8,128)S(1)} %get-tuple-element.61._.mixed_t_ref, f32[192,256]{1,0:T(8,128)S(1)} %get-tuple-element.83.att_t_ref, f32[192,192]{1,0:T(8,128)S(1)} %copy-done), custom_call_target="tpu_custom_call" | custom-call | flops 100000000 | bytes 1000000 | tf_op jit(solution)/shard_map/pallas_call | solution.py:92
  34.7 1.0 %collective-permute-done.11.refs_2_ = f32[48,128]{1,0:T(8,128)S(1)} collective-permute-done((f32[48,128]{1,0:T(8,128)S(1)}, f32[48,128]{1,0:T(8,128)S(1)}, u32[]{:S(2)}, u32[]{:S(2)}) %collective-permute-start.11) | collective-permute-done | bytes 24608 | tf_op jit(solution)/shard_map/ppermute | solution.py:481
  35.8 0.9 %collective-permute-done.12.refs_3_ = f32[48,128]{1,0:T(8,128)S(1)} collective-permute-done((f32[48,128]{1,0:T(8,128)S(1)}, f32[48,128]{1,0:T(8,128)S(1)}, u32[]{:S(2)}, u32[]{:S(2)}) %collective-permute-start.12) | collective-permute-done | bytes 24608 | tf_op jit(solution)/shard_map/ppermute | solution.py:481
  36.7 0.7 %shard_map.153 = f32[32,192]{1,0:T(8,128)} custom-call(f32[48,128]{1,0:T(8,128)S(1)} %get-tuple-element.88.refs_0_, f32[48,128]{1,0:T(8,128)S(1)} %collective-permute-done.10.refs_1_, f32[48,128]{1,0:T(8,128)S(1)} %collective-permute-done.11.refs_2_, f32[48,128]{1,0:T(8,128)S(1)} %collective-permute-done.12.refs_3_), custom_call_target="tpu_custom_call" | custom-call | flops 100000000 | bytes 1000000 | tf_op jit(solution)/shard_map/pallas_call | solution.py:92
  (31 shorter events, 3.4 us)
Async XLA Ops:
  0.6 8.9 %copy-start.6 = (f32[1536]{0:T(1024)S(1)}, f32[1536]{0:T(1024)}, u32[]{:S(2)}) copy-start(f32[1536]{0:T(1024)} %param.14) | copy-start | bytes 18436
  2.1 9.1 %collective-permute-start.1 = (f32[48,128]{1,0:T(8,128)S(1)}, f32[48,128]{1,0:T(8,128)S(1)}, u32[]{:S(2)}, u32[]{:S(2)}) collective-permute-start(f32[48,128]{1,0:T(8,128)S(1)} %get-tuple-element.50), channel_id=1, source_target_pairs={{0,4},{4,8},{8,12},{12,0},{1,5},{5,9},{9,13},{13,1},{2,6},{6,10},{... | collective-permute-start | bytes 73736 | tf_op jit(solution)/shard_map/ppermute | solution.py:481
  5.1 6.0 %collective-permute-start.2 = (f32[48,128]{1,0:T(8,128)S(1)}, f32[48,128]{1,0:T(8,128)S(1)}, u32[]{:S(2)}, u32[]{:S(2)}) collective-permute-start(f32[48,128]{1,0:T(8,128)S(1)} %get-tuple-element.51), channel_id=1, source_target_pairs={{0,12},{4,0},{8,4},{12,8},{1,13},{5,1},{9,5},{13,9},{2,14},{6,2},{... | collective-permute-start | bytes 73736 | tf_op jit(solution)/shard_map/ppermute | solution.py:481
  7.2 4.0 %collective-permute-start = (s32[56,128]{1,0:T(8,128)S(1)}, s32[56,128]{1,0:T(8,128)S(1)}, u32[]{:S(2)}, u32[]{:S(2)}) collective-permute-start(s32[56,128]{1,0:T(8,128)S(1)} %get-tuple-element.49), channel_id=1, source_target_pairs={{0,2},{2,0},{1,3},{3,1},{4,6},{6,4},{5,7},{7,5},{8,10},{10,8},{9,1... | collective-permute-start | bytes 86024 | tf_op jit(solution)/shard_map/ppermute | solution.py:503
  9.5 1.6 %copy-start.1 = (f32[384,192]{0,1:T(8,128)S(1)}, f32[384,192]{0,1:T(8,128)}, u32[]{:S(2)}) copy-start(f32[384,192]{0,1:T(8,128)} %param.20) | copy-start | bytes 884740
  12.5 4.7 %collective-permute-start.4 = (f32[96,128]{1,0:T(8,128)S(1)}, f32[96,128]{1,0:T(8,128)S(1)}, u32[]{:S(2)}, u32[]{:S(2)}) collective-permute-start(f32[96,128]{1,0:T(8,128)S(1)} %get-tuple-element.63.part_ref), channel_id=1, source_target_pairs={{0,2},{2,0},{1,3},{3,1},{4,6},{6,4},{5,7},{7,5},{8,10},{10,8},{9,1... | collective-permute-start | bytes 147464 | tf_op jit(solution)/shard_map/ppermute | solution.py:485
  14.1 1.0 %copy-start = (f32[192,192]{1,0:T(8,128)S(1)}, f32[192,192]{1,0:T(8,128)}, u32[]{:S(2)}) copy-start(f32[192,192]{1,0:T(8,128)} %w_ref.5) | copy-start | bytes 442372
  14.1 1.0 %copy-start.2 = (f32[256,192]{0,1:T(8,128)S(1)}, f32[256,192]{0,1:T(8,128)}, u32[]{:S(2)}) copy-start(f32[256,192]{0,1:T(8,128)} %param.25) | copy-start | bytes 589828
  14.1 1.1 %copy-start.3 = (f32[192,192]{1,0:T(8,128)S(1)}, f32[192,192]{1,0:T(8,128)}, u32[]{:S(2)}) copy-start(f32[192,192]{1,0:T(8,128)} %wv_ref.1) | copy-start | bytes 442372
  14.5 6.9 %collective-permute-start.3 = (f32[192,256]{1,0:T(8,128)S(1)}, f32[192,256]{1,0:T(8,128)S(1)}, u32[]{:S(2)}, u32[]{:S(2)}) collective-permute-start(f32[192,256]{1,0:T(8,128)S(1)} %get-tuple-element.60.part_ref), channel_id=1, source_target_pairs={{0,2},{2,0},{1,3},{3,1},{4,6},{6,4},{5,7},{7,5},{8,10},{10,8},{9,1... | collective-permute-start | bytes 589832 | tf_op jit(solution)/shard_map/ppermute | solution.py:485
  17.2 4.2 %copy-start.4 = (f32[192,192]{1,0:T(8,128)S(1)}, f32[192,192]{1,0:T(8,128)}, u32[]{:S(2)}) copy-start(f32[192,192]{1,0:T(8,128)} %w_ref.3) | copy-start | bytes 442372
  17.2 4.2 %copy-start.5 = (f32[192,192]{1,0:T(8,128)S(1)}, f32[192,192]{1,0:T(8,128)}, u32[]{:S(2)}) copy-start(f32[192,192]{1,0:T(8,128)} %wk_ref.1) | copy-start | bytes 442372
  17.5 5.9 %collective-permute-start.5 = (f32[96,128]{1,0:T(8,128)S(1)}, f32[96,128]{1,0:T(8,128)S(1)}, u32[]{:S(2)}, u32[]{:S(2)}) collective-permute-start(f32[96,128]{1,0:T(8,128)S(1)} %get-tuple-element.66), channel_id=1, source_target_pairs={{0,4},{4,8},{8,12},{12,0},{1,5},{5,9},{9,13},{13,1},{2,6},{6,10},{... | collective-permute-start | bytes 147464 | tf_op jit(solution)/shard_map/ppermute | solution.py:481
  17.6 5.9 %collective-permute-start.6 = (f32[96,128]{1,0:T(8,128)S(1)}, f32[96,128]{1,0:T(8,128)S(1)}, u32[]{:S(2)}, u32[]{:S(2)}) collective-permute-start(f32[96,128]{1,0:T(8,128)S(1)} %get-tuple-element.67), channel_id=1, source_target_pairs={{0,8},{4,12},{8,0},{12,4},{1,9},{5,13},{9,1},{13,5},{2,10},{6,14},... | collective-permute-start | bytes 147464 | tf_op jit(solution)/shard_map/ppermute | solution.py:481
  19.9 4.1 %collective-permute-start.7 = (f32[96,128]{1,0:T(8,128)S(1)}, f32[96,128]{1,0:T(8,128)S(1)}, u32[]{:S(2)}, u32[]{:S(2)}) collective-permute-start(f32[96,128]{1,0:T(8,128)S(1)} %get-tuple-element.68), channel_id=1, source_target_pairs={{0,12},{4,0},{8,4},{12,8},{1,13},{5,1},{9,5},{13,9},{2,14},{6,2},{... | collective-permute-start | bytes 147464 | tf_op jit(solution)/shard_map/ppermute | solution.py:481
  24.2 1.5 %collective-permute-start.8 = (f32[384,128]{1,0:T(8,128)S(1)}, f32[384,128]{1,0:T(8,128)S(1)}, u32[]{:S(2)}, u32[]{:S(2)}) collective-permute-start(f32[384,128]{1,0:T(8,128)S(1)} %get-tuple-element.78), channel_id=1, source_target_pairs={{0,1},{1,0},{2,3},{3,2},{4,5},{5,4},{6,7},{7,6},{8,9},{9,8},{10,11... | collective-permute-start | bytes 589832 | tf_op jit(solution)/shard_map/ppermute | solution.py:558
  27.6 1.4 %collective-permute-start.9 = (f32[192,128]{1,0:T(8,128)S(1)}, f32[192,128]{1,0:T(8,128)S(1)}, u32[]{:S(2)}, u32[]{:S(2)}) collective-permute-start(f32[192,128]{1,0:T(8,128)S(1)} %get-tuple-element.87), channel_id=1, source_target_pairs={{0,1},{1,0},{2,3},{3,2},{4,5},{5,4},{6,7},{7,6},{8,9},{9,8},{10,11... | collective-permute-start | bytes 294920 | tf_op jit(solution)/shard_map/ppermute | solution.py:577
  29.0 5.8 %collective-permute-start.10 = (f32[48,128]{1,0:T(8,128)S(1)}, f32[48,128]{1,0:T(8,128)S(1)}, u32[]{:S(2)}, u32[]{:S(2)}) collective-permute-start(f32[48,128]{1,0:T(8,128)S(1)} %get-tuple-element.89), channel_id=1, source_target_pairs={{0,4},{4,8},{8,12},{12,0},{1,5},{5,9},{9,13},{13,1},{2,6},{6,10},{... | collective-permute-start | bytes 73736 | tf_op jit(solution)/shard_map/ppermute | solution.py:481
  31.0 4.8 %collective-permute-start.11 = (f32[48,128]{1,0:T(8,128)S(1)}, f32[48,128]{1,0:T(8,128)S(1)}, u32[]{:S(2)}, u32[]{:S(2)}) collective-permute-start(f32[48,128]{1,0:T(8,128)S(1)} %get-tuple-element.90), channel_id=1, source_target_pairs={{0,8},{4,12},{8,0},{12,4},{1,9},{5,13},{9,1},{13,5},{2,10},{6,14},... | collective-permute-start | bytes 73736 | tf_op jit(solution)/shard_map/ppermute | solution.py:481
  32.8 3.8 %collective-permute-start.12 = (f32[48,128]{1,0:T(8,128)S(1)}, f32[48,128]{1,0:T(8,128)S(1)}, u32[]{:S(2)}, u32[]{:S(2)}) collective-permute-start(f32[48,128]{1,0:T(8,128)S(1)} %get-tuple-element.91), channel_id=1, source_target_pairs={{0,12},{4,0},{8,4},{12,8},{1,13},{5,1},{9,5},{13,9},{2,14},{6,2},{... | collective-permute-start | bytes 73736 | tf_op jit(solution)/shard_map/ppermute | solution.py:481
